TPU v7x, 128 devices: a whole 4x4x4 slice. The times are simulated.
128 devices in a mesh: ctx: 16 (over z, y), tp: 8 (over x, core).
Axes of the slice: x: 4, y: 4, z: 4, core: 2. Of those that a mesh axis runs over, the one named last changes fastest.
Arguments:
- signal: bfloat16 [8192, 4096], P('ctx', 'tp'), may hold values from -6 to 6
- gate: bfloat16 [8192, 4096], P('ctx', 'tp'), may hold values from -6 to 6
- filt: float32 [8192, 4096], P('ctx', 'tp'), may hold values from -0.0625 to 0.0625
- skip: float32 [4096], P('tp'), may hold values from 0.5 to 1.5
- w_out: bfloat16 [4096, 8192], P(None, 'tp'), may hold values from -0.09375 to 0.09375
Outputs:
- output: bfloat16 [8192, 8192], P('ctx', 'tp')
All inputs are finite; a program needn't handle non-finite values.
Results may differ from a plain program's by a relative error of at most 0.015.
Values may be sent and summed in bfloat16 or wider, within the bound.
No kernel may reach another device: no remote copies, remote signals or barrier semaphores. Data moves between devices by JAX's collectives and lax.ppermute only.
A program may use at most 128 MiB of HBM per device.

v0:
```python
import math

import jax
import jax.numpy as jnp
from jax import lax
from jax.sharding import PartitionSpec as P


def as_sent(shard):

    def short(part):
        return part.astype(jnp.bfloat16) if part.dtype == jnp.float32 else part

    return jax.tree.map(short, shard)


def partner_2(block, axis, distance):
    count = lax.axis_size(axis)
    route = []
    for low in range(count):
        high = low | 1 << distance
        if high != low and high < count:
            route += [(low, high), (high, low)]
    return lax.ppermute(block, axis, route)


def exact_einsum(form, left, right):
    return jnp.einsum(form, left, right, precision=lax.Precision.HIGHEST)


def complex_mul(left_re, left_im, right_re, right_im):
    return (left_re * right_re - left_im * right_im, left_re * right_im + left_im * right_re)


def per_device(signal, gate, filt, skip, w_out):
    axis_size = lax.axis_size("ctx")
    levels = axis_size.bit_length() - 1
    position = lax.axis_index("ctx")
    row_count, channels = signal.shape
    full_length = 2 * axis_size * row_count
    values = signal.astype(jnp.float32)
    stacked = jnp.concatenate([values, filt], axis=1)
    doubled = 2 * channels
    phase = -math.pi * position.astype(jnp.float32) / axis_size
    real_part = jnp.stack([stacked, stacked * jnp.cos(phase)])
    imag_part = jnp.stack([jnp.zeros_like(stacked), stacked * jnp.sin(phase)])
    for bit_number in reversed(range(levels)):
        half_span = 1 << bit_number
        partner = partner_2(
            as_sent(jnp.concatenate([real_part, imag_part], axis=2)), "ctx", bit_number
        )
        partner_re = partner[..., :doubled]
        partner_im = partner[..., doubled:]
        is_upper = position >> bit_number & 1 == 1
        angle = -math.pi * (position % half_span).astype(jnp.float32) / half_span
        diff_re, diff_im = complex_mul(
            partner_re - real_part, partner_im - imag_part, jnp.cos(angle), jnp.sin(angle)
        )
        real_part = jnp.where(is_upper, diff_re, real_part + partner_re)
        imag_part = jnp.where(is_upper, diff_im, imag_part + partner_im)
    reversed_index = jnp.int32(0)
    for bit_number in range(levels):
        reversed_index = reversed_index + (position >> bit_number & 1) * (
            1 << levels - 1 - bit_number
        )
    freqs = 2 * reversed_index + jnp.arange(2, dtype=jnp.int32)
    row_index = jnp.arange(row_count, dtype=jnp.int32)
    twist = (row_index[None, :] * freqs[:, None] % full_length).astype(jnp.float32)
    twist_angle = 2.0 * math.pi / full_length * twist[:, :, None]
    twist_cos = jnp.cos(twist_angle)
    twist_sin = jnp.sin(twist_angle)
    real_part, imag_part = complex_mul(real_part, imag_part, twist_cos, -twist_sin)
    table = (row_index[:, None] * row_index[None, :] % row_count).astype(jnp.float32)
    table_cos = jnp.cos(2.0 * math.pi / row_count * table)
    table_sin = jnp.sin(2.0 * math.pi / row_count * table)
    spec_re = exact_einsum("kr,brc->bkc", table_cos, real_part) + exact_einsum(
        "kr,brc->bkc", table_sin, imag_part
    )
    spec_im = exact_einsum("kr,brc->bkc", table_cos, imag_part) - exact_einsum(
        "kr,brc->bkc", table_sin, real_part
    )
    prod_re, prod_im = complex_mul(
        spec_re[..., :channels],
        spec_im[..., :channels],
        spec_re[..., channels:],
        spec_im[..., channels:],
    )
    back_re = exact_einsum("rk,bkc->brc", table_cos, prod_re) - exact_einsum(
        "rk,bkc->brc", table_sin, prod_im
    )
    back_im = exact_einsum("rk,bkc->brc", table_sin, prod_re) + exact_einsum(
        "rk,bkc->brc", table_cos, prod_im
    )
    back_re, back_im = complex_mul(back_re, back_im, twist_cos, twist_sin)
    for bit_number in range(levels):
        half_span = 1 << bit_number
        partner = partner_2(as_sent(jnp.concatenate([back_re, back_im], axis=2)), "ctx", bit_number)
        partner_re = partner[..., :channels]
        partner_im = partner[..., channels:]
        is_upper = position >> bit_number & 1 == 1
        angle = math.pi * (position % half_span).astype(jnp.float32) / half_span
        turn_cos = jnp.cos(angle)
        turn_sin = jnp.sin(angle)
        lower_re, lower_im = complex_mul(partner_re, partner_im, turn_cos, turn_sin)
        upper_re, upper_im = complex_mul(back_re, back_im, turn_cos, turn_sin)
        back_re, back_im = (
            jnp.where(is_upper, partner_re - upper_re, back_re + lower_re),
            jnp.where(is_upper, partner_im - upper_im, back_im + lower_im),
        )
    phase = math.pi * position.astype(jnp.float32) / axis_size
    convolved = (
        back_re[0] + back_re[1] * jnp.cos(phase) - back_im[1] * jnp.sin(phase)
    ) / full_length
    mixed = (gate.astype(jnp.float32) * (convolved + skip * values)).astype(jnp.bfloat16)
    result = jnp.dot(
        lax.all_gather(mixed, "tp", axis=1, tiled=True), w_out, preferred_element_type=jnp.float32
    )
    return result.astype(jnp.bfloat16)


def solution(mesh):
    return jax.shard_map(
        per_device,
        mesh=mesh,
        in_specs=(P("ctx", "tp"), P("ctx", "tp"), P("ctx", "tp"), P("tp"), P(None, "tp")),
        out_specs=P("ctx", "tp"),
        check_vma=False,
    )
```

profile of v0, /device:TPU:1, one launch (start us, length us, event | category | flops | bytes accessed | tf_op | source)
XLA Modules:
  0.0 751.5 jit_solution(7061018077690797680)
XLA Ops:
  14.1 2.2 pad_maximum_fusion.1
  16.3 4.4 collective-permute-start
  20.9 90.4 %collective-permute-done = bf16[2,512,2048]{1,2,0:T(8,128)(2,1)} collective-permute-done((bf16[2,512,2048]{1,2,0:T(8,128)(2,1)}, bf16[2,512,2048]{1,2,0:T(8,128)(2,1)}, u32[]{:S(2)}, u32[]{:S(2)}) %collective-permute-start) | collective-permute-done | bytes 4194336 | tf_op jit(solution)/shard_map/ppermute | solution.py:24
  111.3 6.5 fusion.127
  117.8 2.3 pad_maximum_fusion.2
  120.9 90.3 %collective-permute-done.1 = bf16[2,512,2048]{1,2,0:T(8,128)(2,1)} collective-permute-done((bf16[2,512,2048]{1,2,0:T(8,128)(2,1)}, bf16[2,512,2048]{1,2,0:T(8,128)(2,1)}, u32[]{:S(2)}, u32[]{:S(2)}) %collective-permute-start.1) | collective-permute-done | bytes 4194336 | tf_op jit(solution)/shard_map/ppermute | solution.py:24
  211.2 7.6 %fusion.123 = (bf16[2,512,1024]{1,2,0:T(8,128)(2,1)S(1)}, f32[2,512,1024]{1,2,0:T(8,128)}, bf16[2,512,1024]{1,2,0:T(8,128)(2,1)S(1)}, f32[2,512,1024]{1,2,0:T(8,128)}) fusion(f32[2,512,1024]{1,2,0:T(8,128)} %get-tuple-element.30, f32[]{:T(128)S(6)} %sin.48, f32[2,512,1024]{1,2,0:T(8,128)} %get-tuple-element.40, ...), kind=kLoop, calls=%fused_computation.183 | loop fusion | flops 16777216 | bytes 25165832 | tf_op jit(solution)/shard_map/convert.10
  218.8 2.2 pad_maximum_fusion.3
  221.1 2.9 collective-permute-start.2
  224.1 88.7 %collective-permute-done.2 = bf16[2,512,2048]{1,2,0:T(8,128)(2,1)} collective-permute-done((bf16[2,512,2048]{1,2,0:T(8,128)(2,1)}, bf16[2,512,2048]{1,2,0:T(8,128)(2,1)}, u32[]{:S(2)}, u32[]{:S(2)}) %collective-permute-start.2) | collective-permute-done | bytes 4194336 | tf_op jit(solution)/shard_map/ppermute | solution.py:24
  312.8 7.7 %fusion.119 = (bf16[2,512,1024]{1,2,0:T(8,128)(2,1)S(1)}, f32[2,512,1024]{1,2,0:T(8,128)}, bf16[2,512,1024]{1,2,0:T(8,128)(2,1)S(1)}, f32[2,512,1024]{1,2,0:T(8,128)}) fusion(f32[2,512,1024]{1,2,0:T(8,128)} %get-tuple-element.26, f32[]{:T(128)S(6)} %sin.49, f32[2,512,1024]{1,2,0:T(8,128)} %get-tuple-element.38, ...), kind=kLoop, calls=%fused_computation.181 | loop fusion | flops 16777216 | bytes 25165832 | tf_op jit(solution)/shard_map/convert.8
  324.1 87.9 %collective-permute-done.3 = bf16[2,512,2048]{1,2,0:T(8,128)(2,1)} collective-permute-done((bf16[2,512,2048]{1,2,0:T(8,128)(2,1)}, bf16[2,512,2048]{1,2,0:T(8,128)(2,1)}, u32[]{:S(2)}, u32[]{:S(2)}) %collective-permute-start.3) | collective-permute-done | bytes 4194336 | tf_op jit(solution)/shard_map/ppermute | solution.py:24
  412.0 5.6 fusion.5
  417.6 11.5 %fusion.29 = f32[2,1024,512]{2,1,0:T(8,128)S(1)} fusion(f32[2,512,1024]{1,2,0:T(8,128)S(1)} %get-tuple-element.34, f32[2,512,1024]{1,2,0:T(8,128)S(1)} %get-tuple-element.33, f32[2,512]{1,0:T(2,128)S(1)} %get-tuple-element.58, f32[2,512]{1,0:T(2,128)S(1)} %get-tuple-element.59), kind=kOutput, calls=%fused_computation.95 | convolution fusion | flops 6449266688 | bytes 12591104 | tf_op jit(solution)/shard_map/kr,brc->bkc/dot_general | solution.py:28
  429.1 11.7 %fusion.28 = f32[2,1024,512]{2,1,0:T(8,128)S(1)} fusion(f32[2,512,1024]{1,2,0:T(8,128)S(1)} %get-tuple-element.34, f32[2,512,1024]{1,2,0:T(8,128)S(1)} %get-tuple-element.33, f32[2,512]{1,0:T(2,128)S(1)} %get-tuple-element.58, f32[2,512]{1,0:T(2,128)S(1)} %get-tuple-element.59), kind=kOutput, calls=%fused_computation.94 | convolution fusion | flops 6449266688 | bytes 12591104 | tf_op jit(solution)/shard_map/kr,brc->bkc/dot_general | solution.py:28
  440.8 12.0 %add_bitcast_fusion = f32[2,512,1024]{1,2,0:T(8,128)S(1)} fusion(f32[2,1024,512]{2,1,0:T(8,128)S(1)} %fusion.29, f32[2,512,1024]{1,2,0:T(8,128)S(1)} %get-tuple-element.34, f32[2,512,1024]{1,2,0:T(8,128)S(1)} %get-tuple-element.33, f32[2,512]{1,0:T(2,128)S(1)} %get-tuple-element.58, f32[2,512]{1,0:T(2,128)S(1)} %get-tuple-element.59), kind=kOutput, calls=%fused_computation.31 | convolution fusion | flops 6450315264 | bytes 16785408 | tf_op jit(solution)/shard_map/kr,brc->bkc/dot_general | solution.py:28
  452.8 11.7 %subtract_bitcast_fusion = f32[2,512,1024]{1,2,0:T(8,128)S(1)} fusion(f32[2,1024,512]{2,1,0:T(8,128)S(1)} %fusion.28, f32[2,512,1024]{1,2,0:T(8,128)S(1)} %get-tuple-element.34, f32[2,512,1024]{1,2,0:T(8,128)S(1)} %get-tuple-element.33, f32[2,512]{1,0:T(2,128)S(1)} %get-tuple-element.58, f32[2,512]{1,0:T(2,128)S(1)} %get-tuple-element.59), kind=kOutput, calls=%fused_computation.30 | convolution fusion | flops 6450315264 | bytes 16785408 | tf_op jit(solution)/shard_map/kr,brc->bkc/dot_general | solution.py:28
  465.6 8.4 %fusion.52 = f32[2,512,512]{2,1,0:T(8,128)S(1)} fusion(f32[2,512,512]{1,2,0:T(8,128)S(1)} %get-tuple-element.42), kind=kOutput, calls=%fused_computation.123 | convolution fusion | flops 3224895488 | bytes 4194304 | tf_op jit(solution)/shard_map/rk,bkc->brc/dot_general | solution.py:28
  474.0 8.6 %fusion.46 = f32[2,512,512]{2,1,0:T(8,128)S(1)} fusion(f32[2,512,512]{1,2,0:T(8,128)S(1)} %get-tuple-element.42), kind=kOutput, calls=%fused_computation.117 | convolution fusion | flops 3224895488 | bytes 4194304 | tf_op jit(solution)/shard_map/rk,bkc->brc/dot_general | solution.py:28
  482.7 8.5 %convolution_subtract_fusion = f32[2,512,512]{2,1,0:T(8,128)S(1)} fusion(f32[2,512,512]{2,1,0:T(8,128)S(1)} %fusion.52, f32[2,512,512]{1,2,0:T(8,128)S(1)} %get-tuple-element.41), kind=kOutput, calls=%fused_computation.89 | convolution fusion | flops 3225419776 | bytes 6291456 | tf_op jit(solution)/shard_map/rk,bkc->brc/dot_general | solution.py:28
  491.1 9.0 %bitcast_convert_fusion.1 = (bf16[2,512,512]{1,2,0:T(8,128)(2,1)S(1)}, f32[2,512,512]{2,1,0:T(8,128)S(1)}, bf16[2,512,512]{1,2,0:T(8,128)(2,1)S(1)}, f32[2,512,512]{2,1,0:T(8,128)S(1)}) fusion(f32[2,512]{1,0:T(2,128)S(1)} %get-tuple-element.57, f32[2,512,512]{2,1,0:T(8,128)S(1)} %convolution_subtract_fusion, f32[2,512]{1,0:T(2,128)S(1)} %get-tuple-element.59, ...), kind=kOutput, calls=%fused_computation.80 | convolution fusion | flops 3229614080 | bytes 12591104 | tf_op jit(solution)/shard_map/rk,bkc->brc/dot_general | solution.py:28
  501.7 41.8 %collective-permute-done.4 = bf16[2,512,1024]{1,2,0:T(8,128)(2,1)S(1)} collective-permute-done((bf16[2,512,1024]{1,2,0:T(8,128)(2,1)S(1)}, bf16[2,512,1024]{1,2,0:T(8,128)(2,1)S(1)}, u32[]{:S(2)}, u32[]{:S(2)}) %collective-permute-start.4) | collective-permute-done | bytes 2097184 | tf_op jit(solution)/shard_map/ppermute | solution.py:24
  543.5 2.5 fusion.115
  547.6 2.9 collective-permute-start.5
  550.6 41.0 %collective-permute-done.5 = bf16[2,512,1024]{1,2,0:T(8,128)(2,1)} collective-permute-done((bf16[2,512,1024]{1,2,0:T(8,128)(2,1)}, bf16[2,512,1024]{1,2,0:T(8,128)(2,1)}, u32[]{:S(2)}, u32[]{:S(2)}) %collective-permute-start.5) | collective-permute-done | bytes 2097184 | tf_op jit(solution)/shard_map/ppermute | solution.py:24
  591.6 4.3 fusion.111
  597.6 41.3 %collective-permute-done.6 = bf16[2,512,1024]{1,2,0:T(8,128)(2,1)S(1)} collective-permute-done((bf16[2,512,1024]{1,2,0:T(8,128)(2,1)}, bf16[2,512,1024]{1,2,0:T(8,128)(2,1)S(1)}, u32[]{:S(2)}, u32[]{:S(2)}) %collective-permute-start.6) | collective-permute-done | bytes 2097184 | tf_op jit(solution)/shard_map/ppermute | solution.py:24
  640.3 4.5 fusion.107
  647.9 40.9 %collective-permute-done.7 = bf16[2,512,1024]{1,2,0:T(8,128)(2,1)} collective-permute-done((bf16[2,512,1024]{1,2,0:T(8,128)(2,1)}, bf16[2,512,1024]{1,2,0:T(8,128)(2,1)}, u32[]{:S(2)}, u32[]{:S(2)}) %collective-permute-start.7) | collective-permute-done | bytes 2097184 | tf_op jit(solution)/shard_map/ppermute | solution.py:24
  690.9 2.4 add_select_fusion
  694.8 39.2 %all-gather.2.cloned.1.call-done = bf16[512,4096]{0,1:T(8,128)(2,1)} async-done(((bf16[512,512]{0,1:T(8,128)(2,1)}), bf16[512,4096]{0,1:T(8,128)(2,1)}) %all-gather.2.cloned.1.call-update) | async-done | bytes 4194320 | tf_op jit(solution)/shard_map/all_gather | solution.py:116
  734.0 10.1 %convolution_convert_fusion = bf16[512,1024]{1,0:T(8,128)(2,1)} fusion(bf16[512,4096]{0,1:T(8,128)(2,1)} %all-gather.2.cloned.1.call-done, bf16[4096,1024]{1,0:T(8,128)(2,1)} %param.9), kind=kOutput, calls=%fused_computation.93 | convolution fusion | flops 4295491584 | bytes 13631488 | tf_op jit(solution)/shard_map/dot_general | solution.py:115
  (44 shorter events, 24.9 us)
Async XLA Ops:
  6.5 3.1 copy-start.7
  6.5 727.5 %all-gather.2.cloned.1.call-start = ((), (), s32[]{:S(2)}) async-start(), calls=%async_computation | async-start | bytes 4718592 | tf_op jit(solution)/shard_map/all_gather | solution.py:116
  8.0 2.0 copy-start.3
  10.0 1.5 copy-start.5
  12.1 1.3 copy-start
  12.1 2.0 copy-start.1
  16.3 95.0 %collective-permute-start = (bf16[2,512,2048]{1,2,0:T(8,128)(2,1)}, bf16[2,512,2048]{1,2,0:T(8,128)(2,1)}, u32[]{:S(2)}, u32[]{:S(2)}) collective-permute-start(bf16[2,512,2048]{1,2,0:T(8,128)(2,1)} %pad_maximum_fusion.1), channel_id=1, source_target_pairs={{0,64},{64,0},{8,72},{72,8},{16,80},{80,16},{24,88},{88,24},{32,96... | collective-permute-start | bytes 12582920 | tf_op jit(solution)/shard_map/ppermute | solution.py:24
  120.1 91.2 %collective-permute-start.1 = (bf16[2,512,2048]{1,2,0:T(8,128)(2,1)}, bf16[2,512,2048]{1,2,0:T(8,128)(2,1)}, u32[]{:S(2)}, u32[]{:S(2)}) collective-permute-start(bf16[2,512,2048]{1,2,0:T(8,128)(2,1)} %pad_maximum_fusion.2), channel_id=1, source_target_pairs={{0,32},{32,0},{8,40},{40,8},{16,48},{48,16},{24,56},{56,24},{64,96... | collective-permute-start | bytes 12582920 | tf_op jit(solution)/shard_map/ppermute | solution.py:24
  221.1 91.7 %collective-permute-start.2 = (bf16[2,512,2048]{1,2,0:T(8,128)(2,1)}, bf16[2,512,2048]{1,2,0:T(8,128)(2,1)}, u32[]{:S(2)}, u32[]{:S(2)}) collective-permute-start(bf16[2,512,2048]{1,2,0:T(8,128)(2,1)} %pad_maximum_fusion.3), channel_id=1, source_target_pairs={{0,16},{16,0},{8,24},{24,8},{32,48},{48,32},{40,56},{56,40},{64,80... | collective-permute-start | bytes 12582920 | tf_op jit(solution)/shard_map/ppermute | solution.py:24
  322.7 89.3 %collective-permute-start.3 = (bf16[2,512,2048]{1,2,0:T(8,128)(2,1)}, bf16[2,512,2048]{1,2,0:T(8,128)(2,1)}, u32[]{:S(2)}, u32[]{:S(2)}) collective-permute-start(bf16[2,512,2048]{1,2,0:T(8,128)(2,1)} %pad_maximum_fusion.4), channel_id=1, source_target_pairs={{0,8},{8,0},{16,24},{24,16},{32,40},{40,32},{48,56},{56,48},{64,72... | collective-permute-start | bytes 12582920 | tf_op jit(solution)/shard_map/ppermute | solution.py:24
  500.3 43.2 %collective-permute-start.4 = (bf16[2,512,1024]{1,2,0:T(8,128)(2,1)S(1)}, bf16[2,512,1024]{1,2,0:T(8,128)(2,1)S(1)}, u32[]{:S(2)}, u32[]{:S(2)}) collective-permute-start(bf16[2,512,1024]{1,2,0:T(8,128)(2,1)S(1)} %pad_maximum_fusion.6), channel_id=1, source_target_pairs={{0,8},{8,0},{16,24},{24,16},{32,40},{40,32},{48,56},{56,48},{64,72... | collective-permute-start | bytes 6291464 | tf_op jit(solution)/shard_map/ppermute | solution.py:24
  547.6 44.0 %collective-permute-start.5 = (bf16[2,512,1024]{1,2,0:T(8,128)(2,1)}, bf16[2,512,1024]{1,2,0:T(8,128)(2,1)}, u32[]{:S(2)}, u32[]{:S(2)}) collective-permute-start(bf16[2,512,1024]{1,2,0:T(8,128)(2,1)} %pad_maximum_fusion.7), channel_id=1, source_target_pairs={{0,16},{16,0},{8,24},{24,8},{32,48},{48,32},{40,56},{56,40},{64,80... | collective-permute-start | bytes 6291464 | tf_op jit(solution)/shard_map/ppermute | solution.py:24
  597.4 41.5 %collective-permute-start.6 = (bf16[2,512,1024]{1,2,0:T(8,128)(2,1)}, bf16[2,512,1024]{1,2,0:T(8,128)(2,1)S(1)}, u32[]{:S(2)}, u32[]{:S(2)}) collective-permute-start(bf16[2,512,1024]{1,2,0:T(8,128)(2,1)} %pad_maximum_fusion.8), channel_id=1, source_target_pairs={{0,32},{32,0},{8,40},{40,8},{16,48},{48,16},{24,56},{56,24},{64,96... | collective-permute-start | bytes 6291464 | tf_op jit(solution)/shard_map/ppermute | solution.py:24
  638.9 1.4 copy-start.6
  644.8 2.8 copy-start.8
  646.3 42.5 %collective-permute-start.7 = (bf16[2,512,1024]{1,2,0:T(8,128)(2,1)}, bf16[2,512,1024]{1,2,0:T(8,128)(2,1)}, u32[]{:S(2)}, u32[]{:S(2)}) collective-permute-start(bf16[2,512,1024]{1,2,0:T(8,128)(2,1)} %pad_maximum_fusion.9), channel_id=1, source_target_pairs={{0,64},{64,0},{8,72},{72,8},{16,80},{80,16},{24,88},{88,24},{32,96... | collective-permute-start | bytes 6291464 | tf_op jit(solution)/shard_map/ppermute | solution.py:24
  647.9 43.0 %copy-start.2 = (f32[2,512,512]{1,2,0:T(8,128)S(1)}, f32[2,512,512]{1,2,0:T(8,128)}, u32[]{:S(2)}) copy-start(f32[2,512,512]{1,2,0:T(8,128)} %get-tuple-element.44) | copy-start | bytes 6291460
  690.9 2.4 copy-start.4
  690.9 2.4 copy-start.9
Sparse Core Ops, SparseCore 0:
  694.9 39.0 all-gather.1
where the time goes:
time: 758 us; the launch traced here: 751 us
  waiting for transfers between devices  561 us (74%)
  matrix products  91.6 us (12%)
  other arithmetic  63.5 us (8%)
  between operations  15.4 us (2%)
  starting transfers between devices  14.6 us (2%)
    ppermute x8, waiting for transfers between devices, partner_2(): return lax.ppermute(block, axis, route)  522 us
    dot_general x8, matrix products, exact_einsum(): return jnp.einsum(form, left, right, precision=lax.Precision.HIGHEST)  81.5 us
    all_gather x1, waiting for transfers between devices, per_device(): lax.all_gather(mixed, 'tp', axis=1, tiled=True)  39.2 us
    another operation x7, other arithmetic  33.6 us
  transfers between devices with their start and end apart: 9, of which 9 were waited for; matrix products, arithmetic and copies ran while one was open for 0% of the time, Pallas kernels for 0%

commit v1 on v0

v1 whole, which is shorter than its diff:
```python
import jax
import jax.numpy as jnp
import numpy as np
from jax import lax
from jax.experimental import pallas as pl
from jax.experimental.pallas import tpu as pltpu
from jax.sharding import PartitionSpec as P

GROUP = 16


def tables(blocks, rows):
    length = blocks * rows
    freq = np.arange(blocks) + 0.25
    turn = 2 * np.pi * np.outer(freq, np.arange(blocks)) / blocks
    same = np.eye(GROUP)
    first = np.concatenate([np.kron(np.cos(turn), same), np.kron(-np.sin(turn), same)], axis=0)
    last = np.concatenate([np.kron(np.cos(turn.T), same), np.kron(-np.sin(turn.T), same)], axis=1)
    twist = np.repeat(2 * np.pi * np.outer(freq, np.arange(rows)) / length, GROUP, axis=0)
    index = np.arange(rows)
    inner = 2 * np.pi * (np.outer(index, index) % rows) / rows
    cos, sin = np.cos(inner), np.sin(inner)
    middle = np.block([[cos, -sin], [sin, cos]])
    return (
        first.astype(jnp.bfloat16),
        middle.astype(jnp.bfloat16),
        (last / length).astype(jnp.bfloat16),
        np.cos(twist).astype(np.float32),
        np.sin(twist).astype(np.float32),
    )


def dot(left, right):
    return jnp.dot(left, right, preferred_element_type=jnp.float32)


def turn_kernel(signal_ref, filt_ref, out_ref):
    share = out_ref.shape[1] // 2
    for part, ref in enumerate((signal_ref, filt_ref)):
        flipped = ref[...].astype(jnp.float32).T.astype(jnp.bfloat16)
        out_ref[:, part * share : (part + 1) * share, :] = flipped.reshape(-1, share, flipped.shape[1])


def turn(signal, filt, ways):
    rows, channels = signal.shape
    share = channels // ways
    lanes = 128
    return pl.pallas_call(
        turn_kernel,
        grid=(channels // lanes,),
        in_specs=[pl.BlockSpec((rows, lanes), lambda b: (0, b))] * 2,
        out_specs=pl.BlockSpec((lanes // share, 2 * share, rows), lambda b: (b, 0, 0)),
        out_shape=jax.ShapeDtypeStruct((ways, 2 * share, rows), jnp.bfloat16),
        name="turn",
    )(signal, filt)


def conv_kernel(x_ref, first_ref, middle_ref, last_ref, cos_ref, sin_ref, out_ref):
    blocks, doubled, rows = x_ref.shape
    share = doubled // 2
    half = blocks * GROUP
    cos, sin = cos_ref[...], sin_ref[...]
    for start in range(0, share, GROUP):
        parts = []
        for base in (start, share + start):
            x = x_ref[:, base : base + GROUP, :].reshape(half, rows)
            a = dot(first_ref[...], x)
            re, im = a[:half], a[half:]
            parts.append(
                jnp.concatenate([re * cos + im * sin, im * cos - re * sin], axis=1).astype(jnp.bfloat16)
            )
        spec = dot(jnp.concatenate(parts, axis=0), middle_ref[...])
        xr, xi = spec[:half, :rows], spec[:half, rows:]
        hr, hi = spec[half:, :rows], spec[half:, rows:]
        prod = jnp.concatenate([xr * hr - xi * hi, xr * hi + xi * hr], axis=1).astype(jnp.bfloat16)
        back = lax.dot_general(
            prod, middle_ref[...], (((1,), (1,)), ((), ())), preferred_element_type=jnp.float32
        )
        re, im = back[:, :rows], back[:, rows:]
        untwisted = jnp.concatenate([re * cos - im * sin, re * sin + im * cos], axis=0).astype(jnp.bfloat16)
        y = dot(last_ref[...], untwisted)
        out_ref[:, start : start + GROUP, :] = y.reshape(blocks, GROUP, rows).astype(jnp.bfloat16)


def convolve(x):
    blocks, doubled, rows = x.shape
    constants = [jnp.asarray(t) for t in tables(blocks, rows)]
    return pl.pallas_call(
        conv_kernel,
        out_shape=jax.ShapeDtypeStruct((blocks, doubled // 2, rows), jnp.bfloat16),
        compiler_params=pltpu.CompilerParams(vmem_limit_bytes=48 * 2**20),
        name="convolve",
    )(x, *constants)


def mix_kernel(conv_ref, signal_ref, gate_ref, skip_ref, out_ref):
    conv = conv_ref[...].astype(jnp.float32).T
    values = signal_ref[...].astype(jnp.float32)
    out_ref[...] = (gate_ref[...].astype(jnp.float32) * (conv + skip_ref[...] * values)).astype(jnp.bfloat16)


def mix(conv, signal, gate, skip):
    rows, channels = signal.shape
    lanes = 128
    wide = pl.BlockSpec((rows, lanes), lambda b: (0, b))
    return pl.pallas_call(
        mix_kernel,
        grid=(channels // lanes,),
        in_specs=[
            pl.BlockSpec((lanes, rows), lambda b: (b, 0)),
            wide,
            wide,
            pl.BlockSpec((1, lanes), lambda b: (0, b)),
        ],
        out_specs=wide,
        out_shape=jax.ShapeDtypeStruct((rows, channels), jnp.bfloat16),
        name="mix",
    )(conv, signal, gate, skip.reshape(1, channels))


def per_device(signal, gate, filt, skip, w_out):
    ways = lax.axis_size("ctx")
    rows, channels = signal.shape
    spread = lax.all_to_all(turn(signal, filt, ways), "ctx", 0, 0, tiled=True)
    conv = lax.all_to_all(convolve(spread), "ctx", 0, 0, tiled=True)
    mixed = mix(conv.reshape(channels, rows), signal, gate, skip)
    result = jnp.dot(
        lax.all_gather(mixed, "tp", axis=1, tiled=True), w_out, preferred_element_type=jnp.float32
    )
    return result.astype(jnp.bfloat16)


def solution(mesh):
    return jax.shard_map(
        per_device,
        mesh=mesh,
        in_specs=(P("ctx", "tp"), P("ctx", "tp"), P("ctx", "tp"), P("tp"), P(None, "tp")),
        out_specs=P("ctx", "tp"),
        check_vma=False,
    )
```

time: 758 us -> 108 us (0.14)
  waiting for transfers between devices: 561 us -> 32.3 us
  matrix products: 91.6 us -> 10.1 us
  other arithmetic: 63.5 us -> 0 us
  blocking collectives: 0 us -> 37.7 us
  starting transfers between devices: 14.6 us -> 0.03 us
  Pallas kernels: 0 us -> 12.8 us
    ppermute x8 -> x0, waiting for transfers between devices: 522 us -> none  [partner_2(): return lax.ppermute(block, axis, route)]
    dot_general x8 -> x0, matrix products: 81.5 us -> none  [exact_einsum(): return jnp.einsum(form, left, right, precision=lax.Precision.HIGHEST)]
    all_to_all x0 -> x2, blocking collectives: none -> 37.7 us  [the longest x1 24.7 us: per_device(): spread = lax.all_to_all(turn(signal, filt, ways), 'ctx', 0, 0, tiled=True)]
    another operation x8 -> x0, other arithmetic: 35.1 us -> none
    ppermute x8 -> x0, starting transfers between devices: 14.6 us -> none  [partner_2(): return lax.ppermute(block, axis, route)]
    concatenate x8 -> x0, other arithmetic: 13.5 us -> none  [the longest x4 8.92 us: per_device(): jnp.concatenate([real_part, imag_part], axis=2)]
    pallas_call x0 -> x3, Pallas kernels: none -> 12.8 us  [the longest x1 5.25 us: convolve(): pl.pallas_call(conv_kernel, out_shape=jax.ShapeDtypeStruct((blocks, doubl...]
    select_n x2 -> x0, other arithmetic: 7.98 us -> none  [the longest x1 5.6 us: per_device(): real_part = jnp.where(is_upper, diff_re, real_part + partner_re)]
  transfers between devices with their start and end apart: 9 -> 1, of which waited for: 9 -> 1; matrix products, arithmetic and copies ran while one was open for 0% -> 0% of each run, Pallas kernels for 0% -> 0%
where the time goes in v1:
time: 108 us; the launch traced here: 107 us
  blocking collectives  37.7 us (35%)
  waiting for transfers between devices  32.3 us (30%)
  between operations  13.4 us (12%)
  Pallas kernels  12.8 us (12%)
  matrix products  10.1 us (9%)
    all_gather x1, waiting for transfers between devices, per_device(): lax.all_gather(mixed, 'tp', axis=1, tiled=True)  32.2 us
    all_to_all x1, blocking collectives, per_device(): spread = lax.all_to_all(turn(signal, filt, ways), 'ctx', 0, 0, tiled=True)  24.7 us
    all_to_all x1, blocking collectives, per_device(): conv = lax.all_to_all(convolve(spread), 'ctx', 0, 0, tiled=True)  13 us
    dot_general x1, matrix products, per_device(): jnp.dot(lax.all_gather(mixed, 'tp', axis=1, tiled=True), w_out, preferred...  10.1 us
    pallas_call x1, Pallas kernels, convolve(): pl.pallas_call(conv_kernel, out_shape=jax.ShapeDtypeStruct((blocks, doubl...  5.25 us
    pallas_call x1, Pallas kernels, turn(): pl.pallas_call(turn_kernel, grid=(channels // lanes,), in_specs=[pl.Block...  3.92 us
    pallas_call x1, Pallas kernels, mix(): pl.pallas_call(mix_kernel, grid=(channels // lanes,), in_specs=[pl.BlockS...  3.61 us
  transfers between devices with their start and end apart: 1, of which 1 were waited for; matrix products, arithmetic and copies ran while one was open for 0% of the time, Pallas kernels for 0%

profile of v1, /device:TPU:1, one launch (start us, length us, event | category | flops | bytes accessed | tf_op | source)
XLA Modules:
  0.0 107.3 jit_solution(13424916312609143)
XLA Ops:
  6.5 0.0 copy-start.1
  6.5 0.0 copy-start.2
  6.5 0.0 copy-start.3
  6.5 0.0 copy-start
  6.5 0.0 all-gather.2.cloned.1.call-start
  6.6 3.9 %turn.1 = bf16[16,64,512]{2,1,0:T(8,128)(2,1)} custom-call(bf16[512,512]{1,0:T(8,128)(2,1)} %signal_ref.3, f32[512,512]{1,0:T(8,128)} %filt_ref.1), custom_call_target="tpu_custom_call" | custom-call | tf_op jit(solution)/shard_map/turn/pallas_call | solution.py:48
  10.5 24.7 %all_to_all.10.x_ref = bf16[16,64,512]{2,1,0:T(8,128)(2,1)S(1)} all-to-all(bf16[16,64,512]{2,1,0:T(8,128)(2,1)} %turn.1), channel_id=1, replica_groups=mesh['ctx'=16,'tp'=8] {'ctx'}, dimensions={0} | all-to-all | bytes 2097152 | tf_op jit(solution)/shard_map/all_to_all | solution.py:124
  35.2 0.0 copy-done.1
  35.2 0.0 copy-done.2
  35.2 0.0 copy-done.3
  35.2 0.0 copy-done
  35.2 0.0 copy-start.4
  35.3 0.9 copy-done.4
  36.2 5.2 %convolve.1 = bf16[16,32,512]{2,1,0:T(8,128)(2,1)S(1)} custom-call(bf16[16,64,512]{2,1,0:T(8,128)(2,1)S(1)} %all_to_all.10.x_ref, bf16[512,256]{1,0:T(8,128)(2,1)S(1)} %copy-done.4, bf16[1024,1024]{1,0:T(8,128)(2,1)S(1)} %copy-done, bf16[256,512]{1,0:T(8,128)(2,1)S(1)} %copy-done.3, f32[256,512]{1,0:T(8,128)S(1)} %copy-done.2, f32[256,512]{1,0:T(8,128)S(1)} %copy-done.1), custom_call_target="tpu_custom_call" | custom-call | tf_op jit(solution)/shard_map/convolve/pallas_call | solution.py:88
  41.5 13.0 %all_to_all.11 = bf16[16,32,512]{2,1,0:T(8,128)(2,1)} all-to-all(bf16[16,32,512]{2,1,0:T(8,128)(2,1)S(1)} %convolve.1), channel_id=1, replica_groups=mesh['ctx'=16,'tp'=8] {'ctx'}, dimensions={0} | all-to-all | bytes 1048576 | tf_op jit(solution)/shard_map/all_to_all | solution.py:125
  54.4 3.6 %mix.1 = bf16[512,512]{1,0:T(8,128)(2,1)} custom-call(bf16[512,512]{1,0:T(8,128)(2,1)} %bitcast.4, bf16[512,512]{1,0:T(8,128)(2,1)} %signal_ref.3, bf16[512,512]{1,0:T(8,128)(2,1)} %gate_ref.1, f32[1,512]{1,0:T(1,128)} %bitcast.5), custom_call_target="tpu_custom_call" | custom-call | tf_op jit(solution)/shard_map/mix/pallas_call | solution.py:106
  58.0 0.0 all-gather.2.cloned.1.call-update
  58.1 32.2 %all-gather.2.cloned.1.call-done = bf16[512,4096]{1,0:T(8,128)(2,1)} async-done(((bf16[512,512]{1,0:T(8,128)(2,1)}), bf16[512,4096]{1,0:T(8,128)(2,1)}) %all-gather.2.cloned.1.call-update) | async-done | bytes 4194320 | tf_op jit(solution)/shard_map/all_gather | solution.py:128
  90.3 10.1 %convolution_convert_fusion = bf16[512,1024]{1,0:T(8,128)(2,1)} fusion(bf16[512,4096]{1,0:T(8,128)(2,1)} %all-gather.2.cloned.1.call-done, bf16[4096,1024]{1,0:T(8,128)(2,1)} %param.14), kind=kOutput, calls=%fused_computation | convolution fusion | flops 4295491584 | bytes 13631488 | tf_op jit(solution)/shard_map/dot_general | solution.py:127
Async XLA Ops:
  6.5 28.7 %copy-start.1 = (f32[256,512]{1,0:T(8,128)S(1)}, f32[256,512]{1,0:T(8,128)}, u32[]{:S(2)}) copy-start(f32[256,512]{1,0:T(8,128)} %constant.14.clone.sin_ref) | copy-start | bytes 1572868
  6.5 28.7 %copy-start.2 = (f32[256,512]{1,0:T(8,128)S(1)}, f32[256,512]{1,0:T(8,128)}, u32[]{:S(2)}) copy-start(f32[256,512]{1,0:T(8,128)} %constant.13.clone.cos_ref) | copy-start | bytes 1572868
  6.5 28.7 %copy-start.3 = (bf16[256,512]{1,0:T(8,128)(2,1)S(1)}, bf16[256,512]{1,0:T(8,128)(2,1)}, u32[]{:S(2)}) copy-start(bf16[256,512]{1,0:T(8,128)(2,1)} %constant.12.clone.last_ref) | copy-start | bytes 786436
  6.5 28.7 %copy-start = (bf16[1024,1024]{1,0:T(8,128)(2,1)S(1)}, bf16[1024,1024]{1,0:T(8,128)(2,1)}, u32[]{:S(2)}) copy-start(bf16[1024,1024]{1,0:T(8,128)(2,1)} %constant.11.clone.middle_ref) | copy-start | bytes 6291460
  6.5 83.8 %all-gather.2.cloned.1.call-start = ((), (), s32[]{:S(2)}) async-start(), calls=%async_computation.2 | async-start | bytes 4718592 | tf_op jit(solution)/shard_map/all_gather | solution.py:128
  35.2 1.0 copy-start.4
Sparse Core Ops, SparseCore 0:
  58.2 32.0 all-gather.1

commit v2 on v1

--- a/solution.py
+++ b/solution.py
@@ -1,3 +1,5 @@
+import functools
+
 import jax
 import jax.numpy as jnp
 import numpy as np
@@ -51,6 +53,7 @@
         in_specs=[pl.BlockSpec((rows, lanes), lambda b: (0, b))] * 2,
         out_specs=pl.BlockSpec((lanes // share, 2 * share, rows), lambda b: (b, 0, 0)),
         out_shape=jax.ShapeDtypeStruct((ways, 2 * share, rows), jnp.bfloat16),
+        compiler_params=pltpu.CompilerParams(vmem_limit_bytes=8 * 2**20),
         name="turn",
     )(signal, filt)
 
@@ -88,7 +91,7 @@
     return pl.pallas_call(
         conv_kernel,
         out_shape=jax.ShapeDtypeStruct((blocks, doubled // 2, rows), jnp.bfloat16),
-        compiler_params=pltpu.CompilerParams(vmem_limit_bytes=48 * 2**20),
+        compiler_params=pltpu.CompilerParams(vmem_limit_bytes=20 * 2**20),
         name="convolve",
     )(x, *constants)
 
@@ -96,26 +99,134 @@
 def mix_kernel(conv_ref, signal_ref, gate_ref, skip_ref, out_ref):
     conv = conv_ref[...].astype(jnp.float32).T
     values = signal_ref[...].astype(jnp.float32)
-    out_ref[...] = (gate_ref[...].astype(jnp.float32) * (conv + skip_ref[...] * values)).astype(jnp.bfloat16)
+    mixed = (gate_ref[...].astype(jnp.float32) * (conv + skip_ref[...] * values)).astype(jnp.bfloat16)
+    width = out_ref.shape[2]
+    for half in range(2):
+        out_ref[half] = mixed[:, half * width : (half + 1) * width]
 
 
 def mix(conv, signal, gate, skip):
     rows, channels = signal.shape
-    lanes = 128
-    wide = pl.BlockSpec((rows, lanes), lambda b: (0, b))
     return pl.pallas_call(
         mix_kernel,
-        grid=(channels // lanes,),
-        in_specs=[
-            pl.BlockSpec((lanes, rows), lambda b: (b, 0)),
-            wide,
-            wide,
-            pl.BlockSpec((1, lanes), lambda b: (0, b)),
-        ],
-        out_specs=wide,
-        out_shape=jax.ShapeDtypeStruct((rows, channels), jnp.bfloat16),
+        out_shape=jax.ShapeDtypeStruct((2, rows, channels // 2), jnp.bfloat16),
+        compiler_params=pltpu.CompilerParams(vmem_limit_bytes=8 * 2**20),
         name="mix",
     )(conv, signal, gate, skip.reshape(1, channels))
+
+
+def shifted(block, step):
+    count = lax.axis_size("tp")
+    return lax.ppermute(block, "tp", [(i, (i + step) % count) for i in range(count)])
+
+
+def swapped(block):
+    return lax.ppermute(block, "tp", [(i, i ^ 1) for i in range(lax.axis_size("tp"))])
+
+
+def rows_of(blocks):
+    count = lax.axis_size("tp")
+    me = lax.axis_index("tp")
+    return [2 * lax.rem((me ^ 1 if other else me) + offset + count, count) + half for other, offset, half in blocks]
+
+
+def first_kernel(own, later, weights_ref, mine_ref, beside_ref, total_ref, later_ref, held_ref, sems):
+    copies = []
+    for j, row in enumerate(rows_of(own)):
+        copies.append(pltpu.make_async_copy(weights_ref.at[row], held_ref.at[j], sems.at[j]))
+    for j, row in enumerate(rows_of(later)):
+        copies.append(pltpu.make_async_copy(weights_ref.at[row], later_ref.at[j], sems.at[len(own) + j]))
+    for copy in copies:
+        copy.start()
+    left = jnp.concatenate([mine_ref[0], mine_ref[1], beside_ref[0], beside_ref[1]], axis=1)
+    for copy in copies[: len(own)]:
+        copy.wait()
+    add_product(left, held_ref, 0, None, total_ref)
+    for copy in copies[len(own) :]:
+        copy.wait()
+
+
+def add_product(left, weights_ref, first, total_ref, out_ref):
+    width = weights_ref.shape[1]
+    count = left.shape[1] // width
+    lanes = 256
+    for start in range(0, out_ref.shape[1], lanes):
+        span = slice(start, start + lanes)
+        mine = dot(left, weights_ref[first : first + count, :, span].reshape(count * width, lanes))
+        if total_ref is not None:
+            mine = mine + total_ref[:, span]
+        out_ref[:, span] = mine.astype(out_ref.dtype)
+
+
+def later_kernel(first, weights_ref, *refs):
+    blocks, total_ref, out_ref = refs[:-2], refs[-2], refs[-1]
+    left = jnp.concatenate([block[half] for block in blocks for half in range(block.shape[0])], axis=1)
+    add_product(left, weights_ref, first, total_ref, out_ref)
+
+
+VMEM = pl.BlockSpec(memory_space=pltpu.VMEM)
+
+
+def cost(rows, depth, columns):
+    return pl.CostEstimate(
+        flops=2 * rows * depth * columns,
+        bytes_accessed=2 * (rows + columns) * depth + 8 * rows * columns,
+        transcendentals=0,
+    )
+
+
+def later_call(weights, first, blocks, total, dtype, name):
+    rows, columns = total.shape
+    depth = sum(block.shape[0] for block in blocks) * weights.shape[1]
+    return pl.pallas_call(
+        functools.partial(later_kernel, first),
+        in_specs=[VMEM] * (2 + len(blocks)),
+        out_specs=VMEM,
+        out_shape=jax.ShapeDtypeStruct((rows, columns), dtype),
+        compiler_params=pltpu.CompilerParams(vmem_limit_bytes=12 * 2**20),
+        cost_estimate=cost(rows, depth, columns),
+        name=name,
+    )(weights, *blocks, total)
+
+
+def project(mixed, w_out):
+    width, columns = mixed.shape[2], w_out.shape[1]
+    rows = mixed.shape[1]
+    weights = w_out.reshape(-1, width, columns)
+    own = [(other, 0, half) for other in (0, 1) for half in (0, 1)]
+    near = [(other, offset, half) for other in (0, 1) for offset in (2, -2) for half in (0, 1)]
+    far = [(other, 4, half) for other in (0, 1) for half in (0, 1)]
+    later = near + far
+
+    right, left = shifted(mixed, -2), shifted(mixed, 2)
+    beside = swapped(mixed)
+    total, weights = pl.pallas_call(
+        functools.partial(first_kernel, own, later),
+        in_specs=[pl.BlockSpec(memory_space=pl.ANY), VMEM, VMEM],
+        out_specs=[VMEM, VMEM],
+        out_shape=[
+            jax.ShapeDtypeStruct((rows, columns), jnp.float32),
+            jax.ShapeDtypeStruct((len(later), width, columns), weights.dtype),
+        ],
+        scratch_shapes=[
+            pltpu.VMEM((len(own), width, columns), weights.dtype),
+            pltpu.SemaphoreType.DMA((len(own) + len(later),)),
+        ],
+        compiler_params=pltpu.CompilerParams(vmem_limit_bytes=14 * 2**20),
+        cost_estimate=cost(rows, len(own) * width, columns),
+        name="project_own",
+    )(weights, mixed, beside)
+    right, left, total = lax.optimization_barrier((right, left, total))
+    far_low, far_high = shifted(right[:1], -2), shifted(left[1:], 2)
+    beside_right, beside_left = swapped(right), swapped(left)
+    total = later_call(
+        weights, 0, [right, left, beside_right, beside_left], total, jnp.float32, "project_near"
+    )
+    far_low, far_high, total = lax.optimization_barrier((far_low, far_high, total))
+    beside_low, beside_high = swapped(far_low), swapped(far_high)
+    return later_call(
+        weights, len(near), [far_low, far_high, beside_low, beside_high], total, jnp.bfloat16, "project_far"
+    )
 
 
 def per_device(signal, gate, filt, skip, w_out):
@@ -123,11 +234,7 @@
     rows, channels = signal.shape
     spread = lax.all_to_all(turn(signal, filt, ways), "ctx", 0, 0, tiled=True)
     conv = lax.all_to_all(convolve(spread), "ctx", 0, 0, tiled=True)
-    mixed = mix(conv.reshape(channels, rows), signal, gate, skip)
-    result = jnp.dot(
-        lax.all_gather(mixed, "tp", axis=1, tiled=True), w_out, preferred_element_type=jnp.float32
-    )
-    return result.astype(jnp.bfloat16)
+    return project(mix(conv.reshape(channels, rows), signal, gate, skip), w_out)
 
 
 def solution(mesh):

time: 108 us -> 81.4 us (0.75)
  waiting for transfers between devices: 32.3 us -> 18.4 us
  between operations: 13.4 us -> 0.14 us
  matrix products: 10.1 us -> 0 us
  starting transfers between devices: 0.03 us -> 9.46 us
  local copies, waits for them, and re-layouts: 0.96 us -> 2.35 us
    all_gather x1 -> x0, waiting for transfers between devices: 32.2 us -> none  [per_device(): lax.all_gather(mixed, 'tp', axis=1, tiled=True)]
    ppermute x0 -> x9, waiting for transfers between devices: none -> 18.4 us  [the longest x4 16.2 us: shifted(): lax.ppermute(block, 'tp', [(i, (i + step) % count) for i in range(count)])]
    dot_general x1 -> x0, matrix products: 10.1 us -> none  [per_device(): jnp.dot(lax.all_gather(mixed, 'tp', axis=1, tiled=True), w_out, preferred...]
    ppermute x0 -> x9, starting transfers between devices: none -> 9.46 us  [the longest x5 5.43 us: swapped(): lax.ppermute(block, 'tp', [(i, i ^ 1) for i in range(lax.axis_size('tp'))])]
    pallas_call x1 -> x4, Pallas kernels: 3.61 us -> 6.89 us  [the longest x2 4.54 us: later_call(): pl.pallas_call(functools.partial(later_kernel, first), in_specs=[VMEM] *...]
    pallas_call x1, Pallas kernels: 3.92 us -> 0.86 us  [turn(): pl.pallas_call(turn_kernel, grid=(channels // lanes,), in_specs=[pl.Block...]
    unnamed x10 -> x22, local copies, waits for them, and re-layouts: 0.96 us -> 2.31 us
  transfers between devices with their start and end apart: 1 -> 9, of which waited for: 1 -> 7; matrix products, arithmetic and copies ran while one was open for 0% -> 0% of each run, Pallas kernels for 0% -> 5%
where the time goes in v2:
time: 81.4 us; the launch traced here: 81.1 us
  blocking collectives  37.7 us (46%)
  waiting for transfers between devices  18.4 us (23%)
  Pallas kernels  13 us (16%)
  starting transfers between devices  9.46 us (12%)
  local copies, waits for them, and re-layouts  2.35 us (3%)
    all_to_all x1, blocking collectives, per_device(): spread = lax.all_to_all(turn(signal, filt, ways), 'ctx', 0, 0, tiled=True)  24.7 us
    ppermute x4, waiting for transfers between devices, shifted(): lax.ppermute(block, 'tp', [(i, (i + step) % count) for i in range(count)])  16.2 us
    all_to_all x1, blocking collectives, per_device(): conv = lax.all_to_all(convolve(spread), 'ctx', 0, 0, tiled=True)  13.1 us
    ppermute x5, starting transfers between devices, swapped(): lax.ppermute(block, 'tp', [(i, i ^ 1) for i in range(lax.axis_size('tp'))])  5.43 us
    pallas_call x1, Pallas kernels, convolve(): pl.pallas_call(conv_kernel, out_shape=jax.ShapeDtypeStruct((blocks, doubl...  5.26 us
    pallas_call x2, Pallas kernels, later_call(): pl.pallas_call(functools.partial(later_kernel, first), in_specs=[VMEM] *...  4.54 us
    ppermute x4, starting transfers between devices, shifted(): lax.ppermute(block, 'tp', [(i, (i + step) % count) for i in range(count)])  4.03 us
    unnamed x22, local copies, waits for them, and re-layouts  2.31 us
  transfers between devices with their start and end apart: 9, of which 7 were waited for; matrix products, arithmetic and copies ran while one was open for 0% of the time, Pallas kernels for 5%

profile of v2, /device:TPU:1, one launch (start us, length us, event | category | flops | bytes accessed | tf_op | source)
XLA Modules:
  0.0 81.1 jit_solution(11405720876259337660)
XLA Ops:
  0.0 1.0 %copy-done.1 = bf16[512,512]{1,0:T(8,128)(2,1)S(1)} copy-done((bf16[512,512]{1,0:T(8,128)(2,1)S(1)}, bf16[512,512]{1,0:T(8,128)(2,1)}, u32[]{:S(2)}) %copy-start.1) | copy-done | bytes 524312
  1.0 1.2 %copy-done.4 = f32[512,512]{1,0:T(8,128)S(1)} copy-done((f32[512,512]{1,0:T(8,128)S(1)}, f32[512,512]{1,0:T(8,128)}, u32[]{:S(2)}) %copy-start.4) | copy-done | bytes 1048600
  2.3 0.0 copy-start.9
  2.3 0.9 %turn.1 = bf16[16,64,512]{2,1,0:T(8,128)(2,1)S(1)} custom-call(bf16[512,512]{1,0:T(8,128)(2,1)S(1)} %copy-done.1, f32[512,512]{1,0:T(8,128)S(1)} %copy-done.4), custom_call_target="tpu_custom_call" | custom-call | tf_op jit(solution)/shard_map/turn/pallas_call | solution.py:50
  3.2 0.0 copy-start.2
  3.2 0.0 copy-start.5
  3.2 0.0 copy-start.10
  3.2 24.7 %all_to_all.10.x_ref = bf16[16,64,512]{2,1,0:T(8,128)(2,1)S(1)} all-to-all(bf16[16,64,512]{2,1,0:T(8,128)(2,1)S(1)} %turn.1), channel_id=1, replica_groups=mesh['ctx'=16,'tp'=8] {'ctx'}, dimensions={0} | all-to-all | bytes 2097152 | tf_op jit(solution)/shard_map/all_to_all | solution.py:235
  27.9 0.0 copy-start
  27.9 5.3 %convolve.1 = bf16[16,32,512]{2,1,0:T(8,128)(2,1)S(1)} custom-call(bf16[16,64,512]{2,1,0:T(8,128)(2,1)S(1)} %all_to_all.10.x_ref, bf16[512,256]{1,0:T(8,128)(2,1)S(1)} %copy-done.8, bf16[1024,1024]{1,0:T(8,128)(2,1)S(1)} %copy-done.3, bf16[256,512]{1,0:T(8,128)(2,1)S(1)} %copy-done.9, f32[256,512]{1,0:T(8,128)S(1)} %copy-done.6, f32[256,512]{1,0:T(8,128)S(1)} %copy-done.7), custom_call_target="tpu_custom_call" | custom-call | tf_op jit(solution)/shard_map/convolve/pallas_call | solution.py:91
  33.2 13.1 %all_to_all.11 = bf16[16,32,512]{2,1,0:T(8,128)(2,1)S(1)} all-to-all(bf16[16,32,512]{2,1,0:T(8,128)(2,1)S(1)} %convolve.1), channel_id=1, replica_groups=mesh['ctx'=16,'tp'=8] {'ctx'}, dimensions={0} | all-to-all | bytes 1048576 | tf_op jit(solution)/shard_map/all_to_all | solution.py:236
  46.2 0.3 mix.1.mine_ref
  46.5 2.7 %collective-permute-start = (bf16[2,512,256]{2,1,0:T(8,128)(2,1)S(1)}, bf16[2,512,256]{2,1,0:T(8,128)(2,1)S(1)}, u32[]{:S(2)}, u32[]{:S(2)}) collective-permute-start(bf16[2,512,256]{2,1,0:T(8,128)(2,1)S(1)} %mix.1.mine_ref), channel_id=1, source_target_pairs={{0,1},{1,0},{2,3},{3,2},{4,5},{5,4},{6,7},{7,6},{8,9},{9,8},{10,11... | collective-permute-start | bytes 1572872 | tf_op jit(solution)/shard_map/ppermute | solution.py:124
  49.2 2.5 %collective-permute-start.1 = (bf16[2,512,256]{2,1,0:T(8,128)(2,1)S(1)}, bf16[2,512,256]{2,1,0:T(8,128)(2,1)S(1)}, u32[]{:S(2)}, u32[]{:S(2)}) collective-permute-start(bf16[2,512,256]{2,1,0:T(8,128)(2,1)S(1)} %mix.1.mine_ref), channel_id=1, source_target_pairs={{0,6},{1,7},{2,0},{3,1},{4,2},{5,3},{6,4},{7,5},{8,14},{9,15},{10,... | collective-permute-start | bytes 1572872 | tf_op jit(solution)/shard_map/ppermute | solution.py:120
  51.7 0.0 collective-permute-start.2
  51.7 0.0 collective-permute-done.beside_ref
  51.7 2.1 %project_own.1 = (f32[512,1024]{1,0:T(8,128)S(1)}, bf16[12,256,1024]{2,1,0:T(8,128)(2,1)S(1)}) custom-call(bf16[16,256,1024]{2,1,0:T(8,128)(2,1)S(1)} %bitcast.3, bf16[2,512,256]{2,1,0:T(8,128)(2,1)S(1)} %mix.1.mine_ref, bf16[2,512,256]{2,1,0:T(8,128)(2,1)S(1)} %collective-permute-done.beside_ref), custom_call_target="tpu_custom_call" | custom-call | flops 1073741824 | bytes 7340032 | tf_op jit(solution)/shard_map/project_own/pallas_call | solution.py:203
  53.8 9.2 %collective-permute-done.1.refs_0_ = bf16[2,512,256]{2,1,0:T(8,128)(2,1)S(1)} collective-permute-done((bf16[2,512,256]{2,1,0:T(8,128)(2,1)S(1)}, bf16[2,512,256]{2,1,0:T(8,128)(2,1)S(1)}, u32[]{:S(2)}, u32[]{:S(2)}) %collective-permute-start.1) | collective-permute-done | bytes 524320 | tf_op jit(solution)/shard_map/ppermute | solution.py:120
  63.0 3.1 %collective-permute-done.2.refs_1_ = bf16[2,512,256]{2,1,0:T(8,128)(2,1)S(1)} collective-permute-done((bf16[2,512,256]{2,1,0:T(8,128)(2,1)S(1)}, bf16[2,512,256]{2,1,0:T(8,128)(2,1)S(1)}, u32[]{:S(2)}, u32[]{:S(2)}) %collective-permute-start.2) | collective-permute-done | bytes 524320 | tf_op jit(solution)/shard_map/ppermute | solution.py:120
  66.0 1.2 %collective-permute-start.5 = (bf16[2,512,256]{2,1,0:T(8,128)(2,1)S(1)}, bf16[2,512,256]{2,1,0:T(8,128)(2,1)S(1)}, u32[]{:S(2)}, u32[]{:S(2)}) collective-permute-start(bf16[2,512,256]{2,1,0:T(8,128)(2,1)S(1)} %collective-permute-done.1.refs_0_), channel_id=1, source_target_pairs={{0,1},{1,0},{2,3},{3,2},{4,5},{5,4},{6,7},{7,6},{8,9},{9,8},{10,11... | collective-permute-start | bytes 1572872 | tf_op jit(solution)/shard_map/ppermute | solution.py:124
  67.2 0.0 collective-permute-start.6
  67.3 0.1 collective-permute-start.3
  67.4 1.5 %collective-permute-start.4 = (bf16[1,512,256]{2,1,0:T(8,128)(2,1)S(1)}, bf16[1,512,256]{2,1,0:T(8,128)(2,1)S(1)}, u32[]{:S(2)}, u32[]{:S(2)}) collective-permute-start(bf16[1,512,256]{2,1,0:T(8,128)(2,1)S(1)} %slice.7), channel_id=1, source_target_pairs={{0,2},{1,3},{2,4},{3,5},{4,6},{5,7},{6,0},{7,1},{8,10},{9,11},{10,... | collective-permute-start | bytes 786440 | tf_op jit(solution)/shard_map/ppermute | solution.py:120
  68.8 0.7 collective-permute-done.6.refs_3_
  69.5 2.3 %project_near.1.refs_4_ = f32[512,1024]{1,0:T(8,128)S(1)} custom-call(bf16[12,256,1024]{2,1,0:T(8,128)(2,1)S(1)} %get-tuple-element.13.weights_ref, bf16[2,512,256]{2,1,0:T(8,128)(2,1)S(1)} %collective-permute-done.1.refs_0_, bf16[2,512,256]{2,1,0:T(8,128)(2,1)S(1)} %collective-permute-done.2.refs_1_, ...), custom_call_target="tpu_custom_call" | custom-call | flops 2147483648 | bytes 10485760 | tf_op jit(solution)/shard_map/project_near/pallas_call | solution.py:181
  71.8 2.9 %collective-permute-done.3.refs_0_ = bf16[1,512,256]{2,1,0:T(8,128)(2,1)S(1)} collective-permute-done((bf16[1,512,256]{2,1,0:T(8,128)(2,1)S(1)}, bf16[1,512,256]{2,1,0:T(8,128)(2,1)S(1)}, u32[]{:S(2)}, u32[]{:S(2)}) %collective-permute-start.3) | collective-permute-done | bytes 262176 | tf_op jit(solution)/shard_map/ppermute | solution.py:120
  74.7 1.1 %collective-permute-done.4.refs_1_ = bf16[1,512,256]{2,1,0:T(8,128)(2,1)S(1)} collective-permute-done((bf16[1,512,256]{2,1,0:T(8,128)(2,1)S(1)}, bf16[1,512,256]{2,1,0:T(8,128)(2,1)S(1)}, u32[]{:S(2)}, u32[]{:S(2)}) %collective-permute-start.4) | collective-permute-done | bytes 262176 | tf_op jit(solution)/shard_map/ppermute | solution.py:120
  75.8 1.6 %collective-permute-start.7 = (bf16[1,512,256]{2,1,0:T(8,128)(2,1)S(1)}, bf16[1,512,256]{2,1,0:T(8,128)(2,1)S(1)}, u32[]{:S(2)}, u32[]{:S(2)}) collective-permute-start(bf16[1,512,256]{2,1,0:T(8,128)(2,1)S(1)} %collective-permute-done.3.refs_0_), channel_id=1, source_target_pairs={{0,1},{1,0},{2,3},{3,2},{4,5},{5,4},{6,7},{7,6},{8,9},{9,8},{10,11... | collective-permute-start | bytes 786440 | tf_op jit(solution)/shard_map/ppermute | solution.py:124
  77.4 0.0 collective-permute-start.8
  77.4 1.2 %collective-permute-done.7.refs_2_ = bf16[1,512,256]{2,1,0:T(8,128)(2,1)S(1)} collective-permute-done((bf16[1,512,256]{2,1,0:T(8,128)(2,1)S(1)}, bf16[1,512,256]{2,1,0:T(8,128)(2,1)S(1)}, u32[]{:S(2)}, u32[]{:S(2)}) %collective-permute-start.7) | collective-permute-done | bytes 262176 | tf_op jit(solution)/shard_map/ppermute | solution.py:124
  78.5 0.4 collective-permute-done.8.refs_3_
  78.9 2.2 %project_far.1 = bf16[512,1024]{1,0:T(8,128)(2,1)} custom-call(bf16[12,256,1024]{2,1,0:T(8,128)(2,1)S(1)} %get-tuple-element.13.weights_ref, bf16[1,512,256]{2,1,0:T(8,128)(2,1)S(1)} %collective-permute-done.3.refs_0_, bf16[1,512,256]{2,1,0:T(8,128)(2,1)S(1)} %collective-permute-done.4.refs_1_, bf16[1,512,256]{2,1,0:T(8,128)(2,1)S(1)} %collective-permute-done.7.refs_2_, ...), custom_call_target="tpu_custom_call" | custom-call | flops 1073741824 | bytes 7340032 | tf_op jit(solution)/shard_map/project_far/pallas_call | solution.py:181
  (18 shorter events, 0.1 us)
Async XLA Ops:
  0.0 1.0 %copy-start.1 = (bf16[512,512]{1,0:T(8,128)(2,1)S(1)}, bf16[512,512]{1,0:T(8,128)(2,1)}, u32[]{:S(2)}) copy-start(bf16[512,512]{1,0:T(8,128)(2,1)} %signal_ref.3) | copy-start | bytes 1572868
  1.0 1.2 %copy-start.4 = (f32[512,512]{1,0:T(8,128)S(1)}, f32[512,512]{1,0:T(8,128)}, u32[]{:S(2)}) copy-start(f32[512,512]{1,0:T(8,128)} %filt_ref.1) | copy-start | bytes 3145732
  2.3 25.6 %copy-start.3 = (bf16[1024,1024]{1,0:T(8,128)(2,1)S(1)}, bf16[1024,1024]{1,0:T(8,128)(2,1)}, u32[]{:S(2)}) copy-start(bf16[1024,1024]{1,0:T(8,128)(2,1)} %constant.11.clone.middle_ref) | copy-start | bytes 6291460
  2.3 25.6 %copy-start.6 = (f32[256,512]{1,0:T(8,128)S(1)}, f32[256,512]{1,0:T(8,128)}, u32[]{:S(2)}) copy-start(f32[256,512]{1,0:T(8,128)} %constant.13.clone.cos_ref) | copy-start | bytes 1572868
  2.3 25.6 %copy-start.7 = (f32[256,512]{1,0:T(8,128)S(1)}, f32[256,512]{1,0:T(8,128)}, u32[]{:S(2)}) copy-start(f32[256,512]{1,0:T(8,128)} %constant.14.clone.sin_ref) | copy-start | bytes 1572868
  2.3 25.6 %copy-start.8 = (bf16[512,256]{1,0:T(8,128)(2,1)S(1)}, bf16[512,256]{1,0:T(8,128)(2,1)}, u32[]{:S(2)}) copy-start(bf16[512,256]{1,0:T(8,128)(2,1)} %constant.10.clone.first_ref) | copy-start | bytes 786436
  2.3 25.6 %copy-start.9 = (bf16[256,512]{1,0:T(8,128)(2,1)S(1)}, bf16[256,512]{1,0:T(8,128)(2,1)}, u32[]{:S(2)}) copy-start(bf16[256,512]{1,0:T(8,128)(2,1)} %constant.12.clone.last_ref) | copy-start | bytes 786436
  3.2 43.1 %copy-start.2 = (bf16[512,512]{1,0:T(8,128)(2,1)S(1)}, bf16[512,512]{1,0:T(8,128)(2,1)}, u32[]{:S(2)}) copy-start(bf16[512,512]{1,0:T(8,128)(2,1)} %signal_ref.3) | copy-start | bytes 1572868
  3.2 43.1 %copy-start.5 = (bf16[512,512]{1,0:T(8,128)(2,1)S(1)}, bf16[512,512]{1,0:T(8,128)(2,1)}, u32[]{:S(2)}) copy-start(bf16[512,512]{1,0:T(8,128)(2,1)} %gate_ref.1) | copy-start | bytes 1572868
  3.2 43.1 %copy-start.10 = (f32[512]{0:T(512)S(1)}, f32[512]{0:T(512)}, u32[]{:S(2)}) copy-start(f32[512]{0:T(512)} %param.13) | copy-start | bytes 6148
  27.9 23.8 %copy-start = (bf16[4096,1024]{1,0:T(8,128)(2,1)S(1)}, bf16[4096,1024]{1,0:T(8,128)(2,1)}, u32[]{:S(2)}) copy-start(bf16[4096,1024]{1,0:T(8,128)(2,1)} %param.14) | copy-start | bytes 25165828
  46.5 5.2 %collective-permute-start = (bf16[2,512,256]{2,1,0:T(8,128)(2,1)S(1)}, bf16[2,512,256]{2,1,0:T(8,128)(2,1)S(1)}, u32[]{:S(2)}, u32[]{:S(2)}) collective-permute-start(bf16[2,512,256]{2,1,0:T(8,128)(2,1)S(1)} %mix.1.mine_ref), channel_id=1, source_target_pairs={{0,1},{1,0},{2,3},{3,2},{4,5},{5,4},{6,7},{7,6},{8,9},{9,8},{10,11... | collective-permute-start | bytes 1572872 | tf_op jit(solution)/shard_map/ppermute | solution.py:124
  49.2 13.8 %collective-permute-start.1 = (bf16[2,512,256]{2,1,0:T(8,128)(2,1)S(1)}, bf16[2,512,256]{2,1,0:T(8,128)(2,1)S(1)}, u32[]{:S(2)}, u32[]{:S(2)}) collective-permute-start(bf16[2,512,256]{2,1,0:T(8,128)(2,1)S(1)} %mix.1.mine_ref), channel_id=1, source_target_pairs={{0,6},{1,7},{2,0},{3,1},{4,2},{5,3},{6,4},{7,5},{8,14},{9,15},{10,... | collective-permute-start | bytes 1572872 | tf_op jit(solution)/shard_map/ppermute | solution.py:120
  51.7 14.4 %collective-permute-start.2 = (bf16[2,512,256]{2,1,0:T(8,128)(2,1)S(1)}, bf16[2,512,256]{2,1,0:T(8,128)(2,1)S(1)}, u32[]{:S(2)}, u32[]{:S(2)}) collective-permute-start(bf16[2,512,256]{2,1,0:T(8,128)(2,1)S(1)} %mix.1.mine_ref), channel_id=1, source_target_pairs={{0,2},{1,3},{2,4},{3,5},{4,6},{5,7},{6,0},{7,1},{8,10},{9,11},{10,... | collective-permute-start | bytes 1572872 | tf_op jit(solution)/shard_map/ppermute | solution.py:120
  66.0 2.8 %collective-permute-start.5 = (bf16[2,512,256]{2,1,0:T(8,128)(2,1)S(1)}, bf16[2,512,256]{2,1,0:T(8,128)(2,1)S(1)}, u32[]{:S(2)}, u32[]{:S(2)}) collective-permute-start(bf16[2,512,256]{2,1,0:T(8,128)(2,1)S(1)} %collective-permute-done.1.refs_0_), channel_id=1, source_target_pairs={{0,1},{1,0},{2,3},{3,2},{4,5},{5,4},{6,7},{7,6},{8,9},{9,8},{10,11... | collective-permute-start | bytes 1572872 | tf_op jit(solution)/shard_map/ppermute | solution.py:124
  67.2 2.3 %collective-permute-start.6 = (bf16[2,512,256]{2,1,0:T(8,128)(2,1)S(1)}, bf16[2,512,256]{2,1,0:T(8,128)(2,1)S(1)}, u32[]{:S(2)}, u32[]{:S(2)}) collective-permute-start(bf16[2,512,256]{2,1,0:T(8,128)(2,1)S(1)} %collective-permute-done.2.refs_1_), channel_id=1, source_target_pairs={{0,1},{1,0},{2,3},{3,2},{4,5},{5,4},{6,7},{7,6},{8,9},{9,8},{10,11... | collective-permute-start | bytes 1572872 | tf_op jit(solution)/shard_map/ppermute | solution.py:124
  67.3 7.4 %collective-permute-start.3 = (bf16[1,512,256]{2,1,0:T(8,128)(2,1)S(1)}, bf16[1,512,256]{2,1,0:T(8,128)(2,1)S(1)}, u32[]{:S(2)}, u32[]{:S(2)}) collective-permute-start(bf16[1,512,256]{2,1,0:T(8,128)(2,1)S(1)} %slice.6), channel_id=1, source_target_pairs={{0,6},{1,7},{2,0},{3,1},{4,2},{5,3},{6,4},{7,5},{8,14},{9,15},{10,... | collective-permute-start | bytes 786440 | tf_op jit(solution)/shard_map/ppermute | solution.py:120
  67.4 8.4 %collective-permute-start.4 = (bf16[1,512,256]{2,1,0:T(8,128)(2,1)S(1)}, bf16[1,512,256]{2,1,0:T(8,128)(2,1)S(1)}, u32[]{:S(2)}, u32[]{:S(2)}) collective-permute-start(bf16[1,512,256]{2,1,0:T(8,128)(2,1)S(1)} %slice.7), channel_id=1, source_target_pairs={{0,2},{1,3},{2,4},{3,5},{4,6},{5,7},{6,0},{7,1},{8,10},{9,11},{10,... | collective-permute-start | bytes 786440 | tf_op jit(solution)/shard_map/ppermute | solution.py:120
  75.8 2.7 %collective-permute-start.7 = (bf16[1,512,256]{2,1,0:T(8,128)(2,1)S(1)}, bf16[1,512,256]{2,1,0:T(8,128)(2,1)S(1)}, u32[]{:S(2)}, u32[]{:S(2)}) collective-permute-start(bf16[1,512,256]{2,1,0:T(8,128)(2,1)S(1)} %collective-permute-done.3.refs_0_), channel_id=1, source_target_pairs={{0,1},{1,0},{2,3},{3,2},{4,5},{5,4},{6,7},{7,6},{8,9},{9,8},{10,11... | collective-permute-start | bytes 786440 | tf_op jit(solution)/shard_map/ppermute | solution.py:124
  77.4 1.5 %collective-permute-start.8 = (bf16[1,512,256]{2,1,0:T(8,128)(2,1)S(1)}, bf16[1,512,256]{2,1,0:T(8,128)(2,1)S(1)}, u32[]{:S(2)}, u32[]{:S(2)}) collective-permute-start(bf16[1,512,256]{2,1,0:T(8,128)(2,1)S(1)} %collective-permute-done.4.refs_1_), channel_id=1, source_target_pairs={{0,1},{1,0},{2,3},{3,2},{4,5},{5,4},{6,7},{7,6},{8,9},{9,8},{10,11... | collective-permute-start | bytes 786440 | tf_op jit(solution)/shard_map/ppermute | solution.py:124

commit v3 on v2

--- a/solution.py
+++ b/solution.py
@@ -12,23 +12,19 @@
 
 
 def tables(blocks, rows):
-    length = blocks * rows
     freq = np.arange(blocks) + 0.25
     turn = 2 * np.pi * np.outer(freq, np.arange(blocks)) / blocks
     same = np.eye(GROUP)
-    first = np.concatenate([np.kron(np.cos(turn), same), np.kron(-np.sin(turn), same)], axis=0)
-    last = np.concatenate([np.kron(np.cos(turn.T), same), np.kron(-np.sin(turn.T), same)], axis=1)
-    twist = np.repeat(2 * np.pi * np.outer(freq, np.arange(rows)) / length, GROUP, axis=0)
+    outer = np.concatenate([np.kron(np.cos(turn), same), np.kron(-np.sin(turn), same)], axis=0)
+    twist = np.repeat(2 * np.pi * np.outer(freq, np.arange(rows)) / (blocks * rows), GROUP, axis=0)
     index = np.arange(rows)
     inner = 2 * np.pi * (np.outer(index, index) % rows) / rows
     cos, sin = np.cos(inner), np.sin(inner)
     middle = np.block([[cos, -sin], [sin, cos]])
     return (
-        first.astype(jnp.bfloat16),
+        outer.astype(jnp.bfloat16),
         middle.astype(jnp.bfloat16),
-        (last / length).astype(jnp.bfloat16),
-        np.cos(twist).astype(np.float32),
-        np.sin(twist).astype(np.float32),
+        np.stack([np.cos(twist), np.sin(twist)]).astype(np.float32),
     )
 
 
@@ -37,37 +33,33 @@
 
 
 def turn_kernel(signal_ref, filt_ref, out_ref):
-    share = out_ref.shape[1] // 2
+    ways, share, _ = out_ref.shape
+    rows = signal_ref.shape[0]
     for part, ref in enumerate((signal_ref, filt_ref)):
         flipped = ref[...].astype(jnp.float32).T.astype(jnp.bfloat16)
-        out_ref[:, part * share : (part + 1) * share, :] = flipped.reshape(-1, share, flipped.shape[1])
+        out_ref[:, :, part * rows : (part + 1) * rows] = flipped.reshape(ways, share, rows)
 
 
 def turn(signal, filt, ways):
     rows, channels = signal.shape
-    share = channels // ways
-    lanes = 128
     return pl.pallas_call(
         turn_kernel,
-        grid=(channels // lanes,),
-        in_specs=[pl.BlockSpec((rows, lanes), lambda b: (0, b))] * 2,
-        out_specs=pl.BlockSpec((lanes // share, 2 * share, rows), lambda b: (b, 0, 0)),
-        out_shape=jax.ShapeDtypeStruct((ways, 2 * share, rows), jnp.bfloat16),
-        compiler_params=pltpu.CompilerParams(vmem_limit_bytes=8 * 2**20),
+        out_shape=jax.ShapeDtypeStruct((ways, channels // ways, 2 * rows), jnp.bfloat16),
+        compiler_params=pltpu.CompilerParams(vmem_limit_bytes=12 * 2**20),
         name="turn",
     )(signal, filt)
 
 
-def conv_kernel(x_ref, first_ref, middle_ref, last_ref, cos_ref, sin_ref, out_ref):
-    blocks, doubled, rows = x_ref.shape
-    share = doubled // 2
+def conv_kernel(x_ref, outer_ref, middle_ref, twist_ref, out_ref):
+    blocks, share, rows = out_ref.shape
     half = blocks * GROUP
-    cos, sin = cos_ref[...], sin_ref[...]
+    cos, sin = twist_ref[0], twist_ref[1]
+    scale = 1.0 / (blocks * rows)
     for start in range(0, share, GROUP):
         parts = []
-        for base in (start, share + start):
-            x = x_ref[:, base : base + GROUP, :].reshape(half, rows)
-            a = dot(first_ref[...], x)
+        for lane in (0, rows):
+            x = x_ref[:, start : start + GROUP, lane : lane + rows].reshape(half, rows)
+            a = dot(outer_ref[...], x)
             re, im = a[:half], a[half:]
             parts.append(
                 jnp.concatenate([re * cos + im * sin, im * cos - re * sin], axis=1).astype(jnp.bfloat16)
@@ -81,35 +73,43 @@
         )
         re, im = back[:, :rows], back[:, rows:]
         untwisted = jnp.concatenate([re * cos - im * sin, re * sin + im * cos], axis=0).astype(jnp.bfloat16)
-        y = dot(last_ref[...], untwisted)
+        y = scale * lax.dot_general(
+            outer_ref[...], untwisted, (((0,), (0,)), ((), ())), preferred_element_type=jnp.float32
+        )
         out_ref[:, start : start + GROUP, :] = y.reshape(blocks, GROUP, rows).astype(jnp.bfloat16)
 
 
 def convolve(x):
-    blocks, doubled, rows = x.shape
+    blocks, share, rows = x.shape[0], x.shape[1], x.shape[2] // 2
     constants = [jnp.asarray(t) for t in tables(blocks, rows)]
     return pl.pallas_call(
         conv_kernel,
-        out_shape=jax.ShapeDtypeStruct((blocks, doubled // 2, rows), jnp.bfloat16),
+        out_shape=jax.ShapeDtypeStruct((blocks, share, rows), jnp.bfloat16),
         compiler_params=pltpu.CompilerParams(vmem_limit_bytes=20 * 2**20),
         name="convolve",
     )(x, *constants)
 
 
-def mix_kernel(conv_ref, signal_ref, gate_ref, skip_ref, out_ref):
+def mix_kernel(conv_ref, signal_ref, gate_ref, skip_ref, out_ref, low_ref, high_ref):
     conv = conv_ref[...].astype(jnp.float32).T
     values = signal_ref[...].astype(jnp.float32)
     mixed = (gate_ref[...].astype(jnp.float32) * (conv + skip_ref[...] * values)).astype(jnp.bfloat16)
     width = out_ref.shape[2]
-    for half in range(2):
-        out_ref[half] = mixed[:, half * width : (half + 1) * width]
+    for half, half_ref in enumerate((low_ref, high_ref)):
+        part = mixed[:, half * width : (half + 1) * width]
+        out_ref[half] = part
+        half_ref[...] = part
 
 
 def mix(conv, signal, gate, skip):
     rows, channels = signal.shape
     return pl.pallas_call(
         mix_kernel,
-        out_shape=jax.ShapeDtypeStruct((2, rows, channels // 2), jnp.bfloat16),
+        out_shape=[
+            jax.ShapeDtypeStruct((2, rows, channels // 2), jnp.bfloat16),
+            jax.ShapeDtypeStruct((rows, channels // 2), jnp.bfloat16),
+            jax.ShapeDtypeStruct((rows, channels // 2), jnp.bfloat16),
+        ],
         compiler_params=pltpu.CompilerParams(vmem_limit_bytes=8 * 2**20),
         name="mix",
     )(conv, signal, gate, skip.reshape(1, channels))
@@ -160,7 +160,7 @@
 
 def later_kernel(first, weights_ref, *refs):
     blocks, total_ref, out_ref = refs[:-2], refs[-2], refs[-1]
-    left = jnp.concatenate([block[half] for block in blocks for half in range(block.shape[0])], axis=1)
+    left = jnp.concatenate([block[...] for block in blocks], axis=1)
     add_product(left, weights_ref, first, total_ref, out_ref)
 
 
@@ -177,7 +177,7 @@
 
 def later_call(weights, first, blocks, total, dtype, name):
     rows, columns = total.shape
-    depth = sum(block.shape[0] for block in blocks) * weights.shape[1]
+    depth = len(blocks) * weights.shape[1]
     return pl.pallas_call(
         functools.partial(later_kernel, first),
         in_specs=[VMEM] * (2 + len(blocks)),
@@ -189,7 +189,7 @@
     )(weights, *blocks, total)
 
 
-def project(mixed, w_out):
+def project(mixed, low, high, w_out):
     width, columns = mixed.shape[2], w_out.shape[1]
     rows = mixed.shape[1]
     weights = w_out.reshape(-1, width, columns)
@@ -198,8 +198,10 @@
     far = [(other, 4, half) for other in (0, 1) for half in (0, 1)]
     later = near + far
 
-    right, left = shifted(mixed, -2), shifted(mixed, 2)
+    right_low, left_high = shifted(low, -2), shifted(high, 2)
     beside = swapped(mixed)
+    low, high, beside = lax.optimization_barrier((low, high, beside))
+    right_high, left_low = shifted(high, -2), shifted(low, 2)
     total, weights = pl.pallas_call(
         functools.partial(first_kernel, own, later),
         in_specs=[pl.BlockSpec(memory_space=pl.ANY), VMEM, VMEM],
@@ -212,21 +214,18 @@
             pltpu.VMEM((len(own), width, columns), weights.dtype),
             pltpu.SemaphoreType.DMA((len(own) + len(later),)),
         ],
-        compiler_params=pltpu.CompilerParams(vmem_limit_bytes=14 * 2**20),
+        compiler_params=pltpu.CompilerParams(vmem_limit_bytes=44 * 2**20),
         cost_estimate=cost(rows, len(own) * width, columns),
         name="project_own",
     )(weights, mixed, beside)
-    right, left, total = lax.optimization_barrier((right, left, total))
-    far_low, far_high = shifted(right[:1], -2), shifted(left[1:], 2)
-    beside_right, beside_left = swapped(right), swapped(left)
-    total = later_call(
-        weights, 0, [right, left, beside_right, beside_left], total, jnp.float32, "project_near"
-    )
-    far_low, far_high, total = lax.optimization_barrier((far_low, far_high, total))
+    right_low, left_high, total = lax.optimization_barrier((right_low, left_high, total))
+    far_low, far_high = shifted(right_low, -2), shifted(left_high, 2)
+    near_blocks = [right_low, right_high, left_low, left_high]
+    near_blocks += [swapped(block) for block in near_blocks]
+    *near_blocks, far_low, far_high, total = lax.optimization_barrier((*near_blocks, far_low, far_high, total))
     beside_low, beside_high = swapped(far_low), swapped(far_high)
-    return later_call(
-        weights, len(near), [far_low, far_high, beside_low, beside_high], total, jnp.bfloat16, "project_far"
-    )
+    total = later_call(weights, 0, [*near_blocks, far_low, far_high], total, jnp.float32, "project_near")
+    return later_call(weights, len(near) + 2, [beside_low, beside_high], total, jnp.bfloat16, "project_last")
 
 
 def per_device(signal, gate, filt, skip, w_out):
@@ -234,7 +233,7 @@
     rows, channels = signal.shape
     spread = lax.all_to_all(turn(signal, filt, ways), "ctx", 0, 0, tiled=True)
     conv = lax.all_to_all(convolve(spread), "ctx", 0, 0, tiled=True)
-    return project(mix(conv.reshape(channels, rows), signal, gate, skip), w_out)
+    return project(*mix(conv.reshape(channels, rows), signal, gate, skip), w_out)
 
 
 def solution(mesh):

time: 81.4 us -> 77.4 us (0.951)
  waiting for transfers between devices: 18.4 us -> 7.63 us
  starting transfers between devices: 9.46 us -> 15.3 us
  Pallas kernels: 13 us -> 14 us
    ppermute x4 -> x6, waiting for transfers between devices: 16.2 us -> 7.61 us  [shifted(): lax.ppermute(block, 'tp', [(i, (i + step) % count) for i in range(count)])]
    ppermute x4 -> x6, starting transfers between devices: 4.03 us -> 7.23 us  [shifted(): lax.ppermute(block, 'tp', [(i, (i + step) % count) for i in range(count)])]
    ppermute x5 -> x7, starting transfers between devices: 5.43 us -> 8.08 us  [swapped(): lax.ppermute(block, 'tp', [(i, i ^ 1) for i in range(lax.axis_size('tp'))])]
    ppermute x5 -> x7, waiting for transfers between devices: 2.23 us -> 0.02 us  [swapped(): lax.ppermute(block, 'tp', [(i, i ^ 1) for i in range(lax.axis_size('tp'))])]
    pallas_call x1, Pallas kernels: 2.08 us -> 3.53 us  [project(): pl.pallas_call(functools.partial(first_kernel, own, later), in_specs=[pl....]
    unnamed x22 -> x16, local copies, waits for them, and re-layouts: 2.31 us -> 2.3 us
  transfers between devices with their start and end apart: 9 -> 13, of which waited for: 7 -> 4; matrix products, arithmetic and copies ran while one was open for 0% -> 0% of each run, Pallas kernels for 5% -> 8%
where the time goes in v3:
time: 77.4 us; the launch traced here: 77.1 us
  blocking collectives  37.7 us (49%)
  starting transfers between devices  15.3 us (20%)
  Pallas kernels  14 us (18%)
  waiting for transfers between devices  7.63 us (10%)
  local copies, waits for them, and re-layouts  2.3 us (3%)
    all_to_all x1, blocking collectives, per_device(): spread = lax.all_to_all(turn(signal, filt, ways), 'ctx', 0, 0, tiled=True)  24.7 us
    all_to_all x1, blocking collectives, per_device(): conv = lax.all_to_all(convolve(spread), 'ctx', 0, 0, tiled=True)  13.1 us
    ppermute x7, starting transfers between devices, swapped(): lax.ppermute(block, 'tp', [(i, i ^ 1) for i in range(lax.axis_size('tp'))])  8.08 us
    ppermute x6, waiting for transfers between devices, shifted(): lax.ppermute(block, 'tp', [(i, (i + step) % count) for i in range(count)])  7.61 us
    ppermute x6, starting transfers between devices, shifted(): lax.ppermute(block, 'tp', [(i, (i + step) % count) for i in range(count)])  7.23 us
    pallas_call x1, Pallas kernels, convolve(): pl.pallas_call(conv_kernel, out_shape=jax.ShapeDtypeStruct((blocks, share...  5.33 us
    pallas_call x2, Pallas kernels, later_call(): pl.pallas_call(functools.partial(later_kernel, first), in_specs=[VMEM] *...  4.55 us
    pallas_call x1, Pallas kernels, project(): pl.pallas_call(functools.partial(first_kernel, own, later), in_specs=[pl....  3.53 us
  transfers between devices with their start and end apart: 13, of which 4 were waited for; matrix products, arithmetic and copies ran while one was open for 0% of the time, Pallas kernels for 8%

profile of v3, /device:TPU:1, one launch (start us, length us, event | category | flops | bytes accessed | tf_op | source)
XLA Modules:
  0.0 77.1 jit_solution(9520406376295443583)
XLA Ops:
  0.0 1.0 %copy-done = bf16[512,512]{1,0:T(8,128)(2,1)S(1)} copy-done((bf16[512,512]{1,0:T(8,128)(2,1)S(1)}, bf16[512,512]{1,0:T(8,128)(2,1)}, u32[]{:S(2)}) %copy-start) | copy-done | bytes 524312
  1.0 1.2 %copy-done.4 = f32[512,512]{1,0:T(8,128)S(1)} copy-done((f32[512,512]{1,0:T(8,128)S(1)}, f32[512,512]{1,0:T(8,128)}, u32[]{:S(2)}) %copy-start.4) | copy-done | bytes 1048600
  2.3 0.4 turn.1
  2.6 24.7 %all_to_all.10.x_ref = bf16[16,32,1024]{2,1,0:T(8,128)(2,1)S(1)} all-to-all(bf16[16,32,1024]{2,1,0:T(8,128)(2,1)S(1)} %turn.1), channel_id=1, replica_groups=mesh['ctx'=16,'tp'=8] {'ctx'}, dimensions={0} | all-to-all | bytes 2097152 | tf_op jit(solution)/shard_map/all_to_all | solution.py:234
  27.3 0.0 copy-start.1
  27.3 0.0 copy-start.5
  27.3 0.0 copy-start.7
  27.3 5.3 %convolve.1 = bf16[16,32,512]{2,1,0:T(8,128)(2,1)S(1)} custom-call(bf16[16,32,1024]{2,1,0:T(8,128)(2,1)S(1)} %all_to_all.10.x_ref, bf16[512,256]{1,0:T(8,128)(2,1)S(1)} %copy-done.6, bf16[1024,1024]{1,0:T(8,128)(2,1)S(1)} %copy-done.2, f32[2,256,512]{2,1,0:T(8,128)S(1)} %copy-done.3), custom_call_target="tpu_custom_call" | custom-call | tf_op jit(solution)/shard_map/convolve/pallas_call | solution.py:85
  32.7 13.1 %all_to_all.11 = bf16[16,32,512]{2,1,0:T(8,128)(2,1)S(1)} all-to-all(bf16[16,32,512]{2,1,0:T(8,128)(2,1)S(1)} %convolve.1), channel_id=1, replica_groups=mesh['ctx'=16,'tp'=8] {'ctx'}, dimensions={0} | all-to-all | bytes 1048576 | tf_op jit(solution)/shard_map/all_to_all | solution.py:235
  45.8 0.3 mix.1
  46.0 2.6 %collective-permute-start = (bf16[2,512,256]{2,1,0:T(8,128)(2,1)S(1)}, bf16[2,512,256]{2,1,0:T(8,128)(2,1)S(1)}, u32[]{:S(2)}, u32[]{:S(2)}) collective-permute-start(bf16[2,512,256]{2,1,0:T(8,128)(2,1)S(1)} %get-tuple-element.27.mine_ref), channel_id=1, source_target_pairs={{0,1},{1,0},{2,3},{3,2},{4,5},{5,4},{6,7},{7,6},{8,9},{9,8},{10,11... | collective-permute-start | bytes 1572872 | tf_op jit(solution)/shard_map/ppermute | solution.py:124
  48.7 2.5 %collective-permute-start.1 = (bf16[512,256]{1,0:T(8,128)(2,1)S(1)}, bf16[512,256]{1,0:T(8,128)(2,1)S(1)}, u32[]{:S(2)}, u32[]{:S(2)}) collective-permute-start(bf16[512,256]{1,0:T(8,128)(2,1)S(1)} %get-tuple-element.35), channel_id=1, source_target_pairs={{0,6},{1,7},{2,0},{3,1},{4,2},{5,3},{6,4},{7,5},{8,14},{9,15},{10,... | collective-permute-start | bytes 786440 | tf_op jit(solution)/shard_map/ppermute | solution.py:120
  51.2 0.0 collective-permute-start.2
  51.2 0.0 collective-permute-done.beside_ref
  51.2 2.7 %collective-permute-start.3 = (bf16[512,256]{1,0:T(8,128)(2,1)S(1)}, bf16[512,256]{1,0:T(8,128)(2,1)S(1)}, u32[]{:S(2)}, u32[]{:S(2)}) collective-permute-start(bf16[512,256]{1,0:T(8,128)(2,1)S(1)} %get-tuple-element.34), channel_id=1, source_target_pairs={{0,6},{1,7},{2,0},{3,1},{4,2},{5,3},{6,4},{7,5},{8,14},{9,15},{10,... | collective-permute-start | bytes 786440 | tf_op jit(solution)/shard_map/ppermute | solution.py:120
  53.9 0.0 collective-permute-start.4
  53.9 3.5 %project_own.1 = (f32[512,1024]{1,0:T(8,128)S(1)}, bf16[12,256,1024]{2,1,0:T(8,128)(2,1)S(1)}) custom-call(bf16[16,256,1024]{2,1,0:T(8,128)(2,1)} %bitcast.5, bf16[2,512,256]{2,1,0:T(8,128)(2,1)S(1)} %get-tuple-element.27.mine_ref, bf16[2,512,256]{2,1,0:T(8,128)(2,1)S(1)} %collective-permute-done.beside_ref), custom_call_target="tpu_custom_call" | custom-call | flops 1073741824 | bytes 7340032 | tf_op jit(solution)/shard_map/project_own/pallas_call | solution.py:205
  57.4 0.0 collective-permute-done.1.refs_0_
  57.4 2.5 %collective-permute-done.2.refs_3_ = bf16[512,256]{1,0:T(8,128)(2,1)S(1)} collective-permute-done((bf16[512,256]{1,0:T(8,128)(2,1)S(1)}, bf16[512,256]{1,0:T(8,128)(2,1)S(1)}, u32[]{:S(2)}, u32[]{:S(2)}) %collective-permute-start.2) | collective-permute-done | bytes 262176 | tf_op jit(solution)/shard_map/ppermute | solution.py:120
  59.9 0.3 collective-permute-start.9
  60.3 1.6 %collective-permute-start.5 = (bf16[512,256]{1,0:T(8,128)(2,1)S(1)}, bf16[512,256]{1,0:T(8,128)(2,1)S(1)}, u32[]{:S(2)}, u32[]{:S(2)}) collective-permute-start(bf16[512,256]{1,0:T(8,128)(2,1)S(1)} %collective-permute-done.1.refs_0_), channel_id=1, source_target_pairs={{0,1},{1,0},{2,3},{3,2},{4,5},{5,4},{6,7},{7,6},{8,9},{9,8},{10,11... | collective-permute-start | bytes 786440 | tf_op jit(solution)/shard_map/ppermute | solution.py:124
  61.9 1.7 %collective-permute-start.10 = (bf16[512,256]{1,0:T(8,128)(2,1)S(1)}, bf16[512,256]{1,0:T(8,128)(2,1)S(1)}, u32[]{:S(2)}, u32[]{:S(2)}) collective-permute-start(bf16[512,256]{1,0:T(8,128)(2,1)S(1)} %collective-permute-done.2.refs_3_), channel_id=1, source_target_pairs={{0,2},{1,3},{2,4},{3,5},{4,6},{5,7},{6,0},{7,1},{8,10},{9,11},{10,... | collective-permute-start | bytes 786440 | tf_op jit(solution)/shard_map/ppermute | solution.py:120
  63.6 0.3 collective-permute-start.8
  63.9 1.6 %collective-permute-done.4.refs_2_ = bf16[512,256]{1,0:T(8,128)(2,1)S(1)} collective-permute-done((bf16[512,256]{1,0:T(8,128)(2,1)S(1)}, bf16[512,256]{1,0:T(8,128)(2,1)S(1)}, u32[]{:S(2)}, u32[]{:S(2)}) %collective-permute-start.4) | collective-permute-done | bytes 262176 | tf_op jit(solution)/shard_map/ppermute | solution.py:120
  65.5 1.6 %collective-permute-start.6 = (bf16[512,256]{1,0:T(8,128)(2,1)S(1)}, bf16[512,256]{1,0:T(8,128)(2,1)S(1)}, u32[]{:S(2)}, u32[]{:S(2)}) collective-permute-start(bf16[512,256]{1,0:T(8,128)(2,1)S(1)} %collective-permute-done.3.refs_1_), channel_id=1, source_target_pairs={{0,1},{1,0},{2,3},{3,2},{4,5},{5,4},{6,7},{7,6},{8,9},{9,8},{10,11... | collective-permute-start | bytes 786440 | tf_op jit(solution)/shard_map/ppermute | solution.py:124
  67.2 0.9 %collective-permute-done.9.refs_8_ = bf16[512,256]{1,0:T(8,128)(2,1)S(1)} collective-permute-done((bf16[512,256]{1,0:T(8,128)(2,1)S(1)}, bf16[512,256]{1,0:T(8,128)(2,1)S(1)}, u32[]{:S(2)}, u32[]{:S(2)}) %collective-permute-start.9) | collective-permute-done | bytes 262176 | tf_op jit(solution)/shard_map/ppermute | solution.py:120
  68.1 0.9 %collective-permute-start.7 = (bf16[512,256]{1,0:T(8,128)(2,1)S(1)}, bf16[512,256]{1,0:T(8,128)(2,1)S(1)}, u32[]{:S(2)}, u32[]{:S(2)}) collective-permute-start(bf16[512,256]{1,0:T(8,128)(2,1)S(1)} %collective-permute-done.4.refs_2_), channel_id=1, source_target_pairs={{0,1},{1,0},{2,3},{3,2},{4,5},{5,4},{6,7},{7,6},{8,9},{9,8},{10,11... | collective-permute-start | bytes 786440 | tf_op jit(solution)/shard_map/ppermute | solution.py:124
  68.9 2.6 %collective-permute-done.10.refs_9_ = bf16[512,256]{1,0:T(8,128)(2,1)S(1)} collective-permute-done((bf16[512,256]{1,0:T(8,128)(2,1)S(1)}, bf16[512,256]{1,0:T(8,128)(2,1)S(1)}, u32[]{:S(2)}, u32[]{:S(2)}) %collective-permute-start.10) | collective-permute-done | bytes 262176 | tf_op jit(solution)/shard_map/ppermute | solution.py:120
  71.5 0.9 %collective-permute-start.11 = (bf16[512,256]{1,0:T(8,128)(2,1)S(1)}, bf16[512,256]{1,0:T(8,128)(2,1)S(1)}, u32[]{:S(2)}, u32[]{:S(2)}) collective-permute-start(bf16[512,256]{1,0:T(8,128)(2,1)S(1)} %collective-permute-done.9.refs_8_), channel_id=1, source_target_pairs={{0,1},{1,0},{2,3},{3,2},{4,5},{5,4},{6,7},{7,6},{8,9},{9,8},{10,11... | collective-permute-start | bytes 786440 | tf_op jit(solution)/shard_map/ppermute | solution.py:124
  72.4 0.1 collective-permute-start.12
  72.5 2.9 %project_near.1.refs_2_ = f32[512,1024]{1,0:T(8,128)S(1)} custom-call(bf16[12,256,1024]{2,1,0:T(8,128)(2,1)S(1)} %get-tuple-element.31.weights_ref, bf16[512,256]{1,0:T(8,128)(2,1)S(1)} %collective-permute-done.1.refs_0_, bf16[512,256]{1,0:T(8,128)(2,1)S(1)} %collective-permute-done.3.refs_1_, bf16[512,256]{1,0:T(8,128)(2,1)S(1)} %collective-permute-done.4.refs_2_, ...), custom_call_target="tpu_custom_call" | custom-call | flops 2684354560 | bytes 12058624 | tf_op jit(solution)/shard_map/project_near/pallas_call | solution.py:181
  75.4 1.7 %project_last.1 = bf16[512,1024]{1,0:T(8,128)(2,1)} custom-call(bf16[12,256,1024]{2,1,0:T(8,128)(2,1)S(1)} %get-tuple-element.31.weights_ref, bf16[512,256]{1,0:T(8,128)(2,1)S(1)} %collective-permute-done.11.refs_0_, bf16[512,256]{1,0:T(8,128)(2,1)S(1)} %collective-permute-done.12.refs_1_, f32[512,1024]{1,0:T(8,128)S(1)} %project_near.1.refs_2_), custom_call_target="tpu_custom_call" | custom-call | flops 536870912 | bytes 5767168 | tf_op jit(solution)/shard_map/project_last/pallas_call | solution.py:181
  (18 shorter events, 0.0 us)
Async XLA Ops:
  0.0 1.0 %copy-start = (bf16[512,512]{1,0:T(8,128)(2,1)S(1)}, bf16[512,512]{1,0:T(8,128)(2,1)}, u32[]{:S(2)}) copy-start(bf16[512,512]{1,0:T(8,128)(2,1)} %signal_ref.3) | copy-start | bytes 1572868
  1.0 1.2 %copy-start.4 = (f32[512,512]{1,0:T(8,128)S(1)}, f32[512,512]{1,0:T(8,128)}, u32[]{:S(2)}) copy-start(f32[512,512]{1,0:T(8,128)} %filt_ref.1) | copy-start | bytes 3145732
  2.3 25.0 %copy-start.2 = (bf16[1024,1024]{1,0:T(8,128)(2,1)S(1)}, bf16[1024,1024]{1,0:T(8,128)(2,1)}, u32[]{:S(2)}) copy-start(bf16[1024,1024]{1,0:T(8,128)(2,1)} %constant.7.clone.middle_ref) | copy-start | bytes 6291460
  2.3 25.0 %copy-start.3 = (f32[2,256,512]{2,1,0:T(8,128)S(1)}, f32[2,256,512]{2,1,0:T(8,128)}, u32[]{:S(2)}) copy-start(f32[2,256,512]{2,1,0:T(8,128)} %constant.8.clone.twist_ref) | copy-start | bytes 3145732
  2.3 25.0 %copy-start.6 = (bf16[512,256]{1,0:T(8,128)(2,1)S(1)}, bf16[512,256]{1,0:T(8,128)(2,1)}, u32[]{:S(2)}) copy-start(bf16[512,256]{1,0:T(8,128)(2,1)} %constant.6.clone.outer_ref) | copy-start | bytes 786436
  27.3 18.5 %copy-start.1 = (bf16[512,512]{1,0:T(8,128)(2,1)S(1)}, bf16[512,512]{1,0:T(8,128)(2,1)}, u32[]{:S(2)}) copy-start(bf16[512,512]{1,0:T(8,128)(2,1)} %signal_ref.3) | copy-start | bytes 1572868
  27.3 18.4 %copy-start.5 = (bf16[512,512]{1,0:T(8,128)(2,1)S(1)}, bf16[512,512]{1,0:T(8,128)(2,1)}, u32[]{:S(2)}) copy-start(bf16[512,512]{1,0:T(8,128)(2,1)} %gate_ref.1) | copy-start | bytes 1572868
  27.3 18.4 %copy-start.7 = (f32[512]{0:T(512)S(1)}, f32[512]{0:T(512)}, u32[]{:S(2)}) copy-start(f32[512]{0:T(512)} %param.11) | copy-start | bytes 6148
  46.0 5.1 %collective-permute-start = (bf16[2,512,256]{2,1,0:T(8,128)(2,1)S(1)}, bf16[2,512,256]{2,1,0:T(8,128)(2,1)S(1)}, u32[]{:S(2)}, u32[]{:S(2)}) collective-permute-start(bf16[2,512,256]{2,1,0:T(8,128)(2,1)S(1)} %get-tuple-element.27.mine_ref), channel_id=1, source_target_pairs={{0,1},{1,0},{2,3},{3,2},{4,5},{5,4},{6,7},{7,6},{8,9},{9,8},{10,11... | collective-permute-start | bytes 1572872 | tf_op jit(solution)/shard_map/ppermute | solution.py:124
  48.7 8.7 %collective-permute-start.1 = (bf16[512,256]{1,0:T(8,128)(2,1)S(1)}, bf16[512,256]{1,0:T(8,128)(2,1)S(1)}, u32[]{:S(2)}, u32[]{:S(2)}) collective-permute-start(bf16[512,256]{1,0:T(8,128)(2,1)S(1)} %get-tuple-element.35), channel_id=1, source_target_pairs={{0,6},{1,7},{2,0},{3,1},{4,2},{5,3},{6,4},{7,5},{8,14},{9,15},{10,... | collective-permute-start | bytes 786440 | tf_op jit(solution)/shard_map/ppermute | solution.py:120
  51.2 8.8 %collective-permute-start.2 = (bf16[512,256]{1,0:T(8,128)(2,1)S(1)}, bf16[512,256]{1,0:T(8,128)(2,1)S(1)}, u32[]{:S(2)}, u32[]{:S(2)}) collective-permute-start(bf16[512,256]{1,0:T(8,128)(2,1)S(1)} %get-tuple-element.34), channel_id=1, source_target_pairs={{0,2},{1,3},{2,4},{3,5},{4,6},{5,7},{6,0},{7,1},{8,10},{9,11},{10,... | collective-permute-start | bytes 786440 | tf_op jit(solution)/shard_map/ppermute | solution.py:120
  51.2 12.5 %collective-permute-start.3 = (bf16[512,256]{1,0:T(8,128)(2,1)S(1)}, bf16[512,256]{1,0:T(8,128)(2,1)S(1)}, u32[]{:S(2)}, u32[]{:S(2)}) collective-permute-start(bf16[512,256]{1,0:T(8,128)(2,1)S(1)} %get-tuple-element.34), channel_id=1, source_target_pairs={{0,6},{1,7},{2,0},{3,1},{4,2},{5,3},{6,4},{7,5},{8,14},{9,15},{10,... | collective-permute-start | bytes 786440 | tf_op jit(solution)/shard_map/ppermute | solution.py:120
  53.9 11.7 %collective-permute-start.4 = (bf16[512,256]{1,0:T(8,128)(2,1)S(1)}, bf16[512,256]{1,0:T(8,128)(2,1)S(1)}, u32[]{:S(2)}, u32[]{:S(2)}) collective-permute-start(bf16[512,256]{1,0:T(8,128)(2,1)S(1)} %get-tuple-element.35), channel_id=1, source_target_pairs={{0,2},{1,3},{2,4},{3,5},{4,6},{5,7},{6,0},{7,1},{8,10},{9,11},{10,... | collective-permute-start | bytes 786440 | tf_op jit(solution)/shard_map/ppermute | solution.py:120
  59.9 8.1 %collective-permute-start.9 = (bf16[512,256]{1,0:T(8,128)(2,1)S(1)}, bf16[512,256]{1,0:T(8,128)(2,1)S(1)}, u32[]{:S(2)}, u32[]{:S(2)}) collective-permute-start(bf16[512,256]{1,0:T(8,128)(2,1)S(1)} %collective-permute-done.1.refs_0_), channel_id=1, source_target_pairs={{0,6},{1,7},{2,0},{3,1},{4,2},{5,3},{6,4},{7,5},{8,14},{9,15},{10,... | collective-permute-start | bytes 786440 | tf_op jit(solution)/shard_map/ppermute | solution.py:120
  60.3 8.7 %collective-permute-start.5 = (bf16[512,256]{1,0:T(8,128)(2,1)S(1)}, bf16[512,256]{1,0:T(8,128)(2,1)S(1)}, u32[]{:S(2)}, u32[]{:S(2)}) collective-permute-start(bf16[512,256]{1,0:T(8,128)(2,1)S(1)} %collective-permute-done.1.refs_0_), channel_id=1, source_target_pairs={{0,1},{1,0},{2,3},{3,2},{4,5},{5,4},{6,7},{7,6},{8,9},{9,8},{10,11... | collective-permute-start | bytes 786440 | tf_op jit(solution)/shard_map/ppermute | solution.py:124
  61.9 9.6 %collective-permute-start.10 = (bf16[512,256]{1,0:T(8,128)(2,1)S(1)}, bf16[512,256]{1,0:T(8,128)(2,1)S(1)}, u32[]{:S(2)}, u32[]{:S(2)}) collective-permute-start(bf16[512,256]{1,0:T(8,128)(2,1)S(1)} %collective-permute-done.2.refs_3_), channel_id=1, source_target_pairs={{0,2},{1,3},{2,4},{3,5},{4,6},{5,7},{6,0},{7,1},{8,10},{9,11},{10,... | collective-permute-start | bytes 786440 | tf_op jit(solution)/shard_map/ppermute | solution.py:120
  63.6 7.9 %collective-permute-start.8 = (bf16[512,256]{1,0:T(8,128)(2,1)S(1)}, bf16[512,256]{1,0:T(8,128)(2,1)S(1)}, u32[]{:S(2)}, u32[]{:S(2)}) collective-permute-start(bf16[512,256]{1,0:T(8,128)(2,1)S(1)} %collective-permute-done.2.refs_3_), channel_id=1, source_target_pairs={{0,1},{1,0},{2,3},{3,2},{4,5},{5,4},{6,7},{7,6},{8,9},{9,8},{10,11... | collective-permute-start | bytes 786440 | tf_op jit(solution)/shard_map/ppermute | solution.py:124
  65.5 6.0 %collective-permute-start.6 = (bf16[512,256]{1,0:T(8,128)(2,1)S(1)}, bf16[512,256]{1,0:T(8,128)(2,1)S(1)}, u32[]{:S(2)}, u32[]{:S(2)}) collective-permute-start(bf16[512,256]{1,0:T(8,128)(2,1)S(1)} %collective-permute-done.3.refs_1_), channel_id=1, source_target_pairs={{0,1},{1,0},{2,3},{3,2},{4,5},{5,4},{6,7},{7,6},{8,9},{9,8},{10,11... | collective-permute-start | bytes 786440 | tf_op jit(solution)/shard_map/ppermute | solution.py:124
  68.1 3.4 %collective-permute-start.7 = (bf16[512,256]{1,0:T(8,128)(2,1)S(1)}, bf16[512,256]{1,0:T(8,128)(2,1)S(1)}, u32[]{:S(2)}, u32[]{:S(2)}) collective-permute-start(bf16[512,256]{1,0:T(8,128)(2,1)S(1)} %collective-permute-done.4.refs_2_), channel_id=1, source_target_pairs={{0,1},{1,0},{2,3},{3,2},{4,5},{5,4},{6,7},{7,6},{8,9},{9,8},{10,11... | collective-permute-start | bytes 786440 | tf_op jit(solution)/shard_map/ppermute | solution.py:124
  71.5 3.9 %collective-permute-start.11 = (bf16[512,256]{1,0:T(8,128)(2,1)S(1)}, bf16[512,256]{1,0:T(8,128)(2,1)S(1)}, u32[]{:S(2)}, u32[]{:S(2)}) collective-permute-start(bf16[512,256]{1,0:T(8,128)(2,1)S(1)} %collective-permute-done.9.refs_8_), channel_id=1, source_target_pairs={{0,1},{1,0},{2,3},{3,2},{4,5},{5,4},{6,7},{7,6},{8,9},{9,8},{10,11... | collective-permute-start | bytes 786440 | tf_op jit(solution)/shard_map/ppermute | solution.py:124
  72.4 3.0 %collective-permute-start.12 = (bf16[512,256]{1,0:T(8,128)(2,1)S(1)}, bf16[512,256]{1,0:T(8,128)(2,1)S(1)}, u32[]{:S(2)}, u32[]{:S(2)}) collective-permute-start(bf16[512,256]{1,0:T(8,128)(2,1)S(1)} %collective-permute-done.10.refs_9_), channel_id=1, source_target_pairs={{0,1},{1,0},{2,3},{3,2},{4,5},{5,4},{6,7},{7,6},{8,9},{9,8},{10,11... | collective-permute-start | bytes 786440 | tf_op jit(solution)/shard_map/ppermute | solution.py:124

commit v4 on v3

--- a/solution.py
+++ b/solution.py
@@ -12,19 +12,20 @@
 
 
 def tables(blocks, rows):
-    freq = np.arange(blocks) + 0.25
-    turn = 2 * np.pi * np.outer(freq, np.arange(blocks)) / blocks
+    coarse, fine = 2 * blocks, rows // 2
+    freq = np.arange(coarse) + 0.25
+    turn = 2 * np.pi * np.outer(freq, np.arange(coarse)) / coarse
+    turn = np.concatenate([turn[:, 0::2], turn[:, 1::2]], axis=1)
     same = np.eye(GROUP)
     outer = np.concatenate([np.kron(np.cos(turn), same), np.kron(-np.sin(turn), same)], axis=0)
-    twist = np.repeat(2 * np.pi * np.outer(freq, np.arange(rows)) / (blocks * rows), GROUP, axis=0)
-    index = np.arange(rows)
-    inner = 2 * np.pi * (np.outer(index, index) % rows) / rows
+    twist = np.repeat(2 * np.pi * np.outer(freq, np.arange(fine)) / (coarse * fine), GROUP, axis=0)
+    index = np.arange(fine)
+    inner = 2 * np.pi * (np.outer(index, index) % fine) / fine
     cos, sin = np.cos(inner), np.sin(inner)
     middle = np.block([[cos, -sin], [sin, cos]])
     return (
-        outer.astype(jnp.bfloat16),
-        middle.astype(jnp.bfloat16),
-        np.stack([np.cos(twist), np.sin(twist)]).astype(np.float32),
+        np.concatenate([outer, middle], axis=0).astype(jnp.bfloat16),
+        np.concatenate([np.cos(twist), np.sin(twist)], axis=1).astype(np.float32),
     )
 
 
@@ -50,33 +51,39 @@
     )(signal, filt)
 
 
-def conv_kernel(x_ref, outer_ref, middle_ref, twist_ref, out_ref):
+def conv_kernel(x_ref, table_ref, twist_ref, out_ref):
     blocks, share, rows = out_ref.shape
-    half = blocks * GROUP
-    cos, sin = twist_ref[0], twist_ref[1]
+    fine = rows // 2
+    half = 2 * blocks * GROUP
+    cos, sin = twist_ref[:, :fine], twist_ref[:, fine:]
+    outer_ref, middle_ref = table_ref.at[: 2 * half], table_ref.at[2 * half :]
     scale = 1.0 / (blocks * rows)
     for start in range(0, share, GROUP):
+        group = slice(start, start + GROUP)
         parts = []
         for lane in (0, rows):
-            x = x_ref[:, start : start + GROUP, lane : lane + rows].reshape(half, rows)
+            spans = [slice(lane, lane + fine), slice(lane + fine, lane + rows)]
+            x = jnp.concatenate([x_ref[:, group, span].reshape(blocks * GROUP, fine) for span in spans], axis=0)
             a = dot(outer_ref[...], x)
             re, im = a[:half], a[half:]
             parts.append(
                 jnp.concatenate([re * cos + im * sin, im * cos - re * sin], axis=1).astype(jnp.bfloat16)
             )
         spec = dot(jnp.concatenate(parts, axis=0), middle_ref[...])
-        xr, xi = spec[:half, :rows], spec[:half, rows:]
-        hr, hi = spec[half:, :rows], spec[half:, rows:]
+        xr, xi = spec[:half, :fine], spec[:half, fine:]
+        hr, hi = spec[half:, :fine], spec[half:, fine:]
         prod = jnp.concatenate([xr * hr - xi * hi, xr * hi + xi * hr], axis=1).astype(jnp.bfloat16)
         back = lax.dot_general(
             prod, middle_ref[...], (((1,), (1,)), ((), ())), preferred_element_type=jnp.float32
         )
-        re, im = back[:, :rows], back[:, rows:]
+        re, im = back[:, :fine], back[:, fine:]
         untwisted = jnp.concatenate([re * cos - im * sin, re * sin + im * cos], axis=0).astype(jnp.bfloat16)
         y = scale * lax.dot_general(
             outer_ref[...], untwisted, (((0,), (0,)), ((), ())), preferred_element_type=jnp.float32
         )
-        out_ref[:, start : start + GROUP, :] = y.reshape(blocks, GROUP, rows).astype(jnp.bfloat16)
+        y = y.astype(jnp.bfloat16).reshape(2, blocks, GROUP, fine)
+        out_ref[:, group, :fine] = y[0]
+        out_ref[:, group, fine:] = y[1]
 
 
 def convolve(x):
@@ -164,6 +171,39 @@
     add_product(left, weights_ref, first, total_ref, out_ref)
 
 
+def last_kernel(first, weights_ref, *refs):
+    blocks, total_ref, out_ref, held_ref, sems = refs[:-4], refs[-4], refs[-3], refs[-2], refs[-1]
+    left = jnp.concatenate([block[...] for block in blocks], axis=1)
+    count, width = len(blocks), weights_ref.shape[1]
+    lanes = held_ref.shape[2]
+    copies = []
+    for step in range(held_ref.shape[0]):
+        span = slice(step * lanes, (step + 1) * lanes)
+        mine = dot(left, weights_ref[first : first + count, :, span].reshape(count * width, lanes))
+        held_ref[step] = (mine + total_ref[:, span]).astype(out_ref.dtype)
+        copies.append(pltpu.make_async_copy(held_ref.at[step], out_ref.at[:, span], sems.at[step]))
+        copies[-1].start()
+    for copy in copies:
+        copy.wait()
+
+
+def last_call(weights, first, blocks, total, dtype):
+    rows, columns = total.shape
+    steps = 4
+    return pl.pallas_call(
+        functools.partial(last_kernel, first),
+        in_specs=[VMEM] * (2 + len(blocks)),
+        out_specs=pl.BlockSpec(memory_space=pl.ANY),
+        out_shape=jax.ShapeDtypeStruct((rows, columns), dtype),
+        scratch_shapes=[
+            pltpu.VMEM((steps, rows, columns // steps), dtype),
+            pltpu.SemaphoreType.DMA((steps,)),
+        ],
+        compiler_params=pltpu.CompilerParams(vmem_limit_bytes=12 * 2**20),
+        name="project_last",
+    )(weights, *blocks, total)
+
+
 VMEM = pl.BlockSpec(memory_space=pltpu.VMEM)
 
 
@@ -225,7 +265,7 @@
     *near_blocks, far_low, far_high, total = lax.optimization_barrier((*near_blocks, far_low, far_high, total))
     beside_low, beside_high = swapped(far_low), swapped(far_high)
     total = later_call(weights, 0, [*near_blocks, far_low, far_high], total, jnp.float32, "project_near")
-    return later_call(weights, len(near) + 2, [beside_low, beside_high], total, jnp.bfloat16, "project_last")
+    return last_call(weights, len(near) + 2, [beside_low, beside_high], total, jnp.bfloat16)
 
 
 def per_device(signal, gate, filt, skip, w_out):

time: 77.4 us -> 76.6 us (0.990)
  Pallas kernels: 14 us -> 13.2 us
    pallas_call x2 -> x1, Pallas kernels: 4.55 us -> 2.86 us  [later_call(): pl.pallas_call(functools.partial(later_kernel, first), in_specs=[VMEM] *...]
    pallas_call x0 -> x1, Pallas kernels: none -> 1.56 us  [last_call(): pl.pallas_call(functools.partial(last_kernel, first), in_specs=[VMEM] * (...]
    unnamed x16 -> x14, local copies, waits for them, and re-layouts: 2.3 us -> 2.29 us
where the time goes in v4:
time: 76.6 us; the launch traced here: 76.3 us
  blocking collectives  37.7 us (49%)
  starting transfers between devices  15.3 us (20%)
  Pallas kernels  13.2 us (17%)
  waiting for transfers between devices  7.63 us (10%)
  local copies, waits for them, and re-layouts  2.29 us (3%)
    all_to_all x1, blocking collectives, per_device(): spread = lax.all_to_all(turn(signal, filt, ways), 'ctx', 0, 0, tiled=True)  24.7 us
    all_to_all x1, blocking collectives, per_device(): conv = lax.all_to_all(convolve(spread), 'ctx', 0, 0, tiled=True)  13.1 us
    ppermute x7, starting transfers between devices, swapped(): lax.ppermute(block, 'tp', [(i, i ^ 1) for i in range(lax.axis_size('tp'))])  8.08 us
    ppermute x6, waiting for transfers between devices, shifted(): lax.ppermute(block, 'tp', [(i, (i + step) % count) for i in range(count)])  7.61 us
    ppermute x6, starting transfers between devices, shifted(): lax.ppermute(block, 'tp', [(i, (i + step) % count) for i in range(count)])  7.24 us
    pallas_call x1, Pallas kernels, convolve(): pl.pallas_call(conv_kernel, out_shape=jax.ShapeDtypeStruct((blocks, share...  4.67 us
    pallas_call x1, Pallas kernels, project(): pl.pallas_call(functools.partial(first_kernel, own, later), in_specs=[pl....  3.53 us
    pallas_call x1, Pallas kernels, later_call(): pl.pallas_call(functools.partial(later_kernel, first), in_specs=[VMEM] *...  2.86 us
  transfers between devices with their start and end apart: 13, of which 4 were waited for; matrix products, arithmetic and copies ran while one was open for 0% of the time, Pallas kernels for 8%

profile of v4, /device:TPU:1, one launch (start us, length us, event | category | flops | bytes accessed | tf_op | source)
XLA Modules:
  0.0 76.3 jit_solution(18016365731028333286)
XLA Ops:
  0.0 1.0 %copy-done = bf16[512,512]{1,0:T(8,128)(2,1)S(1)} copy-done((bf16[512,512]{1,0:T(8,128)(2,1)S(1)}, bf16[512,512]{1,0:T(8,128)(2,1)}, u32[]{:S(2)}) %copy-start) | copy-done | bytes 524312
  1.0 1.2 %copy-done.3 = f32[512,512]{1,0:T(8,128)S(1)} copy-done((f32[512,512]{1,0:T(8,128)S(1)}, f32[512,512]{1,0:T(8,128)}, u32[]{:S(2)}) %copy-start.3) | copy-done | bytes 1048600
  2.3 0.4 turn.1
  2.6 24.7 %all_to_all.10.x_ref = bf16[16,32,1024]{2,1,0:T(8,128)(2,1)S(1)} all-to-all(bf16[16,32,1024]{2,1,0:T(8,128)(2,1)S(1)} %turn.1), channel_id=1, replica_groups=mesh['ctx'=16,'tp'=8] {'ctx'}, dimensions={0} | all-to-all | bytes 2097152 | tf_op jit(solution)/shard_map/all_to_all | solution.py:274
  27.3 0.0 copy-start.6
  27.3 4.7 %convolve.1 = bf16[16,32,512]{2,1,0:T(8,128)(2,1)S(1)} custom-call(bf16[16,32,1024]{2,1,0:T(8,128)(2,1)S(1)} %all_to_all.10.x_ref, bf16[1536,512]{1,0:T(8,128)(2,1)S(1)} %copy-done.2, f32[512,512]{1,0:T(8,128)S(1)} %copy-done.4), custom_call_target="tpu_custom_call" | custom-call | tf_op jit(solution)/shard_map/convolve/pallas_call | solution.py:92
  32.0 13.1 %all_to_all.11 = bf16[16,32,512]{2,1,0:T(8,128)(2,1)S(1)} all-to-all(bf16[16,32,512]{2,1,0:T(8,128)(2,1)S(1)} %convolve.1), channel_id=1, replica_groups=mesh['ctx'=16,'tp'=8] {'ctx'}, dimensions={0} | all-to-all | bytes 1048576 | tf_op jit(solution)/shard_map/all_to_all | solution.py:275
  45.1 0.3 mix.1
  45.4 2.6 %collective-permute-start = (bf16[2,512,256]{2,1,0:T(8,128)(2,1)S(1)}, bf16[2,512,256]{2,1,0:T(8,128)(2,1)S(1)}, u32[]{:S(2)}, u32[]{:S(2)}) collective-permute-start(bf16[2,512,256]{2,1,0:T(8,128)(2,1)S(1)} %get-tuple-element.27.mine_ref), channel_id=1, source_target_pairs={{0,1},{1,0},{2,3},{3,2},{4,5},{5,4},{6,7},{7,6},{8,9},{9,8},{10,11... | collective-permute-start | bytes 1572872 | tf_op jit(solution)/shard_map/ppermute | solution.py:131
  48.0 2.5 %collective-permute-start.1 = (bf16[512,256]{1,0:T(8,128)(2,1)S(1)}, bf16[512,256]{1,0:T(8,128)(2,1)S(1)}, u32[]{:S(2)}, u32[]{:S(2)}) collective-permute-start(bf16[512,256]{1,0:T(8,128)(2,1)S(1)} %get-tuple-element.35), channel_id=1, source_target_pairs={{0,6},{1,7},{2,0},{3,1},{4,2},{5,3},{6,4},{7,5},{8,14},{9,15},{10,... | collective-permute-start | bytes 786440 | tf_op jit(solution)/shard_map/ppermute | solution.py:127
  50.5 0.0 collective-permute-start.2
  50.5 0.0 collective-permute-done.beside_ref
  50.5 2.7 %collective-permute-start.3 = (bf16[512,256]{1,0:T(8,128)(2,1)S(1)}, bf16[512,256]{1,0:T(8,128)(2,1)S(1)}, u32[]{:S(2)}, u32[]{:S(2)}) collective-permute-start(bf16[512,256]{1,0:T(8,128)(2,1)S(1)} %get-tuple-element.34), channel_id=1, source_target_pairs={{0,6},{1,7},{2,0},{3,1},{4,2},{5,3},{6,4},{7,5},{8,14},{9,15},{10,... | collective-permute-start | bytes 786440 | tf_op jit(solution)/shard_map/ppermute | solution.py:127
  53.2 0.0 collective-permute-start.4
  53.2 3.5 %project_own.1 = (f32[512,1024]{1,0:T(8,128)S(1)}, bf16[12,256,1024]{2,1,0:T(8,128)(2,1)S(1)}) custom-call(bf16[16,256,1024]{2,1,0:T(8,128)(2,1)} %bitcast.5, bf16[2,512,256]{2,1,0:T(8,128)(2,1)S(1)} %get-tuple-element.27.mine_ref, bf16[2,512,256]{2,1,0:T(8,128)(2,1)S(1)} %collective-permute-done.beside_ref), custom_call_target="tpu_custom_call" | custom-call | flops 1073741824 | bytes 7340032 | tf_op jit(solution)/shard_map/project_own/pallas_call | solution.py:245
  56.7 0.0 collective-permute-done.1.refs_0_
  56.7 2.5 %collective-permute-done.2.refs_3_ = bf16[512,256]{1,0:T(8,128)(2,1)S(1)} collective-permute-done((bf16[512,256]{1,0:T(8,128)(2,1)S(1)}, bf16[512,256]{1,0:T(8,128)(2,1)S(1)}, u32[]{:S(2)}, u32[]{:S(2)}) %collective-permute-start.2) | collective-permute-done | bytes 262176 | tf_op jit(solution)/shard_map/ppermute | solution.py:127
  59.3 0.3 collective-permute-start.9
  59.6 1.6 %collective-permute-start.5 = (bf16[512,256]{1,0:T(8,128)(2,1)S(1)}, bf16[512,256]{1,0:T(8,128)(2,1)S(1)}, u32[]{:S(2)}, u32[]{:S(2)}) collective-permute-start(bf16[512,256]{1,0:T(8,128)(2,1)S(1)} %collective-permute-done.1.refs_0_), channel_id=1, source_target_pairs={{0,1},{1,0},{2,3},{3,2},{4,5},{5,4},{6,7},{7,6},{8,9},{9,8},{10,11... | collective-permute-start | bytes 786440 | tf_op jit(solution)/shard_map/ppermute | solution.py:131
  61.2 1.7 %collective-permute-start.10 = (bf16[512,256]{1,0:T(8,128)(2,1)S(1)}, bf16[512,256]{1,0:T(8,128)(2,1)S(1)}, u32[]{:S(2)}, u32[]{:S(2)}) collective-permute-start(bf16[512,256]{1,0:T(8,128)(2,1)S(1)} %collective-permute-done.2.refs_3_), channel_id=1, source_target_pairs={{0,2},{1,3},{2,4},{3,5},{4,6},{5,7},{6,0},{7,1},{8,10},{9,11},{10,... | collective-permute-start | bytes 786440 | tf_op jit(solution)/shard_map/ppermute | solution.py:127
  63.0 0.0 collective-permute-done.3.refs_1_
  63.0 0.3 collective-permute-start.8
  63.3 1.6 %collective-permute-done.4.refs_2_ = bf16[512,256]{1,0:T(8,128)(2,1)S(1)} collective-permute-done((bf16[512,256]{1,0:T(8,128)(2,1)S(1)}, bf16[512,256]{1,0:T(8,128)(2,1)S(1)}, u32[]{:S(2)}, u32[]{:S(2)}) %collective-permute-start.4) | collective-permute-done | bytes 262176 | tf_op jit(solution)/shard_map/ppermute | solution.py:127
  64.9 1.6 %collective-permute-start.6 = (bf16[512,256]{1,0:T(8,128)(2,1)S(1)}, bf16[512,256]{1,0:T(8,128)(2,1)S(1)}, u32[]{:S(2)}, u32[]{:S(2)}) collective-permute-start(bf16[512,256]{1,0:T(8,128)(2,1)S(1)} %collective-permute-done.3.refs_1_), channel_id=1, source_target_pairs={{0,1},{1,0},{2,3},{3,2},{4,5},{5,4},{6,7},{7,6},{8,9},{9,8},{10,11... | collective-permute-start | bytes 786440 | tf_op jit(solution)/shard_map/ppermute | solution.py:131
  66.5 0.9 %collective-permute-done.9.refs_8_ = bf16[512,256]{1,0:T(8,128)(2,1)S(1)} collective-permute-done((bf16[512,256]{1,0:T(8,128)(2,1)S(1)}, bf16[512,256]{1,0:T(8,128)(2,1)S(1)}, u32[]{:S(2)}, u32[]{:S(2)}) %collective-permute-start.9) | collective-permute-done | bytes 262176 | tf_op jit(solution)/shard_map/ppermute | solution.py:127
  67.4 0.9 %collective-permute-start.7 = (bf16[512,256]{1,0:T(8,128)(2,1)S(1)}, bf16[512,256]{1,0:T(8,128)(2,1)S(1)}, u32[]{:S(2)}, u32[]{:S(2)}) collective-permute-start(bf16[512,256]{1,0:T(8,128)(2,1)S(1)} %collective-permute-done.4.refs_2_), channel_id=1, source_target_pairs={{0,1},{1,0},{2,3},{3,2},{4,5},{5,4},{6,7},{7,6},{8,9},{9,8},{10,11... | collective-permute-start | bytes 786440 | tf_op jit(solution)/shard_map/ppermute | solution.py:131
  68.3 2.6 %collective-permute-done.10.refs_9_ = bf16[512,256]{1,0:T(8,128)(2,1)S(1)} collective-permute-done((bf16[512,256]{1,0:T(8,128)(2,1)S(1)}, bf16[512,256]{1,0:T(8,128)(2,1)S(1)}, u32[]{:S(2)}, u32[]{:S(2)}) %collective-permute-start.10) | collective-permute-done | bytes 262176 | tf_op jit(solution)/shard_map/ppermute | solution.py:127
  70.8 0.9 %collective-permute-start.11 = (bf16[512,256]{1,0:T(8,128)(2,1)S(1)}, bf16[512,256]{1,0:T(8,128)(2,1)S(1)}, u32[]{:S(2)}, u32[]{:S(2)}) collective-permute-start(bf16[512,256]{1,0:T(8,128)(2,1)S(1)} %collective-permute-done.9.refs_8_), channel_id=1, source_target_pairs={{0,1},{1,0},{2,3},{3,2},{4,5},{5,4},{6,7},{7,6},{8,9},{9,8},{10,11... | collective-permute-start | bytes 786440 | tf_op jit(solution)/shard_map/ppermute | solution.py:131
  71.8 0.1 collective-permute-start.12
  71.9 2.9 %project_near.1.refs_2_ = f32[512,1024]{1,0:T(8,128)S(1)} custom-call(bf16[12,256,1024]{2,1,0:T(8,128)(2,1)S(1)} %get-tuple-element.31.weights_ref, bf16[512,256]{1,0:T(8,128)(2,1)S(1)} %collective-permute-done.1.refs_0_, bf16[512,256]{1,0:T(8,128)(2,1)S(1)} %collective-permute-done.3.refs_1_, bf16[512,256]{1,0:T(8,128)(2,1)S(1)} %collective-permute-done.4.refs_2_, ...), custom_call_target="tpu_custom_call" | custom-call | flops 2684354560 | bytes 12058624 | tf_op jit(solution)/shard_map/project_near/pallas_call | solution.py:221
  74.7 0.0 collective-permute-done.11.refs_0_
  74.8 1.6 %project_last.1 = bf16[512,1024]{1,0:T(8,128)(2,1)} custom-call(bf16[12,256,1024]{2,1,0:T(8,128)(2,1)S(1)} %get-tuple-element.31.weights_ref, bf16[512,256]{1,0:T(8,128)(2,1)S(1)} %collective-permute-done.11.refs_0_, bf16[512,256]{1,0:T(8,128)(2,1)S(1)} %collective-permute-done.12.refs_1_, f32[512,1024]{1,0:T(8,128)S(1)} %project_near.1.refs_2_), custom_call_target="tpu_custom_call" | custom-call | tf_op jit(solution)/shard_map/project_last/pallas_call | solution.py:193
  (16 shorter events, 0.0 us)
Async XLA Ops:
  0.0 1.0 %copy-start = (bf16[512,512]{1,0:T(8,128)(2,1)S(1)}, bf16[512,512]{1,0:T(8,128)(2,1)}, u32[]{:S(2)}) copy-start(bf16[512,512]{1,0:T(8,128)(2,1)} %signal_ref.3) | copy-start | bytes 1572868
  1.0 1.2 %copy-start.3 = (f32[512,512]{1,0:T(8,128)S(1)}, f32[512,512]{1,0:T(8,128)}, u32[]{:S(2)}) copy-start(f32[512,512]{1,0:T(8,128)} %filt_ref.1) | copy-start | bytes 3145732
  2.3 25.0 %copy-start.2 = (bf16[1536,512]{1,0:T(8,128)(2,1)S(1)}, bf16[1536,512]{1,0:T(8,128)(2,1)}, u32[]{:S(2)}) copy-start(bf16[1536,512]{1,0:T(8,128)(2,1)} %constant.4.clone.table_ref) | copy-start | bytes 4718596
  2.3 25.0 %copy-start.4 = (f32[512,512]{1,0:T(8,128)S(1)}, f32[512,512]{1,0:T(8,128)}, u32[]{:S(2)}) copy-start(f32[512,512]{1,0:T(8,128)} %constant.5.clone.twist_ref) | copy-start | bytes 3145732
  27.3 17.8 %copy-start.1 = (bf16[512,512]{1,0:T(8,128)(2,1)S(1)}, bf16[512,512]{1,0:T(8,128)(2,1)}, u32[]{:S(2)}) copy-start(bf16[512,512]{1,0:T(8,128)(2,1)} %signal_ref.3) | copy-start | bytes 1572868
  27.3 17.8 %copy-start.5 = (bf16[512,512]{1,0:T(8,128)(2,1)S(1)}, bf16[512,512]{1,0:T(8,128)(2,1)}, u32[]{:S(2)}) copy-start(bf16[512,512]{1,0:T(8,128)(2,1)} %gate_ref.1) | copy-start | bytes 1572868
  27.3 17.8 %copy-start.6 = (f32[512]{0:T(512)S(1)}, f32[512]{0:T(512)}, u32[]{:S(2)}) copy-start(f32[512]{0:T(512)} %param.10) | copy-start | bytes 6148
  45.4 5.1 %collective-permute-start = (bf16[2,512,256]{2,1,0:T(8,128)(2,1)S(1)}, bf16[2,512,256]{2,1,0:T(8,128)(2,1)S(1)}, u32[]{:S(2)}, u32[]{:S(2)}) collective-permute-start(bf16[2,512,256]{2,1,0:T(8,128)(2,1)S(1)} %get-tuple-element.27.mine_ref), channel_id=1, source_target_pairs={{0,1},{1,0},{2,3},{3,2},{4,5},{5,4},{6,7},{7,6},{8,9},{9,8},{10,11... | collective-permute-start | bytes 1572872 | tf_op jit(solution)/shard_map/ppermute | solution.py:131
  48.0 8.7 %collective-permute-start.1 = (bf16[512,256]{1,0:T(8,128)(2,1)S(1)}, bf16[512,256]{1,0:T(8,128)(2,1)S(1)}, u32[]{:S(2)}, u32[]{:S(2)}) collective-permute-start(bf16[512,256]{1,0:T(8,128)(2,1)S(1)} %get-tuple-element.35), channel_id=1, source_target_pairs={{0,6},{1,7},{2,0},{3,1},{4,2},{5,3},{6,4},{7,5},{8,14},{9,15},{10,... | collective-permute-start | bytes 786440 | tf_op jit(solution)/shard_map/ppermute | solution.py:127
  50.5 8.8 %collective-permute-start.2 = (bf16[512,256]{1,0:T(8,128)(2,1)S(1)}, bf16[512,256]{1,0:T(8,128)(2,1)S(1)}, u32[]{:S(2)}, u32[]{:S(2)}) collective-permute-start(bf16[512,256]{1,0:T(8,128)(2,1)S(1)} %get-tuple-element.34), channel_id=1, source_target_pairs={{0,2},{1,3},{2,4},{3,5},{4,6},{5,7},{6,0},{7,1},{8,10},{9,11},{10,... | collective-permute-start | bytes 786440 | tf_op jit(solution)/shard_map/ppermute | solution.py:127
  50.5 12.5 %collective-permute-start.3 = (bf16[512,256]{1,0:T(8,128)(2,1)S(1)}, bf16[512,256]{1,0:T(8,128)(2,1)S(1)}, u32[]{:S(2)}, u32[]{:S(2)}) collective-permute-start(bf16[512,256]{1,0:T(8,128)(2,1)S(1)} %get-tuple-element.34), channel_id=1, source_target_pairs={{0,6},{1,7},{2,0},{3,1},{4,2},{5,3},{6,4},{7,5},{8,14},{9,15},{10,... | collective-permute-start | bytes 786440 | tf_op jit(solution)/shard_map/ppermute | solution.py:127
  53.2 11.7 %collective-permute-start.4 = (bf16[512,256]{1,0:T(8,128)(2,1)S(1)}, bf16[512,256]{1,0:T(8,128)(2,1)S(1)}, u32[]{:S(2)}, u32[]{:S(2)}) collective-permute-start(bf16[512,256]{1,0:T(8,128)(2,1)S(1)} %get-tuple-element.35), channel_id=1, source_target_pairs={{0,2},{1,3},{2,4},{3,5},{4,6},{5,7},{6,0},{7,1},{8,10},{9,11},{10,... | collective-permute-start | bytes 786440 | tf_op jit(solution)/shard_map/ppermute | solution.py:127
  59.3 8.1 %collective-permute-start.9 = (bf16[512,256]{1,0:T(8,128)(2,1)S(1)}, bf16[512,256]{1,0:T(8,128)(2,1)S(1)}, u32[]{:S(2)}, u32[]{:S(2)}) collective-permute-start(bf16[512,256]{1,0:T(8,128)(2,1)S(1)} %collective-permute-done.1.refs_0_), channel_id=1, source_target_pairs={{0,6},{1,7},{2,0},{3,1},{4,2},{5,3},{6,4},{7,5},{8,14},{9,15},{10,... | collective-permute-start | bytes 786440 | tf_op jit(solution)/shard_map/ppermute | solution.py:127
  59.6 8.7 %collective-permute-start.5 = (bf16[512,256]{1,0:T(8,128)(2,1)S(1)}, bf16[512,256]{1,0:T(8,128)(2,1)S(1)}, u32[]{:S(2)}, u32[]{:S(2)}) collective-permute-start(bf16[512,256]{1,0:T(8,128)(2,1)S(1)} %collective-permute-done.1.refs_0_), channel_id=1, source_target_pairs={{0,1},{1,0},{2,3},{3,2},{4,5},{5,4},{6,7},{7,6},{8,9},{9,8},{10,11... | collective-permute-start | bytes 786440 | tf_op jit(solution)/shard_map/ppermute | solution.py:131
  61.2 9.6 %collective-permute-start.10 = (bf16[512,256]{1,0:T(8,128)(2,1)S(1)}, bf16[512,256]{1,0:T(8,128)(2,1)S(1)}, u32[]{:S(2)}, u32[]{:S(2)}) collective-permute-start(bf16[512,256]{1,0:T(8,128)(2,1)S(1)} %collective-permute-done.2.refs_3_), channel_id=1, source_target_pairs={{0,2},{1,3},{2,4},{3,5},{4,6},{5,7},{6,0},{7,1},{8,10},{9,11},{10,... | collective-permute-start | bytes 786440 | tf_op jit(solution)/shard_map/ppermute | solution.py:127
  63.0 7.9 %collective-permute-start.8 = (bf16[512,256]{1,0:T(8,128)(2,1)S(1)}, bf16[512,256]{1,0:T(8,128)(2,1)S(1)}, u32[]{:S(2)}, u32[]{:S(2)}) collective-permute-start(bf16[512,256]{1,0:T(8,128)(2,1)S(1)} %collective-permute-done.2.refs_3_), channel_id=1, source_target_pairs={{0,1},{1,0},{2,3},{3,2},{4,5},{5,4},{6,7},{7,6},{8,9},{9,8},{10,11... | collective-permute-start | bytes 786440 | tf_op jit(solution)/shard_map/ppermute | solution.py:131
  64.9 6.0 %collective-permute-start.6 = (bf16[512,256]{1,0:T(8,128)(2,1)S(1)}, bf16[512,256]{1,0:T(8,128)(2,1)S(1)}, u32[]{:S(2)}, u32[]{:S(2)}) collective-permute-start(bf16[512,256]{1,0:T(8,128)(2,1)S(1)} %collective-permute-done.3.refs_1_), channel_id=1, source_target_pairs={{0,1},{1,0},{2,3},{3,2},{4,5},{5,4},{6,7},{7,6},{8,9},{9,8},{10,11... | collective-permute-start | bytes 786440 | tf_op jit(solution)/shard_map/ppermute | solution.py:131
  67.4 3.4 %collective-permute-start.7 = (bf16[512,256]{1,0:T(8,128)(2,1)S(1)}, bf16[512,256]{1,0:T(8,128)(2,1)S(1)}, u32[]{:S(2)}, u32[]{:S(2)}) collective-permute-start(bf16[512,256]{1,0:T(8,128)(2,1)S(1)} %collective-permute-done.4.refs_2_), channel_id=1, source_target_pairs={{0,1},{1,0},{2,3},{3,2},{4,5},{5,4},{6,7},{7,6},{8,9},{9,8},{10,11... | collective-permute-start | bytes 786440 | tf_op jit(solution)/shard_map/ppermute | solution.py:131
  70.8 3.9 %collective-permute-start.11 = (bf16[512,256]{1,0:T(8,128)(2,1)S(1)}, bf16[512,256]{1,0:T(8,128)(2,1)S(1)}, u32[]{:S(2)}, u32[]{:S(2)}) collective-permute-start(bf16[512,256]{1,0:T(8,128)(2,1)S(1)} %collective-permute-done.9.refs_8_), channel_id=1, source_target_pairs={{0,1},{1,0},{2,3},{3,2},{4,5},{5,4},{6,7},{7,6},{8,9},{9,8},{10,11... | collective-permute-start | bytes 786440 | tf_op jit(solution)/shard_map/ppermute | solution.py:131
  71.8 3.0 %collective-permute-start.12 = (bf16[512,256]{1,0:T(8,128)(2,1)S(1)}, bf16[512,256]{1,0:T(8,128)(2,1)S(1)}, u32[]{:S(2)}, u32[]{:S(2)}) collective-permute-start(bf16[512,256]{1,0:T(8,128)(2,1)S(1)} %collective-permute-done.10.refs_9_), channel_id=1, source_target_pairs={{0,1},{1,0},{2,3},{3,2},{4,5},{5,4},{6,7},{7,6},{8,9},{9,8},{10,11... | collective-permute-start | bytes 786440 | tf_op jit(solution)/shard_map/ppermute | solution.py:131

commit v5 on v4

--- a/solution.py
+++ b/solution.py
@@ -97,34 +97,29 @@
     )(x, *constants)
 
 
-def mix_kernel(conv_ref, signal_ref, gate_ref, skip_ref, out_ref, low_ref, high_ref):
+def mix_kernel(conv_ref, signal_ref, gate_ref, skip_ref, out_ref):
     conv = conv_ref[...].astype(jnp.float32).T
     values = signal_ref[...].astype(jnp.float32)
-    mixed = (gate_ref[...].astype(jnp.float32) * (conv + skip_ref[...] * values)).astype(jnp.bfloat16)
-    width = out_ref.shape[2]
-    for half, half_ref in enumerate((low_ref, high_ref)):
-        part = mixed[:, half * width : (half + 1) * width]
-        out_ref[half] = part
-        half_ref[...] = part
+    out_ref[...] = (gate_ref[...].astype(jnp.float32) * (conv + skip_ref[...] * values)).astype(jnp.bfloat16)
 
 
 def mix(conv, signal, gate, skip):
     rows, channels = signal.shape
     return pl.pallas_call(
         mix_kernel,
-        out_shape=[
-            jax.ShapeDtypeStruct((2, rows, channels // 2), jnp.bfloat16),
-            jax.ShapeDtypeStruct((rows, channels // 2), jnp.bfloat16),
-            jax.ShapeDtypeStruct((rows, channels // 2), jnp.bfloat16),
-        ],
+        out_shape=jax.ShapeDtypeStruct((rows, channels), jnp.bfloat16),
         compiler_params=pltpu.CompilerParams(vmem_limit_bytes=8 * 2**20),
         name="mix",
     )(conv, signal, gate, skip.reshape(1, channels))
 
 
+def toward(device, step):
+    count = lax.axis_size("tp")
+    return (device + 2 * step * (1 - 2 * (device % 2)) + count) % count
+
+
 def shifted(block, step):
-    count = lax.axis_size("tp")
-    return lax.ppermute(block, "tp", [(i, (i + step) % count) for i in range(count)])
+    return lax.ppermute(block, "tp", [(i, toward(i, step)) for i in range(lax.axis_size("tp"))])
 
 
 def swapped(block):
@@ -132,9 +127,8 @@
 
 
 def rows_of(blocks):
-    count = lax.axis_size("tp")
     me = lax.axis_index("tp")
-    return [2 * lax.rem((me ^ 1 if other else me) + offset + count, count) + half for other, offset, half in blocks]
+    return [toward(me ^ 1 if other else me, step) for other, step in blocks]
 
 
 def first_kernel(own, later, weights_ref, mine_ref, beside_ref, total_ref, later_ref, held_ref, sems):
@@ -145,7 +139,7 @@
         copies.append(pltpu.make_async_copy(weights_ref.at[row], later_ref.at[j], sems.at[len(own) + j]))
     for copy in copies:
         copy.start()
-    left = jnp.concatenate([mine_ref[0], mine_ref[1], beside_ref[0], beside_ref[1]], axis=1)
+    left = jnp.concatenate([mine_ref[...], beside_ref[...]], axis=1)
     for copy in copies[: len(own)]:
         copy.wait()
     add_product(left, held_ref, 0, None, total_ref)
@@ -229,19 +223,15 @@
     )(weights, *blocks, total)
 
 
-def project(mixed, low, high, w_out):
-    width, columns = mixed.shape[2], w_out.shape[1]
-    rows = mixed.shape[1]
+def project(mixed, w_out):
+    rows, width = mixed.shape
+    columns = w_out.shape[1]
     weights = w_out.reshape(-1, width, columns)
-    own = [(other, 0, half) for other in (0, 1) for half in (0, 1)]
-    near = [(other, offset, half) for other in (0, 1) for offset in (2, -2) for half in (0, 1)]
-    far = [(other, 4, half) for other in (0, 1) for half in (0, 1)]
-    later = near + far
-
-    right_low, left_high = shifted(low, -2), shifted(high, 2)
+    own = [(0, 0), (1, 0)]
+    later = [(0, 1), (1, 1), (0, -1), (1, -1), (0, 2), (1, 2)]
+
+    ahead = shifted(mixed, -1)
     beside = swapped(mixed)
-    low, high, beside = lax.optimization_barrier((low, high, beside))
-    right_high, left_low = shifted(high, -2), shifted(low, 2)
     total, weights = pl.pallas_call(
         functools.partial(first_kernel, own, later),
         in_specs=[pl.BlockSpec(memory_space=pl.ANY), VMEM, VMEM],
@@ -258,14 +248,16 @@
         cost_estimate=cost(rows, len(own) * width, columns),
         name="project_own",
     )(weights, mixed, beside)
-    right_low, left_high, total = lax.optimization_barrier((right_low, left_high, total))
-    far_low, far_high = shifted(right_low, -2), shifted(left_high, 2)
-    near_blocks = [right_low, right_high, left_low, left_high]
-    near_blocks += [swapped(block) for block in near_blocks]
-    *near_blocks, far_low, far_high, total = lax.optimization_barrier((*near_blocks, far_low, far_high, total))
-    beside_low, beside_high = swapped(far_low), swapped(far_high)
-    total = later_call(weights, 0, [*near_blocks, far_low, far_high], total, jnp.float32, "project_near")
-    return last_call(weights, len(near) + 2, [beside_low, beside_high], total, jnp.bfloat16)
+    mixed, total = lax.optimization_barrier((mixed, total))
+    behind = shifted(mixed, 1)
+    ahead, total = lax.optimization_barrier((ahead, total))
+    far = shifted(ahead, -1)
+    total = later_call(weights, 0, [ahead, swapped(ahead)], total, jnp.float32, "project_middle")
+    near_blocks = [behind, swapped(behind)]
+    *near_blocks, far, total = lax.optimization_barrier((*near_blocks, far, total))
+    beside_far = swapped(far)
+    total = later_call(weights, 2, [*near_blocks, far], total, jnp.float32, "project_near")
+    return last_call(weights, len(later) - 1, [beside_far], total, jnp.bfloat16)
 
 
 def per_device(signal, gate, filt, skip, w_out):
@@ -273,7 +265,7 @@
     rows, channels = signal.shape
     spread = lax.all_to_all(turn(signal, filt, ways), "ctx", 0, 0, tiled=True)
     conv = lax.all_to_all(convolve(spread), "ctx", 0, 0, tiled=True)
-    return project(*mix(conv.reshape(channels, rows), signal, gate, skip), w_out)
+    return project(mix(conv.reshape(channels, rows), signal, gate, skip), w_out)
 
 
 def solution(mesh):

time: 76.6 us -> 73.5 us (0.960)
  starting transfers between devices: 15.3 us -> 11.4 us
    ppermute x6 -> x3, starting transfers between devices: 7.24 us -> 4.71 us  [shifted(): lax.ppermute(block, 'tp', [(i, toward(i, step)) for i in range(lax.axis_s...]
    ppermute x7 -> x4, starting transfers between devices: 8.08 us -> 6.69 us  [swapped(): lax.ppermute(block, 'tp', [(i, i ^ 1) for i in range(lax.axis_size('tp'))])]
    ppermute x6 -> x3, waiting for transfers between devices: 7.61 us -> 7.9 us  [shifted(): lax.ppermute(block, 'tp', [(i, toward(i, step)) for i in range(lax.axis_s...]
    pallas_call x1 -> x2, Pallas kernels: 2.86 us -> 3.04 us  [later_call(): pl.pallas_call(functools.partial(later_kernel, first), in_specs=[VMEM] *...]
  transfers between devices with their start and end apart: 13 -> 7, of which waited for: 4 -> 5; matrix products, arithmetic and copies ran while one was open for 0% -> 0% of each run, Pallas kernels for 8% -> 9%
where the time goes in v5:
time: 73.5 us; the launch traced here: 73.2 us
  blocking collectives  37.7 us (51%)
  Pallas kernels  13.4 us (18%)
  starting transfers between devices  11.4 us (16%)
  waiting for transfers between devices  8.34 us (11%)
  local copies, waits for them, and re-layouts  2.29 us (3%)
    all_to_all x1, blocking collectives, per_device(): spread = lax.all_to_all(turn(signal, filt, ways), 'ctx', 0, 0, tiled=True)  24.7 us
    all_to_all x1, blocking collectives, per_device(): conv = lax.all_to_all(convolve(spread), 'ctx', 0, 0, tiled=True)  13.1 us
    ppermute x3, waiting for transfers between devices, shifted(): lax.ppermute(block, 'tp', [(i, toward(i, step)) for i in range(lax.axis_s...  7.9 us
    ppermute x4, starting transfers between devices, swapped(): lax.ppermute(block, 'tp', [(i, i ^ 1) for i in range(lax.axis_size('tp'))])  6.69 us
    ppermute x3, starting transfers between devices, shifted(): lax.ppermute(block, 'tp', [(i, toward(i, step)) for i in range(lax.axis_s...  4.71 us
    pallas_call x1, Pallas kernels, convolve(): pl.pallas_call(conv_kernel, out_shape=jax.ShapeDtypeStruct((blocks, share...  4.67 us
    pallas_call x1, Pallas kernels, project(): pl.pallas_call(functools.partial(first_kernel, own, later), in_specs=[pl....  3.49 us
    pallas_call x2, Pallas kernels, later_call(): pl.pallas_call(functools.partial(later_kernel, first), in_specs=[VMEM] *...  3.04 us
  transfers between devices with their start and end apart: 7, of which 5 were waited for; matrix products, arithmetic and copies ran while one was open for 0% of the time, Pallas kernels for 9%

profile of v5, /device:TPU:1, one launch (start us, length us, event | category | flops | bytes accessed | tf_op | source)
XLA Modules:
  0.0 73.2 jit_solution(12861265097597217282)
XLA Ops:
  0.0 0.0 copy-start
  0.0 1.0 %copy-done = bf16[512,512]{1,0:T(8,128)(2,1)S(1)} copy-done((bf16[512,512]{1,0:T(8,128)(2,1)S(1)}, bf16[512,512]{1,0:T(8,128)(2,1)}, u32[]{:S(2)}) %copy-start) | copy-done | bytes 524312
  1.0 1.2 %copy-done.3 = f32[512,512]{1,0:T(8,128)S(1)} copy-done((f32[512,512]{1,0:T(8,128)S(1)}, f32[512,512]{1,0:T(8,128)}, u32[]{:S(2)}) %copy-start.3) | copy-done | bytes 1048600
  2.3 0.4 turn.1
  2.6 24.7 %all_to_all.10.x_ref = bf16[16,32,1024]{2,1,0:T(8,128)(2,1)S(1)} all-to-all(bf16[16,32,1024]{2,1,0:T(8,128)(2,1)S(1)} %turn.1), channel_id=1, replica_groups=mesh['ctx'=16,'tp'=8] {'ctx'}, dimensions={0} | all-to-all | bytes 2097152 | tf_op jit(solution)/shard_map/all_to_all | solution.py:266
  27.3 0.0 copy-done.2
  27.3 0.0 copy-done.4
  27.3 0.0 copy-start.6
  27.3 4.7 %convolve.1 = bf16[16,32,512]{2,1,0:T(8,128)(2,1)S(1)} custom-call(bf16[16,32,1024]{2,1,0:T(8,128)(2,1)S(1)} %all_to_all.10.x_ref, bf16[1536,512]{1,0:T(8,128)(2,1)S(1)} %copy-done.2, f32[512,512]{1,0:T(8,128)S(1)} %copy-done.4), custom_call_target="tpu_custom_call" | custom-call | tf_op jit(solution)/shard_map/convolve/pallas_call | solution.py:92
  32.0 13.1 %all_to_all.11 = bf16[16,32,512]{2,1,0:T(8,128)(2,1)S(1)} all-to-all(bf16[16,32,512]{2,1,0:T(8,128)(2,1)S(1)} %convolve.1), channel_id=1, replica_groups=mesh['ctx'=16,'tp'=8] {'ctx'}, dimensions={0} | all-to-all | bytes 1048576 | tf_op jit(solution)/shard_map/all_to_all | solution.py:267
  45.1 0.0 copy-done.1
  45.1 0.0 copy-done.5
  45.1 0.0 copy-done.6
  45.1 0.3 mix.1.mine_ref
  45.4 2.6 %collective-permute-start = (bf16[512,512]{1,0:T(8,128)(2,1)S(1)}, bf16[512,512]{1,0:T(8,128)(2,1)S(1)}, u32[]{:S(2)}, u32[]{:S(2)}) collective-permute-start(bf16[512,512]{1,0:T(8,128)(2,1)S(1)} %mix.1.mine_ref), channel_id=1, source_target_pairs={{0,1},{1,0},{2,3},{3,2},{4,5},{5,4},{6,7},{7,6},{8,9},{9,8},{10,11... | collective-permute-start | bytes 1572872 | tf_op jit(solution)/shard_map/ppermute | solution.py:126
  48.0 1.2 %collective-permute-start.3 = (bf16[512,512]{1,0:T(8,128)(2,1)S(1)}, bf16[512,512]{1,0:T(8,128)(2,1)S(1)}, u32[]{:S(2)}, u32[]{:S(2)}) collective-permute-start(bf16[512,512]{1,0:T(8,128)(2,1)S(1)} %mix.1.mine_ref), channel_id=1, source_target_pairs={{0,6},{1,3},{2,0},{3,5},{4,2},{5,7},{6,4},{7,1},{8,14},{9,11},{10,... | collective-permute-start | bytes 1572872 | tf_op jit(solution)/shard_map/ppermute | solution.py:122
  49.2 0.3 collective-permute-done.beside_ref
  49.6 3.5 %project_own.1 = (f32[512,1024]{1,0:T(8,128)S(1)}, bf16[6,512,1024]{2,1,0:T(8,128)(2,1)S(1)}) custom-call(bf16[8,512,1024]{2,1,0:T(8,128)(2,1)} %bitcast.5, bf16[512,512]{1,0:T(8,128)(2,1)S(1)} %mix.1.mine_ref, bf16[512,512]{1,0:T(8,128)(2,1)S(1)} %collective-permute-done.beside_ref), custom_call_target="tpu_custom_call" | custom-call | flops 1073741824 | bytes 7340032 | tf_op jit(solution)/shard_map/project_own/pallas_call | solution.py:235
  53.1 2.5 %collective-permute-start.1 = (bf16[512,512]{1,0:T(8,128)(2,1)S(1)}, bf16[512,512]{1,0:T(8,128)(2,1)S(1)}, u32[]{:S(2)}, u32[]{:S(2)}) collective-permute-start(bf16[512,512]{1,0:T(8,128)(2,1)S(1)} %mix.1.mine_ref), channel_id=1, source_target_pairs={{0,2},{1,7},{2,4},{3,1},{4,6},{5,3},{6,0},{7,5},{8,10},{9,15},{10,... | collective-permute-start | bytes 1572872 | tf_op jit(solution)/shard_map/ppermute | solution.py:122
  55.6 1.7 %collective-permute-done.3.refs_0_ = bf16[512,512]{1,0:T(8,128)(2,1)S(1)} collective-permute-done((bf16[512,512]{1,0:T(8,128)(2,1)S(1)}, bf16[512,512]{1,0:T(8,128)(2,1)S(1)}, u32[]{:S(2)}, u32[]{:S(2)}) %collective-permute-start.3) | collective-permute-done | bytes 524320 | tf_op jit(solution)/shard_map/ppermute | solution.py:122
  57.3 1.3 %collective-permute-start.5 = (bf16[512,512]{1,0:T(8,128)(2,1)S(1)}, bf16[512,512]{1,0:T(8,128)(2,1)S(1)}, u32[]{:S(2)}, u32[]{:S(2)}) collective-permute-start(bf16[512,512]{1,0:T(8,128)(2,1)S(1)} %collective-permute-done.3.refs_0_), channel_id=1, source_target_pairs={{0,1},{1,0},{2,3},{3,2},{4,5},{5,4},{6,7},{7,6},{8,9},{9,8},{10,11... | collective-permute-start | bytes 1572872 | tf_op jit(solution)/shard_map/ppermute | solution.py:126
  58.5 0.9 %collective-permute-start.4 = (bf16[512,512]{1,0:T(8,128)(2,1)S(1)}, bf16[512,512]{1,0:T(8,128)(2,1)S(1)}, u32[]{:S(2)}, u32[]{:S(2)}) collective-permute-start(bf16[512,512]{1,0:T(8,128)(2,1)S(1)} %collective-permute-done.3.refs_0_), channel_id=1, source_target_pairs={{0,6},{1,3},{2,0},{3,5},{4,2},{5,7},{6,4},{7,1},{8,14},{9,11},{10,... | collective-permute-start | bytes 1572872 | tf_op jit(solution)/shard_map/ppermute | solution.py:122
  59.5 3.7 %collective-permute-done.1.refs_0_ = bf16[512,512]{1,0:T(8,128)(2,1)S(1)} collective-permute-done((bf16[512,512]{1,0:T(8,128)(2,1)S(1)}, bf16[512,512]{1,0:T(8,128)(2,1)S(1)}, u32[]{:S(2)}, u32[]{:S(2)}) %collective-permute-start.1) | collective-permute-done | bytes 524320 | tf_op jit(solution)/shard_map/ppermute | solution.py:122
  63.2 2.8 %collective-permute-start.2 = (bf16[512,512]{1,0:T(8,128)(2,1)S(1)}, bf16[512,512]{1,0:T(8,128)(2,1)S(1)}, u32[]{:S(2)}, u32[]{:S(2)}) collective-permute-start(bf16[512,512]{1,0:T(8,128)(2,1)S(1)} %collective-permute-done.1.refs_0_), channel_id=1, source_target_pairs={{0,1},{1,0},{2,3},{3,2},{4,5},{5,4},{6,7},{7,6},{8,9},{9,8},{10,11... | collective-permute-start | bytes 1572872 | tf_op jit(solution)/shard_map/ppermute | solution.py:126
  66.0 0.0 collective-permute-done.5.refs_1_
  66.0 1.2 %project_middle.1.refs_3_ = f32[512,1024]{1,0:T(8,128)S(1)} custom-call(bf16[6,512,1024]{2,1,0:T(8,128)(2,1)S(1)} %get-tuple-element.15.weights_ref, bf16[512,512]{1,0:T(8,128)(2,1)S(1)} %collective-permute-done.3.refs_0_, bf16[512,512]{1,0:T(8,128)(2,1)S(1)} %collective-permute-done.5.refs_1_, f32[512,1024]{1,0:T(8,128)S(1)} %get-tuple-element.20.refs_2_), custom_call_target="tpu_custom_call" | custom-call | flops 1073741824 | bytes 7340032 | tf_op jit(solution)/shard_map/project_middle/pallas_call | solution.py:215
  67.2 2.5 %collective-permute-done.4.refs_2_ = bf16[512,512]{1,0:T(8,128)(2,1)S(1)} collective-permute-done((bf16[512,512]{1,0:T(8,128)(2,1)S(1)}, bf16[512,512]{1,0:T(8,128)(2,1)S(1)}, u32[]{:S(2)}, u32[]{:S(2)}) %collective-permute-start.4) | collective-permute-done | bytes 524320 | tf_op jit(solution)/shard_map/ppermute | solution.py:122
  69.7 0.0 collective-permute-done.2.refs_1_
  69.8 0.0 collective-permute-start.6
  69.8 1.8 %project_near.1.refs_1_ = f32[512,1024]{1,0:T(8,128)S(1)} custom-call(bf16[6,512,1024]{2,1,0:T(8,128)(2,1)S(1)} %get-tuple-element.15.weights_ref, bf16[512,512]{1,0:T(8,128)(2,1)S(1)} %collective-permute-done.1.refs_0_, bf16[512,512]{1,0:T(8,128)(2,1)S(1)} %collective-permute-done.2.refs_1_, bf16[512,512]{1,0:T(8,128)(2,1)S(1)} %collective-permute-done.4.refs_2_, ...), custom_call_target="tpu_custom_call" | custom-call | flops 1610612736 | bytes 8912896 | tf_op jit(solution)/shard_map/project_near/pallas_call | solution.py:215
  71.5 0.1 collective-permute-done.6.refs_0_
  71.7 1.6 %project_last.1 = bf16[512,1024]{1,0:T(8,128)(2,1)} custom-call(bf16[6,512,1024]{2,1,0:T(8,128)(2,1)S(1)} %get-tuple-element.15.weights_ref, bf16[512,512]{1,0:T(8,128)(2,1)S(1)} %collective-permute-done.6.refs_0_, f32[512,1024]{1,0:T(8,128)S(1)} %project_near.1.refs_1_), custom_call_target="tpu_custom_call" | custom-call | tf_op jit(solution)/shard_map/project_last/pallas_call | solution.py:187
  (5 shorter events, 0.0 us)
Async XLA Ops:
  0.0 1.0 %copy-start = (bf16[512,512]{1,0:T(8,128)(2,1)S(1)}, bf16[512,512]{1,0:T(8,128)(2,1)}, u32[]{:S(2)}) copy-start(bf16[512,512]{1,0:T(8,128)(2,1)} %signal_ref.3) | copy-start | bytes 1572868
  1.0 1.2 %copy-start.3 = (f32[512,512]{1,0:T(8,128)S(1)}, f32[512,512]{1,0:T(8,128)}, u32[]{:S(2)}) copy-start(f32[512,512]{1,0:T(8,128)} %filt_ref.1) | copy-start | bytes 3145732
  2.3 25.0 %copy-start.2 = (bf16[1536,512]{1,0:T(8,128)(2,1)S(1)}, bf16[1536,512]{1,0:T(8,128)(2,1)}, u32[]{:S(2)}) copy-start(bf16[1536,512]{1,0:T(8,128)(2,1)} %constant.4.clone.table_ref) | copy-start | bytes 4718596
  2.3 25.0 %copy-start.4 = (f32[512,512]{1,0:T(8,128)S(1)}, f32[512,512]{1,0:T(8,128)}, u32[]{:S(2)}) copy-start(f32[512,512]{1,0:T(8,128)} %constant.5.clone.twist_ref) | copy-start | bytes 3145732
  27.3 17.8 %copy-start.1 = (bf16[512,512]{1,0:T(8,128)(2,1)S(1)}, bf16[512,512]{1,0:T(8,128)(2,1)}, u32[]{:S(2)}) copy-start(bf16[512,512]{1,0:T(8,128)(2,1)} %signal_ref.3) | copy-start | bytes 1572868
  27.3 17.8 %copy-start.5 = (bf16[512,512]{1,0:T(8,128)(2,1)S(1)}, bf16[512,512]{1,0:T(8,128)(2,1)}, u32[]{:S(2)}) copy-start(bf16[512,512]{1,0:T(8,128)(2,1)} %gate_ref.1) | copy-start | bytes 1572868
  27.3 17.8 %copy-start.6 = (f32[512]{0:T(512)S(1)}, f32[512]{0:T(512)}, u32[]{:S(2)}) copy-start(f32[512]{0:T(512)} %param.10) | copy-start | bytes 6148
  45.4 4.2 %collective-permute-start = (bf16[512,512]{1,0:T(8,128)(2,1)S(1)}, bf16[512,512]{1,0:T(8,128)(2,1)S(1)}, u32[]{:S(2)}, u32[]{:S(2)}) collective-permute-start(bf16[512,512]{1,0:T(8,128)(2,1)S(1)} %mix.1.mine_ref), channel_id=1, source_target_pairs={{0,1},{1,0},{2,3},{3,2},{4,5},{5,4},{6,7},{7,6},{8,9},{9,8},{10,11... | collective-permute-start | bytes 1572872 | tf_op jit(solution)/shard_map/ppermute | solution.py:126
  48.0 9.2 %collective-permute-start.3 = (bf16[512,512]{1,0:T(8,128)(2,1)S(1)}, bf16[512,512]{1,0:T(8,128)(2,1)S(1)}, u32[]{:S(2)}, u32[]{:S(2)}) collective-permute-start(bf16[512,512]{1,0:T(8,128)(2,1)S(1)} %mix.1.mine_ref), channel_id=1, source_target_pairs={{0,6},{1,3},{2,0},{3,5},{4,2},{5,7},{6,4},{7,1},{8,14},{9,11},{10,... | collective-permute-start | bytes 1572872 | tf_op jit(solution)/shard_map/ppermute | solution.py:122
  53.1 10.2 %collective-permute-start.1 = (bf16[512,512]{1,0:T(8,128)(2,1)S(1)}, bf16[512,512]{1,0:T(8,128)(2,1)S(1)}, u32[]{:S(2)}, u32[]{:S(2)}) collective-permute-start(bf16[512,512]{1,0:T(8,128)(2,1)S(1)} %mix.1.mine_ref), channel_id=1, source_target_pairs={{0,2},{1,7},{2,4},{3,1},{4,6},{5,3},{6,0},{7,5},{8,10},{9,15},{10,... | collective-permute-start | bytes 1572872 | tf_op jit(solution)/shard_map/ppermute | solution.py:122
  57.3 8.7 %collective-permute-start.5 = (bf16[512,512]{1,0:T(8,128)(2,1)S(1)}, bf16[512,512]{1,0:T(8,128)(2,1)S(1)}, u32[]{:S(2)}, u32[]{:S(2)}) collective-permute-start(bf16[512,512]{1,0:T(8,128)(2,1)S(1)} %collective-permute-done.3.refs_0_), channel_id=1, source_target_pairs={{0,1},{1,0},{2,3},{3,2},{4,5},{5,4},{6,7},{7,6},{8,9},{9,8},{10,11... | collective-permute-start | bytes 1572872 | tf_op jit(solution)/shard_map/ppermute | solution.py:126
  58.5 11.2 %collective-permute-start.4 = (bf16[512,512]{1,0:T(8,128)(2,1)S(1)}, bf16[512,512]{1,0:T(8,128)(2,1)S(1)}, u32[]{:S(2)}, u32[]{:S(2)}) collective-permute-start(bf16[512,512]{1,0:T(8,128)(2,1)S(1)} %collective-permute-done.3.refs_0_), channel_id=1, source_target_pairs={{0,6},{1,3},{2,0},{3,5},{4,2},{5,7},{6,4},{7,1},{8,14},{9,11},{10,... | collective-permute-start | bytes 1572872 | tf_op jit(solution)/shard_map/ppermute | solution.py:122
  63.2 6.5 %collective-permute-start.2 = (bf16[512,512]{1,0:T(8,128)(2,1)S(1)}, bf16[512,512]{1,0:T(8,128)(2,1)S(1)}, u32[]{:S(2)}, u32[]{:S(2)}) collective-permute-start(bf16[512,512]{1,0:T(8,128)(2,1)S(1)} %collective-permute-done.1.refs_0_), channel_id=1, source_target_pairs={{0,1},{1,0},{2,3},{3,2},{4,5},{5,4},{6,7},{7,6},{8,9},{9,8},{10,11... | collective-permute-start | bytes 1572872 | tf_op jit(solution)/shard_map/ppermute | solution.py:126
  69.8 1.9 %collective-permute-start.6 = (bf16[512,512]{1,0:T(8,128)(2,1)S(1)}, bf16[512,512]{1,0:T(8,128)(2,1)S(1)}, u32[]{:S(2)}, u32[]{:S(2)}) collective-permute-start(bf16[512,512]{1,0:T(8,128)(2,1)S(1)} %collective-permute-done.4.refs_2_), channel_id=1, source_target_pairs={{0,1},{1,0},{2,3},{3,2},{4,5},{5,4},{6,7},{7,6},{8,9},{9,8},{10,11... | collective-permute-start | bytes 1572872 | tf_op jit(solution)/shard_map/ppermute | solution.py:126

commit v6 on v5

--- a/solution.py
+++ b/solution.py
@@ -58,32 +58,43 @@
     cos, sin = twist_ref[:, :fine], twist_ref[:, fine:]
     outer_ref, middle_ref = table_ref.at[: 2 * half], table_ref.at[2 * half :]
     scale = 1.0 / (blocks * rows)
-    for start in range(0, share, GROUP):
-        group = slice(start, start + GROUP)
-        parts = []
-        for lane in (0, rows):
-            spans = [slice(lane, lane + fine), slice(lane + fine, lane + rows)]
-            x = jnp.concatenate([x_ref[:, group, span].reshape(blocks * GROUP, fine) for span in spans], axis=0)
-            a = dot(outer_ref[...], x)
-            re, im = a[:half], a[half:]
-            parts.append(
-                jnp.concatenate([re * cos + im * sin, im * cos - re * sin], axis=1).astype(jnp.bfloat16)
-            )
-        spec = dot(jnp.concatenate(parts, axis=0), middle_ref[...])
-        xr, xi = spec[:half, :fine], spec[:half, fine:]
-        hr, hi = spec[half:, :fine], spec[half:, fine:]
-        prod = jnp.concatenate([xr * hr - xi * hi, xr * hi + xi * hr], axis=1).astype(jnp.bfloat16)
-        back = lax.dot_general(
+    groups = [slice(start, start + GROUP) for start in range(0, share, GROUP)]
+
+    def enter(group, lane):
+        spans = [slice(lane, lane + fine), slice(lane + fine, lane + rows)]
+        x = jnp.concatenate([x_ref[:, group, span].reshape(blocks * GROUP, fine) for span in spans], axis=0)
+        return dot(outer_ref[...], x)
+
+    def twist(a):
+        re, im = a[:half], a[half:]
+        return jnp.concatenate([re * cos + im * sin, im * cos - re * sin], axis=1).astype(jnp.bfloat16)
+
+    def product(spec_x, spec_h):
+        xr, xi, hr, hi = spec_x[:, :fine], spec_x[:, fine:], spec_h[:, :fine], spec_h[:, fine:]
+        return jnp.concatenate([xr * hr - xi * hi, xr * hi + xi * hr], axis=1).astype(jnp.bfloat16)
+
+    def back(prod):
+        return lax.dot_general(
             prod, middle_ref[...], (((1,), (1,)), ((), ())), preferred_element_type=jnp.float32
         )
-        re, im = back[:, :fine], back[:, fine:]
-        untwisted = jnp.concatenate([re * cos - im * sin, re * sin + im * cos], axis=0).astype(jnp.bfloat16)
+
+    def untwist(b):
+        re, im = b[:, :fine], b[:, fine:]
+        return jnp.concatenate([re * cos - im * sin, re * sin + im * cos], axis=0).astype(jnp.bfloat16)
+
+    def leave(group, turned):
         y = scale * lax.dot_general(
-            outer_ref[...], untwisted, (((0,), (0,)), ((), ())), preferred_element_type=jnp.float32
+            outer_ref[...], turned, (((0,), (0,)), ((), ())), preferred_element_type=jnp.float32
         )
         y = y.astype(jnp.bfloat16).reshape(2, blocks, GROUP, fine)
         out_ref[:, group, :fine] = y[0]
         out_ref[:, group, fine:] = y[1]
+
+    entered = [[enter(group, lane) for lane in (0, rows)] for group in groups]
+    spectra = [[dot(twist(a), middle_ref[...]) for a in pair] for pair in entered]
+    returned = [back(product(*pair)) for pair in spectra]
+    for group, b in zip(groups, returned):
+        leave(group, untwist(b))
 
 
 def convolve(x):

time: 73.5 us -> 72.5 us (0.986)
  Pallas kernels: 13.4 us -> 12.4 us
    pallas_call x1, Pallas kernels: 4.67 us -> 3.69 us  [convolve(): pl.pallas_call(conv_kernel, out_shape=jax.ShapeDtypeStruct((blocks, share...]
where the time goes in v6:
time: 72.5 us; the launch traced here: 72.2 us
  blocking collectives  37.8 us (52%)
  Pallas kernels  12.4 us (17%)
  starting transfers between devices  11.3 us (16%)
  waiting for transfers between devices  8.38 us (12%)
  local copies, waits for them, and re-layouts  2.29 us (3%)
    all_to_all x1, blocking collectives, per_device(): spread = lax.all_to_all(turn(signal, filt, ways), 'ctx', 0, 0, tiled=True)  24.7 us
    all_to_all x1, blocking collectives, per_device(): conv = lax.all_to_all(convolve(spread), 'ctx', 0, 0, tiled=True)  13.1 us
    ppermute x3, waiting for transfers between devices, shifted(): lax.ppermute(block, 'tp', [(i, toward(i, step)) for i in range(lax.axis_s...  7.93 us
    ppermute x4, starting transfers between devices, swapped(): lax.ppermute(block, 'tp', [(i, i ^ 1) for i in range(lax.axis_size('tp'))])  6.67 us
    ppermute x3, starting transfers between devices, shifted(): lax.ppermute(block, 'tp', [(i, toward(i, step)) for i in range(lax.axis_s...  4.68 us
    pallas_call x1, Pallas kernels, convolve(): pl.pallas_call(conv_kernel, out_shape=jax.ShapeDtypeStruct((blocks, share...  3.69 us
    pallas_call x1, Pallas kernels, project(): pl.pallas_call(functools.partial(first_kernel, own, later), in_specs=[pl....  3.49 us
    pallas_call x2, Pallas kernels, later_call(): pl.pallas_call(functools.partial(later_kernel, first), in_specs=[VMEM] *...  3.04 us
  transfers between devices with their start and end apart: 7, of which 5 were waited for; matrix products, arithmetic and copies ran while one was open for 0% of the time, Pallas kernels for 9%

profile of v6, /device:TPU:1, one launch (start us, length us, event | category | flops | bytes accessed | tf_op | source)
XLA Modules:
  0.0 72.2 jit_solution(9649533365829524222)
XLA Ops:
  0.0 0.0 copy-start
  0.0 1.0 %copy-done = bf16[512,512]{1,0:T(8,128)(2,1)S(1)} copy-done((bf16[512,512]{1,0:T(8,128)(2,1)S(1)}, bf16[512,512]{1,0:T(8,128)(2,1)}, u32[]{:S(2)}) %copy-start) | copy-done | bytes 524312
  1.0 1.2 %copy-done.3 = f32[512,512]{1,0:T(8,128)S(1)} copy-done((f32[512,512]{1,0:T(8,128)S(1)}, f32[512,512]{1,0:T(8,128)}, u32[]{:S(2)}) %copy-start.3) | copy-done | bytes 1048600
  2.3 0.4 turn.1
  2.6 24.7 %all_to_all.10.x_ref = bf16[16,32,1024]{2,1,0:T(8,128)(2,1)S(1)} all-to-all(bf16[16,32,1024]{2,1,0:T(8,128)(2,1)S(1)} %turn.1), channel_id=1, replica_groups=mesh['ctx'=16,'tp'=8] {'ctx'}, dimensions={0} | all-to-all | bytes 2097152 | tf_op jit(solution)/shard_map/all_to_all | solution.py:277
  27.3 0.0 copy-done.2
  27.3 0.0 copy-done.4
  27.3 0.0 copy-start.6
  27.3 3.7 %convolve.1 = bf16[16,32,512]{2,1,0:T(8,128)(2,1)S(1)} custom-call(bf16[16,32,1024]{2,1,0:T(8,128)(2,1)S(1)} %all_to_all.10.x_ref, bf16[1536,512]{1,0:T(8,128)(2,1)S(1)} %copy-done.2, f32[512,512]{1,0:T(8,128)S(1)} %copy-done.4), custom_call_target="tpu_custom_call" | custom-call | tf_op jit(solution)/shard_map/convolve/pallas_call | solution.py:103
  31.0 13.1 %all_to_all.11 = bf16[16,32,512]{2,1,0:T(8,128)(2,1)S(1)} all-to-all(bf16[16,32,512]{2,1,0:T(8,128)(2,1)S(1)} %convolve.1), channel_id=1, replica_groups=mesh['ctx'=16,'tp'=8] {'ctx'}, dimensions={0} | all-to-all | bytes 1048576 | tf_op jit(solution)/shard_map/all_to_all | solution.py:278
  44.1 0.0 copy-done.1
  44.1 0.0 copy-done.5
  44.1 0.0 copy-done.6
  44.1 0.3 mix.1.mine_ref
  44.4 2.6 %collective-permute-start = (bf16[512,512]{1,0:T(8,128)(2,1)S(1)}, bf16[512,512]{1,0:T(8,128)(2,1)S(1)}, u32[]{:S(2)}, u32[]{:S(2)}) collective-permute-start(bf16[512,512]{1,0:T(8,128)(2,1)S(1)} %mix.1.mine_ref), channel_id=1, source_target_pairs={{0,1},{1,0},{2,3},{3,2},{4,5},{5,4},{6,7},{7,6},{8,9},{9,8},{10,11... | collective-permute-start | bytes 1572872 | tf_op jit(solution)/shard_map/ppermute | solution.py:137
  47.0 1.2 %collective-permute-start.3 = (bf16[512,512]{1,0:T(8,128)(2,1)S(1)}, bf16[512,512]{1,0:T(8,128)(2,1)S(1)}, u32[]{:S(2)}, u32[]{:S(2)}) collective-permute-start(bf16[512,512]{1,0:T(8,128)(2,1)S(1)} %mix.1.mine_ref), channel_id=1, source_target_pairs={{0,6},{1,3},{2,0},{3,5},{4,2},{5,7},{6,4},{7,1},{8,14},{9,11},{10,... | collective-permute-start | bytes 1572872 | tf_op jit(solution)/shard_map/ppermute | solution.py:133
  48.2 0.3 collective-permute-done.beside_ref
  48.6 3.5 %project_own.1 = (f32[512,1024]{1,0:T(8,128)S(1)}, bf16[6,512,1024]{2,1,0:T(8,128)(2,1)S(1)}) custom-call(bf16[8,512,1024]{2,1,0:T(8,128)(2,1)} %bitcast.5, bf16[512,512]{1,0:T(8,128)(2,1)S(1)} %mix.1.mine_ref, bf16[512,512]{1,0:T(8,128)(2,1)S(1)} %collective-permute-done.beside_ref), custom_call_target="tpu_custom_call" | custom-call | flops 1073741824 | bytes 7340032 | tf_op jit(solution)/shard_map/project_own/pallas_call | solution.py:246
  52.1 2.5 %collective-permute-start.1 = (bf16[512,512]{1,0:T(8,128)(2,1)S(1)}, bf16[512,512]{1,0:T(8,128)(2,1)S(1)}, u32[]{:S(2)}, u32[]{:S(2)}) collective-permute-start(bf16[512,512]{1,0:T(8,128)(2,1)S(1)} %mix.1.mine_ref), channel_id=1, source_target_pairs={{0,2},{1,7},{2,4},{3,1},{4,6},{5,3},{6,0},{7,5},{8,10},{9,15},{10,... | collective-permute-start | bytes 1572872 | tf_op jit(solution)/shard_map/ppermute | solution.py:133
  54.6 1.7 %collective-permute-done.3.refs_0_ = bf16[512,512]{1,0:T(8,128)(2,1)S(1)} collective-permute-done((bf16[512,512]{1,0:T(8,128)(2,1)S(1)}, bf16[512,512]{1,0:T(8,128)(2,1)S(1)}, u32[]{:S(2)}, u32[]{:S(2)}) %collective-permute-start.3) | collective-permute-done | bytes 524320 | tf_op jit(solution)/shard_map/ppermute | solution.py:133
  56.3 1.3 %collective-permute-start.5 = (bf16[512,512]{1,0:T(8,128)(2,1)S(1)}, bf16[512,512]{1,0:T(8,128)(2,1)S(1)}, u32[]{:S(2)}, u32[]{:S(2)}) collective-permute-start(bf16[512,512]{1,0:T(8,128)(2,1)S(1)} %collective-permute-done.3.refs_0_), channel_id=1, source_target_pairs={{0,1},{1,0},{2,3},{3,2},{4,5},{5,4},{6,7},{7,6},{8,9},{9,8},{10,11... | collective-permute-start | bytes 1572872 | tf_op jit(solution)/shard_map/ppermute | solution.py:137
  57.6 0.9 %collective-permute-start.4 = (bf16[512,512]{1,0:T(8,128)(2,1)S(1)}, bf16[512,512]{1,0:T(8,128)(2,1)S(1)}, u32[]{:S(2)}, u32[]{:S(2)}) collective-permute-start(bf16[512,512]{1,0:T(8,128)(2,1)S(1)} %collective-permute-done.3.refs_0_), channel_id=1, source_target_pairs={{0,6},{1,3},{2,0},{3,5},{4,2},{5,7},{6,4},{7,1},{8,14},{9,11},{10,... | collective-permute-start | bytes 1572872 | tf_op jit(solution)/shard_map/ppermute | solution.py:133
  58.5 3.8 %collective-permute-done.1.refs_0_ = bf16[512,512]{1,0:T(8,128)(2,1)S(1)} collective-permute-done((bf16[512,512]{1,0:T(8,128)(2,1)S(1)}, bf16[512,512]{1,0:T(8,128)(2,1)S(1)}, u32[]{:S(2)}, u32[]{:S(2)}) %collective-permute-start.1) | collective-permute-done | bytes 524320 | tf_op jit(solution)/shard_map/ppermute | solution.py:133
  62.3 2.7 %collective-permute-start.2 = (bf16[512,512]{1,0:T(8,128)(2,1)S(1)}, bf16[512,512]{1,0:T(8,128)(2,1)S(1)}, u32[]{:S(2)}, u32[]{:S(2)}) collective-permute-start(bf16[512,512]{1,0:T(8,128)(2,1)S(1)} %collective-permute-done.1.refs_0_), channel_id=1, source_target_pairs={{0,1},{1,0},{2,3},{3,2},{4,5},{5,4},{6,7},{7,6},{8,9},{9,8},{10,11... | collective-permute-start | bytes 1572872 | tf_op jit(solution)/shard_map/ppermute | solution.py:137
  65.0 0.0 collective-permute-done.5.refs_1_
  65.0 1.2 %project_middle.1.refs_3_ = f32[512,1024]{1,0:T(8,128)S(1)} custom-call(bf16[6,512,1024]{2,1,0:T(8,128)(2,1)S(1)} %get-tuple-element.15.weights_ref, bf16[512,512]{1,0:T(8,128)(2,1)S(1)} %collective-permute-done.3.refs_0_, bf16[512,512]{1,0:T(8,128)(2,1)S(1)} %collective-permute-done.5.refs_1_, f32[512,1024]{1,0:T(8,128)S(1)} %get-tuple-element.20.refs_2_), custom_call_target="tpu_custom_call" | custom-call | flops 1073741824 | bytes 7340032 | tf_op jit(solution)/shard_map/project_middle/pallas_call | solution.py:226
  66.3 2.5 %collective-permute-done.4.refs_2_ = bf16[512,512]{1,0:T(8,128)(2,1)S(1)} collective-permute-done((bf16[512,512]{1,0:T(8,128)(2,1)S(1)}, bf16[512,512]{1,0:T(8,128)(2,1)S(1)}, u32[]{:S(2)}, u32[]{:S(2)}) %collective-permute-start.4) | collective-permute-done | bytes 524320 | tf_op jit(solution)/shard_map/ppermute | solution.py:133
  68.8 0.0 collective-permute-done.2.refs_1_
  68.8 0.0 collective-permute-start.6
  68.8 1.8 %project_near.1.refs_1_ = f32[512,1024]{1,0:T(8,128)S(1)} custom-call(bf16[6,512,1024]{2,1,0:T(8,128)(2,1)S(1)} %get-tuple-element.15.weights_ref, bf16[512,512]{1,0:T(8,128)(2,1)S(1)} %collective-permute-done.1.refs_0_, bf16[512,512]{1,0:T(8,128)(2,1)S(1)} %collective-permute-done.2.refs_1_, bf16[512,512]{1,0:T(8,128)(2,1)S(1)} %collective-permute-done.4.refs_2_, ...), custom_call_target="tpu_custom_call" | custom-call | flops 1610612736 | bytes 8912896 | tf_op jit(solution)/shard_map/project_near/pallas_call | solution.py:226
  70.6 0.1 collective-permute-done.6.refs_0_
  70.7 1.6 %project_last.1 = bf16[512,1024]{1,0:T(8,128)(2,1)} custom-call(bf16[6,512,1024]{2,1,0:T(8,128)(2,1)S(1)} %get-tuple-element.15.weights_ref, bf16[512,512]{1,0:T(8,128)(2,1)S(1)} %collective-permute-done.6.refs_0_, f32[512,1024]{1,0:T(8,128)S(1)} %project_near.1.refs_1_), custom_call_target="tpu_custom_call" | custom-call | tf_op jit(solution)/shard_map/project_last/pallas_call | solution.py:198
  (5 shorter events, 0.0 us)
Async XLA Ops:
  0.0 1.0 %copy-start = (bf16[512,512]{1,0:T(8,128)(2,1)S(1)}, bf16[512,512]{1,0:T(8,128)(2,1)}, u32[]{:S(2)}) copy-start(bf16[512,512]{1,0:T(8,128)(2,1)} %signal_ref.3) | copy-start | bytes 1572868
  1.0 1.2 %copy-start.3 = (f32[512,512]{1,0:T(8,128)S(1)}, f32[512,512]{1,0:T(8,128)}, u32[]{:S(2)}) copy-start(f32[512,512]{1,0:T(8,128)} %filt_ref.1) | copy-start | bytes 3145732
  2.3 25.0 %copy-start.2 = (bf16[1536,512]{1,0:T(8,128)(2,1)S(1)}, bf16[1536,512]{1,0:T(8,128)(2,1)}, u32[]{:S(2)}) copy-start(bf16[1536,512]{1,0:T(8,128)(2,1)} %constant.4.clone.table_ref) | copy-start | bytes 4718596
  2.3 25.0 %copy-start.4 = (f32[512,512]{1,0:T(8,128)S(1)}, f32[512,512]{1,0:T(8,128)}, u32[]{:S(2)}) copy-start(f32[512,512]{1,0:T(8,128)} %constant.5.clone.twist_ref) | copy-start | bytes 3145732
  27.3 16.8 %copy-start.1 = (bf16[512,512]{1,0:T(8,128)(2,1)S(1)}, bf16[512,512]{1,0:T(8,128)(2,1)}, u32[]{:S(2)}) copy-start(bf16[512,512]{1,0:T(8,128)(2,1)} %signal_ref.3) | copy-start | bytes 1572868
  27.3 16.8 %copy-start.5 = (bf16[512,512]{1,0:T(8,128)(2,1)S(1)}, bf16[512,512]{1,0:T(8,128)(2,1)}, u32[]{:S(2)}) copy-start(bf16[512,512]{1,0:T(8,128)(2,1)} %gate_ref.1) | copy-start | bytes 1572868
  27.3 16.8 %copy-start.6 = (f32[512]{0:T(512)S(1)}, f32[512]{0:T(512)}, u32[]{:S(2)}) copy-start(f32[512]{0:T(512)} %param.10) | copy-start | bytes 6148
  44.4 4.2 %collective-permute-start = (bf16[512,512]{1,0:T(8,128)(2,1)S(1)}, bf16[512,512]{1,0:T(8,128)(2,1)S(1)}, u32[]{:S(2)}, u32[]{:S(2)}) collective-permute-start(bf16[512,512]{1,0:T(8,128)(2,1)S(1)} %mix.1.mine_ref), channel_id=1, source_target_pairs={{0,1},{1,0},{2,3},{3,2},{4,5},{5,4},{6,7},{7,6},{8,9},{9,8},{10,11... | collective-permute-start | bytes 1572872 | tf_op jit(solution)/shard_map/ppermute | solution.py:137
  47.0 9.2 %collective-permute-start.3 = (bf16[512,512]{1,0:T(8,128)(2,1)S(1)}, bf16[512,512]{1,0:T(8,128)(2,1)S(1)}, u32[]{:S(2)}, u32[]{:S(2)}) collective-permute-start(bf16[512,512]{1,0:T(8,128)(2,1)S(1)} %mix.1.mine_ref), channel_id=1, source_target_pairs={{0,6},{1,3},{2,0},{3,5},{4,2},{5,7},{6,4},{7,1},{8,14},{9,11},{10,... | collective-permute-start | bytes 1572872 | tf_op jit(solution)/shard_map/ppermute | solution.py:133
  52.1 10.2 %collective-permute-start.1 = (bf16[512,512]{1,0:T(8,128)(2,1)S(1)}, bf16[512,512]{1,0:T(8,128)(2,1)S(1)}, u32[]{:S(2)}, u32[]{:S(2)}) collective-permute-start(bf16[512,512]{1,0:T(8,128)(2,1)S(1)} %mix.1.mine_ref), channel_id=1, source_target_pairs={{0,2},{1,7},{2,4},{3,1},{4,6},{5,3},{6,0},{7,5},{8,10},{9,15},{10,... | collective-permute-start | bytes 1572872 | tf_op jit(solution)/shard_map/ppermute | solution.py:133
  56.3 8.7 %collective-permute-start.5 = (bf16[512,512]{1,0:T(8,128)(2,1)S(1)}, bf16[512,512]{1,0:T(8,128)(2,1)S(1)}, u32[]{:S(2)}, u32[]{:S(2)}) collective-permute-start(bf16[512,512]{1,0:T(8,128)(2,1)S(1)} %collective-permute-done.3.refs_0_), channel_id=1, source_target_pairs={{0,1},{1,0},{2,3},{3,2},{4,5},{5,4},{6,7},{7,6},{8,9},{9,8},{10,11... | collective-permute-start | bytes 1572872 | tf_op jit(solution)/shard_map/ppermute | solution.py:137
  57.6 11.2 %collective-permute-start.4 = (bf16[512,512]{1,0:T(8,128)(2,1)S(1)}, bf16[512,512]{1,0:T(8,128)(2,1)S(1)}, u32[]{:S(2)}, u32[]{:S(2)}) collective-permute-start(bf16[512,512]{1,0:T(8,128)(2,1)S(1)} %collective-permute-done.3.refs_0_), channel_id=1, source_target_pairs={{0,6},{1,3},{2,0},{3,5},{4,2},{5,7},{6,4},{7,1},{8,14},{9,11},{10,... | collective-permute-start | bytes 1572872 | tf_op jit(solution)/shard_map/ppermute | solution.py:133
  62.3 6.5 %collective-permute-start.2 = (bf16[512,512]{1,0:T(8,128)(2,1)S(1)}, bf16[512,512]{1,0:T(8,128)(2,1)S(1)}, u32[]{:S(2)}, u32[]{:S(2)}) collective-permute-start(bf16[512,512]{1,0:T(8,128)(2,1)S(1)} %collective-permute-done.1.refs_0_), channel_id=1, source_target_pairs={{0,1},{1,0},{2,3},{3,2},{4,5},{5,4},{6,7},{7,6},{8,9},{9,8},{10,11... | collective-permute-start | bytes 1572872 | tf_op jit(solution)/shard_map/ppermute | solution.py:137
  68.8 1.9 %collective-permute-start.6 = (bf16[512,512]{1,0:T(8,128)(2,1)S(1)}, bf16[512,512]{1,0:T(8,128)(2,1)S(1)}, u32[]{:S(2)}, u32[]{:S(2)}) collective-permute-start(bf16[512,512]{1,0:T(8,128)(2,1)S(1)} %collective-permute-done.4.refs_2_), channel_id=1, source_target_pairs={{0,1},{1,0},{2,3},{3,2},{4,5},{5,4},{6,7},{7,6},{8,9},{9,8},{10,11... | collective-permute-start | bytes 1572872 | tf_op jit(solution)/shard_map/ppermute | solution.py:137

commit v7 on v6

--- a/solution.py
+++ b/solution.py
@@ -91,10 +91,13 @@
         out_ref[:, group, fine:] = y[1]
 
     entered = [[enter(group, lane) for lane in (0, rows)] for group in groups]
-    spectra = [[dot(twist(a), middle_ref[...]) for a in pair] for pair in entered]
-    returned = [back(product(*pair)) for pair in spectra]
-    for group, b in zip(groups, returned):
-        leave(group, untwist(b))
+    spectra = dot(jnp.concatenate([twist(a) for pair in entered for a in pair], axis=0), middle_ref[...])
+    spectra = [spectra[k * half : (k + 1) * half] for k in range(2 * len(groups))]
+    returned = back(
+        jnp.concatenate([product(*spectra[2 * k : 2 * k + 2]) for k in range(len(groups))], axis=0)
+    )
+    for k, group in enumerate(groups):
+        leave(group, untwist(returned[k * half : (k + 1) * half]))
 
 
 def convolve(x):
@@ -180,13 +183,13 @@
     blocks, total_ref, out_ref, held_ref, sems = refs[:-4], refs[-4], refs[-3], refs[-2], refs[-1]
     left = jnp.concatenate([block[...] for block in blocks], axis=1)
     count, width = len(blocks), weights_ref.shape[1]
-    lanes = held_ref.shape[2]
+    right = weights_ref[first : first + count].reshape(count * width, weights_ref.shape[2])
+    high = held_ref.shape[1]
     copies = []
     for step in range(held_ref.shape[0]):
-        span = slice(step * lanes, (step + 1) * lanes)
-        mine = dot(left, weights_ref[first : first + count, :, span].reshape(count * width, lanes))
-        held_ref[step] = (mine + total_ref[:, span]).astype(out_ref.dtype)
-        copies.append(pltpu.make_async_copy(held_ref.at[step], out_ref.at[:, span], sems.at[step]))
+        span = slice(step * high, (step + 1) * high)
+        held_ref[step] = (dot(left[span], right) + total_ref[span, :]).astype(out_ref.dtype)
+        copies.append(pltpu.make_async_copy(held_ref.at[step], out_ref.at[pl.ds(step * high, high)], sems.at[step]))
         copies[-1].start()
     for copy in copies:
         copy.wait()
@@ -201,7 +204,7 @@
         out_specs=pl.BlockSpec(memory_space=pl.ANY),
         out_shape=jax.ShapeDtypeStruct((rows, columns), dtype),
         scratch_shapes=[
-            pltpu.VMEM((steps, rows, columns // steps), dtype),
+            pltpu.VMEM((steps, rows // steps, columns), dtype),
             pltpu.SemaphoreType.DMA((steps,)),
         ],
         compiler_params=pltpu.CompilerParams(vmem_limit_bytes=12 * 2**20),
@@ -263,11 +266,11 @@
     behind = shifted(mixed, 1)
     ahead, total = lax.optimization_barrier((ahead, total))
     far = shifted(ahead, -1)
-    total = later_call(weights, 0, [ahead, swapped(ahead)], total, jnp.float32, "project_middle")
-    near_blocks = [behind, swapped(behind)]
+    total = later_call(weights, 0, [ahead, swapped(ahead), behind], total, jnp.float32, "project_middle")
+    near_blocks = [swapped(behind)]
     *near_blocks, far, total = lax.optimization_barrier((*near_blocks, far, total))
     beside_far = swapped(far)
-    total = later_call(weights, 2, [*near_blocks, far], total, jnp.float32, "project_near")
+    total = later_call(weights, 3, [*near_blocks, far], total, jnp.float32, "project_near")
     return last_call(weights, len(later) - 1, [beside_far], total, jnp.bfloat16)
 
 

time: 72.5 us -> 72.5 us (level)
  no operation moved by 1% of the time
where the time goes in v7:
time: 72.5 us; the launch traced here: 72.2 us
  blocking collectives  37.8 us (52%)
  Pallas kernels  12.3 us (17%)
  starting transfers between devices  11.4 us (16%)
  waiting for transfers between devices  8.35 us (12%)
  local copies, waits for them, and re-layouts  2.29 us (3%)
    all_to_all x1, blocking collectives, per_device(): spread = lax.all_to_all(turn(signal, filt, ways), 'ctx', 0, 0, tiled=True)  24.7 us
    all_to_all x1, blocking collectives, per_device(): conv = lax.all_to_all(convolve(spread), 'ctx', 0, 0, tiled=True)  13.1 us
    ppermute x3, waiting for transfers between devices, shifted(): lax.ppermute(block, 'tp', [(i, toward(i, step)) for i in range(lax.axis_s...  7.37 us
    ppermute x4, starting transfers between devices, swapped(): lax.ppermute(block, 'tp', [(i, i ^ 1) for i in range(lax.axis_size('tp'))])  6.7 us
    ppermute x3, starting transfers between devices, shifted(): lax.ppermute(block, 'tp', [(i, toward(i, step)) for i in range(lax.axis_s...  4.7 us
    pallas_call x1, Pallas kernels, convolve(): pl.pallas_call(conv_kernel, out_shape=jax.ShapeDtypeStruct((blocks, share...  3.72 us
    pallas_call x1, Pallas kernels, project(): pl.pallas_call(functools.partial(first_kernel, own, later), in_specs=[pl....  3.49 us
    pallas_call x2, Pallas kernels, later_call(): pl.pallas_call(functools.partial(later_kernel, first), in_specs=[VMEM] *...  3.04 us
  transfers between devices with their start and end apart: 7, of which 5 were waited for; matrix products, arithmetic and copies ran while one was open for 0% of the time, Pallas kernels for 9%

profile of v7, /device:TPU:1, one launch (start us, length us, event | category | flops | bytes accessed | tf_op | source)
XLA Modules:
  0.0 72.2 jit_solution(9271525466932240143)
XLA Ops:
  0.0 0.0 copy-start
  0.0 1.0 %copy-done = bf16[512,512]{1,0:T(8,128)(2,1)S(1)} copy-done((bf16[512,512]{1,0:T(8,128)(2,1)S(1)}, bf16[512,512]{1,0:T(8,128)(2,1)}, u32[]{:S(2)}) %copy-start) | copy-done | bytes 524312
  1.0 1.2 %copy-done.3 = f32[512,512]{1,0:T(8,128)S(1)} copy-done((f32[512,512]{1,0:T(8,128)S(1)}, f32[512,512]{1,0:T(8,128)}, u32[]{:S(2)}) %copy-start.3) | copy-done | bytes 1048600
  2.3 0.4 turn.1
  2.6 24.7 %all_to_all.10.x_ref = bf16[16,32,1024]{2,1,0:T(8,128)(2,1)S(1)} all-to-all(bf16[16,32,1024]{2,1,0:T(8,128)(2,1)S(1)} %turn.1), channel_id=1, replica_groups=mesh['ctx'=16,'tp'=8] {'ctx'}, dimensions={0} | all-to-all | bytes 2097152 | tf_op jit(solution)/shard_map/all_to_all | solution.py:280
  27.3 0.0 copy-done.2
  27.3 0.0 copy-done.4
  27.3 0.0 copy-start.6
  27.3 3.7 %convolve.1 = bf16[16,32,512]{2,1,0:T(8,128)(2,1)S(1)} custom-call(bf16[16,32,1024]{2,1,0:T(8,128)(2,1)S(1)} %all_to_all.10.x_ref, bf16[1536,512]{1,0:T(8,128)(2,1)S(1)} %copy-done.2, f32[512,512]{1,0:T(8,128)S(1)} %copy-done.4), custom_call_target="tpu_custom_call" | custom-call | tf_op jit(solution)/shard_map/convolve/pallas_call | solution.py:106
  31.1 13.1 %all_to_all.11 = bf16[16,32,512]{2,1,0:T(8,128)(2,1)S(1)} all-to-all(bf16[16,32,512]{2,1,0:T(8,128)(2,1)S(1)} %convolve.1), channel_id=1, replica_groups=mesh['ctx'=16,'tp'=8] {'ctx'}, dimensions={0} | all-to-all | bytes 1048576 | tf_op jit(solution)/shard_map/all_to_all | solution.py:281
  44.1 0.0 copy-done.1
  44.1 0.0 copy-done.5
  44.1 0.0 copy-done.6
  44.2 0.3 mix.1.mine_ref
  44.4 2.6 %collective-permute-start = (bf16[512,512]{1,0:T(8,128)(2,1)S(1)}, bf16[512,512]{1,0:T(8,128)(2,1)S(1)}, u32[]{:S(2)}, u32[]{:S(2)}) collective-permute-start(bf16[512,512]{1,0:T(8,128)(2,1)S(1)} %mix.1.mine_ref), channel_id=1, source_target_pairs={{0,1},{1,0},{2,3},{3,2},{4,5},{5,4},{6,7},{7,6},{8,9},{9,8},{10,11... | collective-permute-start | bytes 1572872 | tf_op jit(solution)/shard_map/ppermute | solution.py:140
  47.1 1.2 %collective-permute-start.3 = (bf16[512,512]{1,0:T(8,128)(2,1)S(1)}, bf16[512,512]{1,0:T(8,128)(2,1)S(1)}, u32[]{:S(2)}, u32[]{:S(2)}) collective-permute-start(bf16[512,512]{1,0:T(8,128)(2,1)S(1)} %mix.1.mine_ref), channel_id=1, source_target_pairs={{0,6},{1,3},{2,0},{3,5},{4,2},{5,7},{6,4},{7,1},{8,14},{9,11},{10,... | collective-permute-start | bytes 1572872 | tf_op jit(solution)/shard_map/ppermute | solution.py:136
  48.3 0.3 collective-permute-done.beside_ref
  48.6 3.5 %project_own.1 = (f32[512,1024]{1,0:T(8,128)S(1)}, bf16[6,512,1024]{2,1,0:T(8,128)(2,1)S(1)}) custom-call(bf16[8,512,1024]{2,1,0:T(8,128)(2,1)} %bitcast.5, bf16[512,512]{1,0:T(8,128)(2,1)S(1)} %mix.1.mine_ref, bf16[512,512]{1,0:T(8,128)(2,1)S(1)} %collective-permute-done.beside_ref), custom_call_target="tpu_custom_call" | custom-call | flops 1073741824 | bytes 7340032 | tf_op jit(solution)/shard_map/project_own/pallas_call | solution.py:249
  52.1 2.5 %collective-permute-start.1 = (bf16[512,512]{1,0:T(8,128)(2,1)S(1)}, bf16[512,512]{1,0:T(8,128)(2,1)S(1)}, u32[]{:S(2)}, u32[]{:S(2)}) collective-permute-start(bf16[512,512]{1,0:T(8,128)(2,1)S(1)} %mix.1.mine_ref), channel_id=1, source_target_pairs={{0,2},{1,7},{2,4},{3,1},{4,6},{5,3},{6,0},{7,5},{8,10},{9,15},{10,... | collective-permute-start | bytes 1572872 | tf_op jit(solution)/shard_map/ppermute | solution.py:136
  54.7 1.7 %collective-permute-done.3.refs_0_ = bf16[512,512]{1,0:T(8,128)(2,1)S(1)} collective-permute-done((bf16[512,512]{1,0:T(8,128)(2,1)S(1)}, bf16[512,512]{1,0:T(8,128)(2,1)S(1)}, u32[]{:S(2)}, u32[]{:S(2)}) %collective-permute-start.3) | collective-permute-done | bytes 524320 | tf_op jit(solution)/shard_map/ppermute | solution.py:136
  56.3 1.3 %collective-permute-start.5 = (bf16[512,512]{1,0:T(8,128)(2,1)S(1)}, bf16[512,512]{1,0:T(8,128)(2,1)S(1)}, u32[]{:S(2)}, u32[]{:S(2)}) collective-permute-start(bf16[512,512]{1,0:T(8,128)(2,1)S(1)} %collective-permute-done.3.refs_0_), channel_id=1, source_target_pairs={{0,1},{1,0},{2,3},{3,2},{4,5},{5,4},{6,7},{7,6},{8,9},{9,8},{10,11... | collective-permute-start | bytes 1572872 | tf_op jit(solution)/shard_map/ppermute | solution.py:140
  57.6 0.9 %collective-permute-start.4 = (bf16[512,512]{1,0:T(8,128)(2,1)S(1)}, bf16[512,512]{1,0:T(8,128)(2,1)S(1)}, u32[]{:S(2)}, u32[]{:S(2)}) collective-permute-start(bf16[512,512]{1,0:T(8,128)(2,1)S(1)} %collective-permute-done.3.refs_0_), channel_id=1, source_target_pairs={{0,6},{1,3},{2,0},{3,5},{4,2},{5,7},{6,4},{7,1},{8,14},{9,11},{10,... | collective-permute-start | bytes 1572872 | tf_op jit(solution)/shard_map/ppermute | solution.py:136
  58.5 3.7 %collective-permute-done.1.refs_2_ = bf16[512,512]{1,0:T(8,128)(2,1)S(1)} collective-permute-done((bf16[512,512]{1,0:T(8,128)(2,1)S(1)}, bf16[512,512]{1,0:T(8,128)(2,1)S(1)}, u32[]{:S(2)}, u32[]{:S(2)}) %collective-permute-start.1) | collective-permute-done | bytes 524320 | tf_op jit(solution)/shard_map/ppermute | solution.py:136
  62.3 2.8 %collective-permute-start.2 = (bf16[512,512]{1,0:T(8,128)(2,1)S(1)}, bf16[512,512]{1,0:T(8,128)(2,1)S(1)}, u32[]{:S(2)}, u32[]{:S(2)}) collective-permute-start(bf16[512,512]{1,0:T(8,128)(2,1)S(1)} %collective-permute-done.1.refs_2_), channel_id=1, source_target_pairs={{0,1},{1,0},{2,3},{3,2},{4,5},{5,4},{6,7},{7,6},{8,9},{9,8},{10,11... | collective-permute-start | bytes 1572872 | tf_op jit(solution)/shard_map/ppermute | solution.py:140
  65.0 0.0 collective-permute-done.5.refs_1_
  65.0 1.8 %project_middle.1.refs_2_ = f32[512,1024]{1,0:T(8,128)S(1)} custom-call(bf16[6,512,1024]{2,1,0:T(8,128)(2,1)S(1)} %get-tuple-element.14.weights_ref, bf16[512,512]{1,0:T(8,128)(2,1)S(1)} %collective-permute-done.3.refs_0_, bf16[512,512]{1,0:T(8,128)(2,1)S(1)} %collective-permute-done.5.refs_1_, bf16[512,512]{1,0:T(8,128)(2,1)S(1)} %collective-permute-done.1.refs_2_, ...), custom_call_target="tpu_custom_call" | custom-call | flops 1610612736 | bytes 8912896 | tf_op jit(solution)/shard_map/project_middle/pallas_call | solution.py:229
  66.8 2.0 %collective-permute-done.4.refs_1_ = bf16[512,512]{1,0:T(8,128)(2,1)S(1)} collective-permute-done((bf16[512,512]{1,0:T(8,128)(2,1)S(1)}, bf16[512,512]{1,0:T(8,128)(2,1)S(1)}, u32[]{:S(2)}, u32[]{:S(2)}) %collective-permute-start.4) | collective-permute-done | bytes 524320 | tf_op jit(solution)/shard_map/ppermute | solution.py:136
  68.8 0.0 collective-permute-done.2.refs_0_
  68.8 0.0 collective-permute-start.6
  68.8 1.3 %project_near.1.refs_1_ = f32[512,1024]{1,0:T(8,128)S(1)} custom-call(bf16[6,512,1024]{2,1,0:T(8,128)(2,1)S(1)} %get-tuple-element.14.weights_ref, bf16[512,512]{1,0:T(8,128)(2,1)S(1)} %collective-permute-done.2.refs_0_, bf16[512,512]{1,0:T(8,128)(2,1)S(1)} %collective-permute-done.4.refs_1_, f32[512,1024]{1,0:T(8,128)S(1)} %project_middle.1.refs_2_), custom_call_target="tpu_custom_call" | custom-call | flops 1073741824 | bytes 7340032 | tf_op jit(solution)/shard_map/project_near/pallas_call | solution.py:229
  70.1 0.7 collective-permute-done.6.refs_0_
  70.7 1.5 %project_last.1 = bf16[512,1024]{1,0:T(8,128)(2,1)} custom-call(bf16[6,512,1024]{2,1,0:T(8,128)(2,1)S(1)} %get-tuple-element.14.weights_ref, bf16[512,512]{1,0:T(8,128)(2,1)S(1)} %collective-permute-done.6.refs_0_, f32[512,1024]{1,0:T(8,128)S(1)} %project_near.1.refs_1_), custom_call_target="tpu_custom_call" | custom-call | tf_op jit(solution)/shard_map/project_last/pallas_call | solution.py:201
  (5 shorter events, 0.0 us)
Async XLA Ops:
  0.0 1.0 %copy-start = (bf16[512,512]{1,0:T(8,128)(2,1)S(1)}, bf16[512,512]{1,0:T(8,128)(2,1)}, u32[]{:S(2)}) copy-start(bf16[512,512]{1,0:T(8,128)(2,1)} %signal_ref.3) | copy-start | bytes 1572868
  1.0 1.2 %copy-start.3 = (f32[512,512]{1,0:T(8,128)S(1)}, f32[512,512]{1,0:T(8,128)}, u32[]{:S(2)}) copy-start(f32[512,512]{1,0:T(8,128)} %filt_ref.1) | copy-start | bytes 3145732
  2.3 25.0 %copy-start.2 = (bf16[1536,512]{1,0:T(8,128)(2,1)S(1)}, bf16[1536,512]{1,0:T(8,128)(2,1)}, u32[]{:S(2)}) copy-start(bf16[1536,512]{1,0:T(8,128)(2,1)} %constant.4.clone.table_ref) | copy-start | bytes 4718596
  2.3 25.0 %copy-start.4 = (f32[512,512]{1,0:T(8,128)S(1)}, f32[512,512]{1,0:T(8,128)}, u32[]{:S(2)}) copy-start(f32[512,512]{1,0:T(8,128)} %constant.5.clone.twist_ref) | copy-start | bytes 3145732
  27.3 16.8 %copy-start.1 = (bf16[512,512]{1,0:T(8,128)(2,1)S(1)}, bf16[512,512]{1,0:T(8,128)(2,1)}, u32[]{:S(2)}) copy-start(bf16[512,512]{1,0:T(8,128)(2,1)} %signal_ref.3) | copy-start | bytes 1572868
  27.3 16.8 %copy-start.5 = (bf16[512,512]{1,0:T(8,128)(2,1)S(1)}, bf16[512,512]{1,0:T(8,128)(2,1)}, u32[]{:S(2)}) copy-start(bf16[512,512]{1,0:T(8,128)(2,1)} %gate_ref.1) | copy-start | bytes 1572868
  27.3 16.8 %copy-start.6 = (f32[512]{0:T(512)S(1)}, f32[512]{0:T(512)}, u32[]{:S(2)}) copy-start(f32[512]{0:T(512)} %param.10) | copy-start | bytes 6148
  44.4 4.2 %collective-permute-start = (bf16[512,512]{1,0:T(8,128)(2,1)S(1)}, bf16[512,512]{1,0:T(8,128)(2,1)S(1)}, u32[]{:S(2)}, u32[]{:S(2)}) collective-permute-start(bf16[512,512]{1,0:T(8,128)(2,1)S(1)} %mix.1.mine_ref), channel_id=1, source_target_pairs={{0,1},{1,0},{2,3},{3,2},{4,5},{5,4},{6,7},{7,6},{8,9},{9,8},{10,11... | collective-permute-start | bytes 1572872 | tf_op jit(solution)/shard_map/ppermute | solution.py:140
  47.1 9.2 %collective-permute-start.3 = (bf16[512,512]{1,0:T(8,128)(2,1)S(1)}, bf16[512,512]{1,0:T(8,128)(2,1)S(1)}, u32[]{:S(2)}, u32[]{:S(2)}) collective-permute-start(bf16[512,512]{1,0:T(8,128)(2,1)S(1)} %mix.1.mine_ref), channel_id=1, source_target_pairs={{0,6},{1,3},{2,0},{3,5},{4,2},{5,7},{6,4},{7,1},{8,14},{9,11},{10,... | collective-permute-start | bytes 1572872 | tf_op jit(solution)/shard_map/ppermute | solution.py:136
  52.1 10.2 %collective-permute-start.1 = (bf16[512,512]{1,0:T(8,128)(2,1)S(1)}, bf16[512,512]{1,0:T(8,128)(2,1)S(1)}, u32[]{:S(2)}, u32[]{:S(2)}) collective-permute-start(bf16[512,512]{1,0:T(8,128)(2,1)S(1)} %mix.1.mine_ref), channel_id=1, source_target_pairs={{0,2},{1,7},{2,4},{3,1},{4,6},{5,3},{6,0},{7,5},{8,10},{9,15},{10,... | collective-permute-start | bytes 1572872 | tf_op jit(solution)/shard_map/ppermute | solution.py:136
  56.3 8.7 %collective-permute-start.5 = (bf16[512,512]{1,0:T(8,128)(2,1)S(1)}, bf16[512,512]{1,0:T(8,128)(2,1)S(1)}, u32[]{:S(2)}, u32[]{:S(2)}) collective-permute-start(bf16[512,512]{1,0:T(8,128)(2,1)S(1)} %collective-permute-done.3.refs_0_), channel_id=1, source_target_pairs={{0,1},{1,0},{2,3},{3,2},{4,5},{5,4},{6,7},{7,6},{8,9},{9,8},{10,11... | collective-permute-start | bytes 1572872 | tf_op jit(solution)/shard_map/ppermute | solution.py:140
  57.6 11.2 %collective-permute-start.4 = (bf16[512,512]{1,0:T(8,128)(2,1)S(1)}, bf16[512,512]{1,0:T(8,128)(2,1)S(1)}, u32[]{:S(2)}, u32[]{:S(2)}) collective-permute-start(bf16[512,512]{1,0:T(8,128)(2,1)S(1)} %collective-permute-done.3.refs_0_), channel_id=1, source_target_pairs={{0,6},{1,3},{2,0},{3,5},{4,2},{5,7},{6,4},{7,1},{8,14},{9,11},{10,... | collective-permute-start | bytes 1572872 | tf_op jit(solution)/shard_map/ppermute | solution.py:136
  62.3 6.5 %collective-permute-start.2 = (bf16[512,512]{1,0:T(8,128)(2,1)S(1)}, bf16[512,512]{1,0:T(8,128)(2,1)S(1)}, u32[]{:S(2)}, u32[]{:S(2)}) collective-permute-start(bf16[512,512]{1,0:T(8,128)(2,1)S(1)} %collective-permute-done.1.refs_2_), channel_id=1, source_target_pairs={{0,1},{1,0},{2,3},{3,2},{4,5},{5,4},{6,7},{7,6},{8,9},{9,8},{10,11... | collective-permute-start | bytes 1572872 | tf_op jit(solution)/shard_map/ppermute | solution.py:140
  68.8 1.9 %collective-permute-start.6 = (bf16[512,512]{1,0:T(8,128)(2,1)S(1)}, bf16[512,512]{1,0:T(8,128)(2,1)S(1)}, u32[]{:S(2)}, u32[]{:S(2)}) collective-permute-start(bf16[512,512]{1,0:T(8,128)(2,1)S(1)} %collective-permute-done.4.refs_1_), channel_id=1, source_target_pairs={{0,1},{1,0},{2,3},{3,2},{4,5},{5,4},{6,7},{7,6},{8,9},{9,8},{10,11... | collective-permute-start | bytes 1572872 | tf_op jit(solution)/shard_map/ppermute | solution.py:140
